TPU v7x, 256 devices: a whole 4x4x8 slice. The times are simulated.
256 devices in a mesh: ctx: 32 (over y, z_hi, core), tp: 8 (over x, z_lo).
Axes of the slice: x: 4, y: 4, z: 8 (z_hi: 4, z_lo: 2; z = z_hi * 2 + z_lo), core: 2. Of those that a mesh axis runs over, the one named last changes fastest.
Arguments:
- queries: bfloat16 [1024, 4096], P(None, 'tp'), may hold values from -48 to 48
- prefix_keys: bfloat16 [32768, 4096], P('ctx', 'tp'), may hold values from -30 to 30
- prefix_values: bfloat16 [32768, 4096], P('ctx', 'tp'), may hold values from -24 to 24
- out_weight: bfloat16 [4096, 4096], P('tp'), may hold values from -0.09375 to 0.09375
- out_grad: bfloat16 [1024, 4096], P('ctx', 'tp'), may hold values from -6 to 6
Outputs:
- latent_out: bfloat16 [1024, 4096], P('ctx', 'tp')
- query_grad: bfloat16 [1024, 4096], P('ctx', 'tp')
- key_grad: bfloat16 [32768, 4096], P('ctx', 'tp')
- value_grad: bfloat16 [32768, 4096], P('ctx', 'tp')
- weight_grad: float32 [4096, 4096], P('tp', 'ctx')
All inputs are finite; a program needn't handle non-finite values.
Results may differ from a plain program's by a relative error of at most 0.039.
Values may be sent and summed in bfloat16 or wider, within the bound.
No kernel may reach another device: no remote copies, remote signals or barrier semaphores. Data moves between devices by JAX's collectives and lax.ppermute only.
A program may use at most 128 MiB of HBM per device.

v0:
```python
import jax
import jax.numpy as jnp
from jax import lax
from jax.sharding import PartitionSpec as P

HDIM = 128


def body(queries, prefix_keys, prefix_values, out_weight, out_grad):
    heads_here = queries.shape[1] // HDIM
    latents = queries.shape[0]
    tokens_here = prefix_keys.shape[0]
    rows_here = out_grad.shape[0]
    scale = HDIM ** (-0.5)
    query_heads = queries.reshape(latents, heads_here, HDIM)
    key_heads = prefix_keys.reshape(tokens_here, heads_here, HDIM)
    value_heads = prefix_values.reshape(tokens_here, heads_here, HDIM)
    row_start = lax.axis_index("ctx") * rows_here
    scores = (
        jnp.einsum("lhd,khd->hlk", query_heads, key_heads, preferred_element_type=jnp.float32)
        * scale
    )
    row_top = lax.pmax(jnp.max(scores, axis=2), "ctx")
    expo = jnp.exp(scores - row_top[:, :, None])
    partial_den = jnp.sum(expo, axis=2).T
    partial_num = jnp.einsum(
        "hlk,khd->lhd", expo.astype(jnp.bfloat16), value_heads, preferred_element_type=jnp.float32
    )
    numer, denom = lax.psum((partial_num, partial_den), "ctx")
    attended = (numer / denom[:, :, None]).astype(jnp.bfloat16)
    log_den = row_top + jnp.log(denom.T)
    flat = attended.reshape(latents, heads_here * HDIM)
    own_rows = lax.dynamic_slice_in_dim(flat, row_start, rows_here, 0)
    partial_out = jnp.dot(own_rows, out_weight, preferred_element_type=jnp.float32)
    latent_out = lax.psum_scatter(
        partial_out.astype(jnp.bfloat16), "tp", scatter_dimension=1, tiled=True
    )
    grad_full = lax.all_gather(out_grad, "tp", axis=1, tiled=True)
    dout_own = jnp.einsum(
        "rf,ef->re", grad_full, out_weight, preferred_element_type=jnp.float32
    ).astype(jnp.bfloat16)
    partial_weight = jnp.einsum(
        "re,rf->ef", own_rows, grad_full, preferred_element_type=jnp.float32
    )
    weight_grad = lax.psum_scatter(
        partial_weight.astype(jnp.bfloat16), "ctx", scatter_dimension=1, tiled=True
    ).astype(jnp.float32)
    dout = lax.all_gather(dout_own, "ctx", axis=0, tiled=True)
    dout_heads = dout.reshape(latents, heads_here, HDIM)
    delta = jnp.sum(dout_heads.astype(jnp.float32) * attended.astype(jnp.float32), axis=2).T
    probs = jnp.exp(scores - log_den[:, :, None])
    value_grad = jnp.einsum(
        "hlk,lhd->khd", probs.astype(jnp.bfloat16), dout_heads, preferred_element_type=jnp.float32
    )
    dprob = jnp.einsum("lhd,khd->hlk", dout_heads, value_heads, preferred_element_type=jnp.float32)
    dscore = (probs * (dprob - delta[:, :, None]) * scale).astype(jnp.bfloat16)
    partial_query = jnp.einsum(
        "hlk,khd->lhd", dscore, key_heads, preferred_element_type=jnp.float32
    )
    query_grad = lax.psum_scatter(
        partial_query.reshape(latents, heads_here * HDIM), "ctx", scatter_dimension=0, tiled=True
    )
    key_grad = jnp.einsum("hlk,lhd->khd", dscore, query_heads, preferred_element_type=jnp.float32)
    return (
        latent_out,
        query_grad.astype(jnp.bfloat16),
        key_grad.astype(jnp.bfloat16).reshape(tokens_here, heads_here * HDIM),
        value_grad.astype(jnp.bfloat16).reshape(tokens_here, heads_here * HDIM),
        weight_grad,
    )


def solution(mesh):
    placed = (P(None, "tp"), P("ctx", "tp"), P("ctx", "tp"), P("tp", None), P("ctx", "tp"))
    return jax.shard_map(
        body,
        mesh=mesh,
        in_specs=placed,
        out_specs=(P("ctx", "tp"), P("ctx", "tp"), P("ctx", "tp"), P("ctx", "tp"), P("tp", "ctx")),
        check_vma=False,
    )
```

profile of v0, /device:TPU:1, one launch (start us, length us, event | category | flops | bytes accessed | tf_op | source)
XLA Modules:
  0.0 741.1 jit_solution(15479897217327153881)
XLA Ops:
  7.2 24.7 %all_gather.6 = bf16[32,4096]{1,0:T(8,128)(2,1)S(1)} all-gather(bf16[32,512]{1,0:T(8,128)(2,1)} %param.9), channel_id=1, replica_groups=mesh['ctx'=32,'tp'=8] {'tp'}, dimensions={1}, use_global_device_ids=true | all-gather | bytes 294912 | tf_op jit(solution)/shard_map/all_gather | solution.py:38
  31.9 4.2 convolution_convert_fusion.3
  36.1 1.5 copy.69
  37.6 1.9 copy.70
  39.5 8.1 %multiply_reduce_fusion = (f32[4,1024]{1,0:T(4,128)S(1)}, f32[4,1024,1024]{1,2,0:T(8,128)}) fusion(bf16[1024,4,128]{0,2,1:T(8,128)(2,1)S(1)} %bitcast.52, bf16[1024,4,128]{0,2,1:T(8,128)(2,1)S(1)} %bitcast.46), kind=kOutput, calls=%fused_computation.6 | convolution fusion | flops 1082126336 | bytes 18890752 | tf_op jit(solution)/shard_map/lhd,khd->hlk/dot_general | solution.py:20
  47.6 140.8 %pmax.7 = f32[4,1024]{1,0:T(4,128)S(1)} all-reduce(f32[4,1024]{1,0:T(4,128)S(1)} %get-tuple-element.22), channel_id=1, replica_groups=mesh['ctx'=32,'tp'=8] {'ctx'}, use_global_device_ids=true, to_apply=%region_1.0 | all-reduce | flops 4096 | bytes 32768 | tf_op jit(solution)/shard_map/pmax | solution.py:23
  188.5 10.9 %fusion.11 = f32[1024,4,128]{2,0,1:T(8,128)} fusion(f32[4,1024,1024]{1,2,0:T(8,128)} %get-tuple-element.23, f32[4,1024]{1,0:T(4,128)S(1)} %pmax.7, bf16[1024,512]{1,0:T(8,128)(2,1)S(1)} %copy-done), kind=kOutput, calls=%fused_computation.17 | convolution fusion | flops 1086324736 | bytes 19939328 | tf_op jit(solution)/shard_map/hlk,khd->lhd/dot_general | solution.py:26
  199.4 8.5 %fusion = f32[4,1024]{1,0:T(4,128)S(1)} fusion(f32[4,1024,1024]{1,2,0:T(8,128)} %get-tuple-element.23, f32[4,1024]{1,0:T(4,128)S(1)} %pmax.7), kind=kLoop, calls=%fused_computation.3 | loop fusion | flops 12578816 | bytes 16809984 | tf_op jit(solution)/shard_map/reduce_sum | solution.py:25
  207.9 138.7 %psum.15 = f32[1024,4]{0,1:T(4,128)S(1)} all-reduce(f32[1024,4]{0,1:T(4,128)S(1)} %bitcast.59), channel_id=1, replica_groups=mesh['ctx'=32,'tp'=8] {'ctx'}, use_global_device_ids=true, to_apply=%region_4.0 | all-reduce | flops 4096 | bytes 32768 | tf_op jit(solution)/shard_map/psum | solution.py:29
  346.6 1.5 copy.48
  349.4 139.1 %all-reduce.2.cloned.1.call-done = f32[1024,4,128]{2,0,1:T(8,128)} async-done(((f32[1024,4,128]{2,0,1:T(8,128)}), f32[1024,4,128]{2,0,1:T(8,128)}) %all-reduce.2.cloned.1.call-update) | async-done | bytes 2097168 | tf_op jit(solution)/shard_map/psum | solution.py:29
  488.5 3.5 multiply_reduce_fusion.1
  492.0 8.1 %multiply_convert_fusion = bf16[4,1024,1024]{1,2,0:T(8,128)(2,1)S(1)} fusion(f32[4,1024,1024]{1,2,0:T(8,128)} %get-tuple-element.23, bf16[1024,4,128]{0,2,1:T(8,128)(2,1)S(1)} %bitcast.49, f32[4,1024]{1,0:T(4,128)S(1)} %bitcast.60, f32[4,1024]{1,0:T(4,128)S(1)} %bitcast_add_fusion, bf16[1024,512]{1,0:T(8,128)(2,1)S(1)} %copy-done), kind=kOutput, calls=%fused_computation | convolution fusion | flops 1098907648 | bytes 27295744 | tf_op jit(solution)/shard_map/lhd,khd->hlk/dot_general | solution.py:55
  500.1 3.3 fusion.27
  504.1 2.9 copy.55
  508.6 3.3 convolution_convert_fusion
  511.8 6.5 copy.67
  518.6 10.4 %fusion.14 = bf16[4,128,1024]{2,1,0:T(8,128)(2,1)} fusion(bf16[1024,4,128]{0,2,1:T(8,128)(2,1)S(1)} %bitcast.50, f32[4,1024,1024]{1,2,0:T(8,128)} %get-tuple-element.23, f32[4,1024]{1,0:T(4,128)S(1)} %bitcast_add_fusion), kind=kOutput, calls=%fused_computation.18 | convolution fusion | flops 1086849024 | bytes 18890752 | tf_op jit(solution)/shard_map/hlk,lhd->khd/dot_general | solution.py:52
  529.0 2.3 copy.60
  531.3 4.0 convolution_convert_fusion.1
  535.3 6.4 convolution_convert_fusion.2
  543.1 52.9 %reduce-scatter.8.cloned.1.call-done = f32[32,512]{1,0:T(8,128)} async-done(((f32[1024,512]{1,0:T(8,128)}), f32[32,512]{1,0:T(8,128)}) %reduce-scatter.8.cloned.1.call-update) | async-done | bytes 65552 | tf_op jit(solution)/shard_map/reduce_scatter | solution.py:60
  597.4 100.5 %reduce-scatter.10.cloned.1.call-done = bf16[128,512]{1,0:T(8,128)(2,1)} async-done(((bf16[4096,512]{1,0:T(8,128)(2,1)}), bf16[128,512]{1,0:T(8,128)(2,1)}) %reduce-scatter.10.cloned.1.call-update) | async-done | bytes 131088
  699.7 35.0 %reduce-scatter.6.cloned.1.call-done = bf16[32,512]{1,0:T(8,128)(2,1)} async-done(((bf16[32,4096]{1,0:T(8,128)(2,1)}), bf16[32,512]{1,0:T(8,128)(2,1)}) %reduce-scatter.6.cloned.1.call-update) | async-done | bytes 32784 | tf_op jit(solution)/shard_map/reduce_scatter | solution.py:35
  (28 shorter events, 8.6 us)
Async XLA Ops:
  7.2 181.3 %copy-start = (bf16[1024,512]{1,0:T(8,128)(2,1)S(1)}, bf16[1024,512]{1,0:T(8,128)(2,1)}, u32[]{:S(2)}) copy-start(bf16[1024,512]{1,0:T(8,128)(2,1)} %param.7) | copy-start | bytes 3145732
  7.2 339.4 %all-gather.2.cloned.1.call-start = ((), (), s32[]{:S(2)}) async-start(), calls=%async_computation.5 | async-start | bytes 1081344 | tf_op jit(solution)/shard_map/all_gather | solution.py:48
  36.1 452.4 %all-reduce.2.cloned.1.call-start = ((), (), s32[]{:S(2)}) async-start(), calls=%async_computation.3 | async-start | bytes 4194304 | tf_op jit(solution)/shard_map/psum | solution.py:29
  37.6 10.0 %copy-start.2 = (bf16[1024,512]{0,1:T(8,128)(2,1)}, bf16[1024,512]{0,1:T(8,128)(2,1)S(1)}, u32[]{:S(2)}) copy-start(bf16[1024,512]{0,1:T(8,128)(2,1)S(1)} %copy.69) | copy-start | bytes 3145732
  199.3 396.6 %reduce-scatter.8.cloned.1.call-start = ((), (), s32[]{:S(2)}) async-start(), calls=%async_computation.6 | async-start | bytes 2162688 | tf_op jit(solution)/shard_map/reduce_scatter | solution.py:60
  500.1 4.0 copy-start.1
  507.0 190.9 %reduce-scatter.10.cloned.1.call-start = ((), (), s32[]{:S(2)}) async-start(), calls=%async_computation.7 | async-start | bytes 4325376
  508.5 9.8 %copy-start.4 = (bf16[1024,4,128]{0,2,1:T(8,128)(2,1)}, bf16[1024,4,128]{0,2,1:T(8,128)(2,1)S(1)}, u32[]{:S(2)}) copy-start(bf16[1024,4,128]{0,2,1:T(8,128)(2,1)S(1)} %copy.47) | copy-start | bytes 3145732
  518.3 17.0 %copy-start.3 = (bf16[1024,512]{0,1:T(8,128)(2,1)S(1)}, bf16[1024,512]{0,1:T(8,128)(2,1)}, u32[]{:S(2)}) copy-start(bf16[1024,512]{0,1:T(8,128)(2,1)} %copy-done.2) | copy-start | bytes 3145732
  518.3 216.3 %reduce-scatter.6.cloned.1.call-start = ((), (), s32[]{:S(2)}) async-start(), calls=%async_computation.4 | async-start | bytes 294912 | tf_op jit(solution)/shard_map/reduce_scatter | solution.py:35
Sparse Core Ops, SparseCore 0:
  36.2 60.0 all-gather.1
  199.5 288.9 all-reduce.1
  507.1 88.7 reduce-scatter.7
  600.3 97.5 reduce-scatter.9
  700.8 33.7 reduce-scatter.5
where the time goes:
time: 746 us; the launch traced here: 741 us
  waiting for transfers between devices  328 us (44%)
  blocking collectives  304 us (41%)
  matrix products  58.6 us (8%)
  local copies, waits for them, and re-layouts  22.4 us (3%)
  other arithmetic  14.2 us (2%)
  between operations  13.9 us (2%)
    pmax x1, blocking collectives, body(): row_top = lax.pmax(jnp.max(scores, axis=2), 'ctx')  141 us
    psum x1, waiting for transfers between devices, body(): numer, denom = lax.psum((partial_num, partial_den), 'ctx')  139 us
    psum x1, blocking collectives, body(): numer, denom = lax.psum((partial_num, partial_den), 'ctx')  139 us
    unnamed x6, waiting for transfers between devices  101 us
    reduce_scatter x1, waiting for transfers between devices, body(): lax.psum_scatter(partial_query.reshape(latents, heads_here * HDIM), 'ctx'...  52.9 us
    reduce_scatter x1, waiting for transfers between devices, body(): lax.psum_scatter(partial_out.astype(jnp.bfloat16), 'tp', scatter_dimensio...  35 us
    all_gather x1, blocking collectives, body(): grad_full = lax.all_gather(out_grad, 'tp', axis=1, tiled=True)  24.7 us
  transfers between devices with their start and end apart: 5, of which 4 were waited for; matrix products, arithmetic and copies ran while one was open for 10% of the time, Pallas kernels for 0%

commit v1 on v0

v1 whole, which is shorter than its diff:
```python
import functools
import math

import jax
import jax.numpy as jnp
from jax import lax
from jax.experimental import pallas as pl
from jax.experimental.pallas import tpu as pltpu
from jax.sharding import Mesh
from jax.sharding import PartitionSpec as P

HDIM = 128
SCALE = HDIM ** (-0.5)
LOG2E = math.log2(math.e)
EXP2_SCALE = SCALE * LOG2E
CHIPS = ("y", "zh")
CTX = ("y", "zh", "core")
TP = ("x", "zl")
N_CHIPS = 16
HEADS_HERE = 2
WIDE = HEADS_HERE * HDIM
NUM, DOUT, COT, STAT = 64, 64, 32, 16
ROWS1 = NUM + DOUT + COT + STAT
ROWS2 = NUM + STAT
F32 = jnp.float32
BF16 = jnp.bfloat16
VMEM_BYTES = 50 * 1024 * 1024


def dot(a, b, ca, cb):
    return lax.dot_general(a, b, (((ca,), (cb,)), ((), ())), preferred_element_type=F32)


def in_three(x):
    high = x.astype(BF16)
    rest = x - high.astype(F32)
    middle = rest.astype(BF16)
    low = (rest - middle.astype(F32)).astype(BF16)
    return high, middle, low


def of_three(block, at):
    return (
        block[at : at + 1, :].astype(F32)
        + block[at + 1 : at + 2, :].astype(F32)
        + block[at + 2 : at + 3, :].astype(F32)
    )


def forward_kernel(core_ref, q_ref, ko_ref, kr_ref, vo_ref, vr_ref, dout_ref, cot_ref, msg_ref):
    pieces = []
    for h in range(HEADS_HERE):
        cols = slice(h * HDIM, (h + 1) * HDIM)
        q = q_ref[:, cols]
        scores = [dot(k[:, cols], q, 1, 1) for k in (ko_ref, kr_ref)]
        top = jnp.maximum(
            jnp.max(scores[0], axis=0, keepdims=True), jnp.max(scores[1], axis=0, keepdims=True)
        )
        shift = top * EXP2_SCALE
        expo = [jnp.exp2(s * EXP2_SCALE - shift) for s in scores]
        den = jnp.sum(expo[0], axis=0, keepdims=True) + jnp.sum(expo[1], axis=0, keepdims=True)
        num = dot(vo_ref[:, cols], expo[0].astype(BF16), 0, 0) + dot(
            vr_ref[:, cols], expo[1].astype(BF16), 0, 0
        )
        part = jnp.transpose(num / den).astype(BF16)
        msg_ref[:, 0:NUM, cols] = part.reshape(4, NUM, HDIM)
        pieces.extend(in_three(top * SCALE + jnp.log(den)))
    for d in range(4):
        msg_ref[d, NUM : NUM + DOUT, :] = dout_ref[...]
        msg_ref[d, NUM + DOUT : NUM + DOUT + COT, :] = cot_ref[
            d // 2, :, (d % 2) * WIDE : (d % 2 + 1) * WIDE
        ]
    stats = jnp.concatenate(pieces + [jnp.zeros((STAT - 6, WIDE), BF16)], axis=0)
    for d in range(4):
        msg_ref[d, NUM + DOUT + COT :, :] = stats


def forward(core, queries, keys, keys_in, values, values_in, dout64, cot):
    tokens = keys.shape[0]
    grid_spec = pltpu.PrefetchScalarGridSpec(
        num_scalar_prefetch=1,
        grid=(4,),
        in_specs=[
            pl.BlockSpec((WIDE, WIDE), lambda i, c: (i, c[0])),
            pl.BlockSpec((tokens, WIDE), lambda i, c: (0, c[0])),
            pl.BlockSpec((tokens, WIDE), lambda i, c: (0, 0)),
            pl.BlockSpec((tokens, WIDE), lambda i, c: (0, c[0])),
            pl.BlockSpec((tokens, WIDE), lambda i, c: (0, 0)),
            pl.BlockSpec((DOUT, WIDE), lambda i, c: (0, 0)),
            pl.BlockSpec((2, COT, 2 * WIDE), lambda i, c: (i, 0, 0)),
        ],
        out_specs=pl.BlockSpec((4, ROWS1, WIDE), lambda i, c: (i, 0, 0)),
    )
    return pl.pallas_call(
        forward_kernel,
        out_shape=jax.ShapeDtypeStruct((N_CHIPS, ROWS1, WIDE), BF16),
        grid_spec=grid_spec,
        compiler_params=pltpu.CompilerParams(vmem_limit_bytes=VMEM_BYTES),
        name="forward",
    )(core, queries, keys, keys_in, values, values_in, dout64, cot)


def combine_kernel(zh_ref, num_ref, stat_ref, dout_ref, msg_ref):
    zh = zh_ref[0]
    lanes = lax.broadcasted_iota(jnp.int32, (1, WIDE), 1)
    pieces = []
    deltas = []
    att_all = []
    for h in range(HEADS_HERE):
        cols = slice(h * HDIM, (h + 1) * HDIM)
        lse = jnp.concatenate([of_three(stat_ref[c], 3 * h) for c in range(N_CHIPS)], axis=0)
        mine = jnp.zeros((N_CHIPS, NUM), F32)
        for z in range(4):
            mine = jnp.where(zh == z, lse[:, z * NUM : (z + 1) * NUM], mine)
        top = jnp.max(mine, axis=0, keepdims=True)
        total = top + jnp.log(jnp.sum(jnp.exp(mine - top), axis=0, keepdims=True))
        weight = jnp.transpose(jnp.exp(mine - total))
        att = jnp.zeros((NUM, HDIM), F32)
        for c in range(N_CHIPS):
            att = att + num_ref[c, :, cols].astype(F32) * weight[:, c : c + 1]
        att = att.astype(BF16)
        att_all.append(att)
        delta = jnp.sum(att.astype(F32) * dout_ref[:, cols].astype(F32), axis=1, keepdims=True)
        pieces.extend(in_three(total))
        deltas.extend(in_three(jnp.transpose(jnp.broadcast_to(delta, (NUM, HDIM)))[0:1, :]))
    stats = jnp.concatenate(pieces + deltas + [jnp.zeros((STAT - 12, NUM), BF16)], axis=0)
    stats = jnp.concatenate([stats, jnp.zeros((STAT, WIDE - NUM), BF16)], axis=1)
    att = jnp.concatenate(att_all, axis=1)
    for c in range(N_CHIPS):
        msg_ref[c, 0:NUM, :] = att
        msg_ref[c, NUM:, :] = stats


def combine(zh, msg, dout64):
    grid_spec = pltpu.PrefetchScalarGridSpec(
        num_scalar_prefetch=1,
        grid=(1,),
        in_specs=[
            pl.BlockSpec((N_CHIPS, NUM, WIDE), lambda i, z: (0, 0, 0)),
            pl.BlockSpec((N_CHIPS, STAT, WIDE), lambda i, z: (0, (ROWS1 - STAT) // STAT, 0)),
            pl.BlockSpec((DOUT, WIDE), lambda i, z: (0, 0)),
        ],
        out_specs=pl.BlockSpec((N_CHIPS, ROWS2, WIDE), lambda i, z: (0, 0, 0)),
    )
    return pl.pallas_call(
        combine_kernel,
        out_shape=jax.ShapeDtypeStruct((N_CHIPS, ROWS2, WIDE), BF16),
        grid_spec=grid_spec,
        compiler_params=pltpu.CompilerParams(vmem_limit_bytes=VMEM_BYTES),
        name="combine",
    )(zh, msg, msg, dout64)


def backward_kernel(
    core_ref, q_ref, dout_ref, stat_ref, ko_ref, kr_ref, vo_ref, vr_ref,
    dq_ref, dko_ref, dkr_ref, dvo_ref, dvr_ref, dq_acc, stat_acc,
):
    step = pl.program_id(0)
    latents = q_ref.shape[0]

    @pl.when(step == 0)
    def _():
        dq_acc[...] = jnp.zeros_like(dq_acc)
        for pair in range(N_CHIPS // 2):
            both = []
            for c in (2 * pair, 2 * pair + 1):
                block = stat_ref[c]
                both.append(
                    jnp.concatenate([of_three(block, 3 * r)[:, :NUM] for r in range(4)], axis=0)
                )
            stat_acc[0:4, pair * 2 * NUM : (pair + 1) * 2 * NUM] = jnp.concatenate(both, axis=1)

    for h in range(HEADS_HERE):
        cols = slice(h * HDIM, (h + 1) * HDIM)
        q = q_ref[:, cols]
        dout = dout_ref[:, :, cols].reshape(latents, HDIM)
        lse = stat_acc[h : h + 1, :] * LOG2E
        delta = stat_acc[2 + h : 3 + h, :]
        for k_ref, v_ref, dk_ref, dv_ref in (
            (ko_ref, vo_ref, dko_ref, dvo_ref),
            (kr_ref, vr_ref, dkr_ref, dvr_ref),
        ):
            k = k_ref[:, cols]
            scores = dot(k, q, 1, 1)
            probs = jnp.exp2(scores * EXP2_SCALE - lse)
            dprob = dot(v_ref[:, cols], dout, 1, 1)
            dscore = (probs * (dprob - delta)).astype(BF16)
            dv_ref[:, cols] = dot(probs.astype(BF16), dout, 1, 0).astype(BF16)
            dk_ref[:, cols] = (dot(dscore, q, 1, 0) * SCALE).astype(BF16)
            dq_acc[cols, :] += dot(k, dscore, 0, 0)

    @pl.when(step == pl.num_programs(0) - 1)
    def _():
        dq_ref[...] = jnp.transpose(dq_acc[...] * SCALE).astype(BF16)


def backward(core, queries, msg1, msg2, keys, keys_in, values, values_in):
    latents = queries.shape[0]
    tokens = keys.shape[0]
    block = 256
    own = pl.BlockSpec((block, WIDE), lambda i, c: (i, c[0]))
    plain = pl.BlockSpec((block, WIDE), lambda i, c: (i, 0))
    grid_spec = pltpu.PrefetchScalarGridSpec(
        num_scalar_prefetch=1,
        grid=(tokens // block,),
        in_specs=[
            pl.BlockSpec((latents, WIDE), lambda i, c: (0, c[0])),
            pl.BlockSpec((N_CHIPS, DOUT, WIDE), lambda i, c: (0, 1, 0)),
            pl.BlockSpec((N_CHIPS, STAT, WIDE), lambda i, c: (0, NUM // STAT, 0)),
            own, plain, own, plain,
        ],
        out_specs=[
            pl.BlockSpec((latents, WIDE), lambda i, c: (0, 0)),
            plain, plain, plain, plain,
        ],
        scratch_shapes=[pltpu.VMEM((WIDE, latents), F32), pltpu.VMEM((8, latents), F32)],
    )
    part = jax.ShapeDtypeStruct((tokens, WIDE), BF16)
    return pl.pallas_call(
        backward_kernel,
        out_shape=[jax.ShapeDtypeStruct((latents, WIDE), BF16), part, part, part, part],
        grid_spec=grid_spec,
        compiler_params=pltpu.CompilerParams(vmem_limit_bytes=VMEM_BYTES),
        name="backward",
    )(core, queries, msg1, msg2, keys, keys_in, values, values_in)


def swap(x):
    return lax.ppermute(x, "core", [(0, 1), (1, 0)])


def half(x, index, axis):
    size = x.shape[axis] // 2
    return lax.dynamic_slice_in_dim(x, index * size, size, axis)


def in_order(core, mine, other, axis):
    return jnp.where(
        core == 0,
        jnp.concatenate([mine, other], axis),
        jnp.concatenate([other, mine], axis),
    )


def gather(x, axes, size):
    tiled = jnp.broadcast_to(x[None], (size,) + x.shape)
    return lax.all_to_all(tiled, axes, 0, 0, tiled=True)


def body(queries, prefix_keys, prefix_values, out_weight, out_grad):
    core = lax.axis_index("core")
    core_arr = core.astype(jnp.int32).reshape(1)
    zh_arr = lax.axis_index("zh").astype(jnp.int32).reshape(1)
    keys_in = swap(half(prefix_keys, 1 - core, 1))
    values_in = swap(half(prefix_values, 1 - core, 1))

    cot = gather(out_grad, TP, 8)
    cot_rows = jnp.concatenate([cot[i] for i in range(8)], axis=1)
    dout32 = dot(cot_rows, out_weight, 1, 1).astype(BF16)
    dout_in = swap(half(dout32, 1 - core, 1))
    dout64 = in_order(core, half(dout32, core, 1), dout_in, 0)

    msg1 = forward(
        core_arr, queries, prefix_keys, keys_in, prefix_values, values_in, dout64, cot
    )
    msg1 = lax.all_to_all(msg1, CHIPS, 0, 0, tiled=True)
    msg2 = combine(zh_arr, msg1, dout64)
    att64 = msg2[0, :NUM]
    att32 = in_order(core, half(att64, core, 0), swap(half(att64, 1 - core, 0)), 1)
    partial_out = dot(att32, out_weight, 1, 0).astype(BF16)
    latent_out = lax.psum_scatter(partial_out, TP, scatter_dimension=1, tiled=True)

    msg2 = lax.all_to_all(msg2, CHIPS, 0, 0, tiled=True)
    dq, dko, dkr, dvo, dvr = backward(
        core_arr, queries, msg1, msg2, prefix_keys, keys_in, prefix_values, values_in
    )
    dk_in = swap(dkr)
    dv_in = swap(dvr)

    cot_mine = msg1[:, NUM + DOUT : NUM + DOUT + COT, :]
    cot_all = in_order(core, cot_mine, swap(cot_mine), 1).reshape(N_CHIPS * NUM, WIDE)
    att_all = msg2[:, :NUM, :].reshape(N_CHIPS * NUM, WIDE)
    weight_part = dot(att_all, cot_all, 0, 0)
    weight_grad = in_order(
        core, half(weight_part, core, 1), swap(half(weight_part, 1 - core, 1)), 0
    )

    dq = lax.all_to_all(dq.reshape(N_CHIPS, NUM, WIDE), CHIPS, 0, 0, tiled=True)
    dq64 = jnp.sum(dq.astype(F32), axis=0).astype(BF16)
    query_grad = in_order(core, half(dq64, core, 0), swap(half(dq64, 1 - core, 0)), 1)
    key_grad = in_order(core, dko, dk_in, 1)
    value_grad = in_order(core, dvo, dv_in, 1)
    return latent_out, query_grad, key_grad, value_grad, weight_grad


def solution(mesh):
    fine = Mesh(mesh.devices.reshape(4, 4, 2, 4, 2), ("y", "zh", "core", "x", "zl"))
    placed = (P(None, TP), P(CTX, TP), P(CTX, TP), P(TP, None), P(CTX, TP))
    return jax.shard_map(
        body,
        mesh=fine,
        in_specs=placed,
        out_specs=(P(CTX, TP), P(CTX, TP), P(CTX, TP), P(CTX, TP), P(TP, CTX)),
        check_vma=False,
    )
```

time: 746 us -> 184 us (0.25)
  the two profiles are of different devices: /device:TPU:1 before, /device:TPU:8 now
where the time goes in v1:
time: 184 us; the launch traced here: 183 us
  waiting for transfers between devices  93.7 us (51%)
  starting transfers between devices  30.7 us (17%)
  Pallas kernels  26.1 us (14%)
  between operations  14.3 us (8%)
  matrix products  6.92 us (4%)
  local copies, waits for them, and re-layouts  6.08 us (3%)
  other arithmetic  5.06 us (3%)
    all_to_all x1, waiting for transfers between devices, body(): msg1 = lax.all_to_all(msg1, CHIPS, 0, 0, tiled=True)  36.6 us
    reduce_scatter x1, waiting for transfers between devices, body(): lax.psum_scatter(partial_out, TP, scatter_dimension=1, tiled=True)  28.3 us
    all_to_all x1, waiting for transfers between devices, body(): msg2 = lax.all_to_all(msg2, CHIPS, 0, 0, tiled=True)  16.7 us
    pallas_call x1, Pallas kernels, backward(): pl.pallas_call(backward_kernel, out_shape=[jax.ShapeDtypeStruct((latents,...  13.6 us
    all_to_all x1, starting transfers between devices, body(): msg1 = lax.all_to_all(msg1, CHIPS, 0, 0, tiled=True)  10.7 us
    pallas_call x1, Pallas kernels, forward(): pl.pallas_call(forward_kernel, out_shape=jax.ShapeDtypeStruct((N_CHIPS, R...  10.6 us
    dot_general x3, matrix products, dot(): lax.dot_general(a, b, (((ca,), (cb,)), ((), ())), preferred_element_type=...  6.92 us
    all_to_all x1, waiting for transfers between devices, body(): dq = lax.all_to_all(dq.reshape(N_CHIPS, NUM, WIDE), CHIPS, 0, 0, tiled=True)  6.84 us
  transfers between devices with their start and end apart: 14, of which 6 were waited for; matrix products, arithmetic and copies ran while one was open for 9% of the time, Pallas kernels for 7%

profile of v1, /device:TPU:8, one launch (start us, length us, event | category | flops | bytes accessed | tf_op | source)
XLA Modules:
  0.0 182.8 jit_solution(12287947124024156299)
XLA Ops:
  7.2 1.6 broadcast_in_dim.2
  8.7 5.7 %all-to-all-start = ((bf16[8,32,512]{2,1,0:T(8,128)(2,1)}), bf16[8,32,512]{2,1,0:T(8,128)(2,1)S(1)}, u32[]{:S(2)}, u32[]{:S(2)}) async-start(bf16[8,32,512]{2,1,0:T(8,128)(2,1)} %broadcast_in_dim.2), calls=%async_computation | async-start | bytes 524288 | tf_op jit(solution)/shard_map/all_to_all | solution.py:247
  14.4 1.9 %constant_dynamic-slice_fusion.7 = bf16[1024,256]{1,0:T(8,128)(2,1)} fusion(bf16[1024,512]{1,0:T(8,128)(2,1)} %ko_ref.3, s32[]{:T(128)S(6)} %select_n.71), kind=kLoop, calls=%fused_computation.48 | loop fusion | bytes 1048580 | tf_op jit(solution)/shard_map/dynamic_slice | solution.py:234
  16.3 0.8 constant_dynamic-slice_fusion.6
  17.6 4.1 %all-to-all-done.cot_ref = bf16[8,32,512]{2,1,0:T(8,128)(2,1)S(1)} async-done(((bf16[8,32,512]{2,1,0:T(8,128)(2,1)}), bf16[8,32,512]{2,1,0:T(8,128)(2,1)S(1)}, u32[]{:S(2)}, u32[]{:S(2)}) %all-to-all-start) | async-done | bytes 262176 | tf_op jit(solution)/shard_map/all_to_all | solution.py:247
  21.8 3.7 %convolution_convert_fusion.1 = bf16[32,512]{1,0:T(8,128)(2,1)S(1)} fusion(bf16[32,4096]{1,0:T(8,128)(2,1)S(1)} %fusion.7, bf16[512,4096]{1,0:T(8,128)(2,1)} %param.8), kind=kOutput, calls=%fused_computation.2 | convolution fusion | flops 134234112 | bytes 4489216 | tf_op jit(solution)/shard_map/dot_general | solution.py:31
  25.6 1.2 collective-permute-done.2
  26.9 10.6 %forward.1 = bf16[16,176,256]{2,1,0:T(8,128)(2,1)} custom-call(s32[1]{0:T(128)} %bitcast.1.core_ref, bf16[1024,512]{1,0:T(8,128)(2,1)S(1)} %copy-done.2, bf16[1024,512]{1,0:T(8,128)(2,1)S(1)} %copy-done.1, bf16[1024,256]{1,0:T(8,128)(2,1)S(1)} %collective-permute-done.kr_ref, bf16[1024,512]{1,0:T(8,128)(2,1)} %vo_ref.3, ...), custom_call_target="tpu_custom_call" | custom-call | tf_op jit(solution)/shard_map/forward/pallas_call | solution.py:94
  37.4 10.7 %all-to-all-start.1 = ((bf16[16,176,256]{2,1,0:T(8,128)(2,1)}), bf16[16,176,256]{2,1,0:T(8,128)(2,1)S(1)}, u32[]{:S(2)}, u32[]{:S(2)}) async-start(bf16[16,176,256]{2,1,0:T(8,128)(2,1)} %forward.1), calls=%async_computation.1 | async-start | bytes 2883584 | tf_op jit(solution)/shard_map/all_to_all | solution.py:266
  48.1 36.6 %all-to-all-done.1.num_ref.stat_ref.dout_ref = bf16[16,176,256]{2,1,0:T(8,128)(2,1)S(1)} async-done(((bf16[16,176,256]{2,1,0:T(8,128)(2,1)}), bf16[16,176,256]{2,1,0:T(8,128)(2,1)S(1)}, u32[]{:S(2)}, u32[]{:S(2)}) %all-to-all-start.1) | async-done | bytes 1441824 | tf_op jit(solution)/shard_map/all_to_all | solution.py:266
  84.8 0.8 copy-done.8
  85.5 2.0 %combine.1 = bf16[16,80,256]{2,1,0:T(8,128)(2,1)} custom-call(s32[1]{0:T(128)} %bitcast.zh_ref, bf16[16,176,256]{2,1,0:T(8,128)(2,1)S(1)} %all-to-all-done.1.num_ref.stat_ref.dout_ref, bf16[16,176,256]{2,1,0:T(8,128)(2,1)S(1)} %all-to-all-done.1.num_ref.stat_ref.dout_ref, bf16[64,256]{1,0:T(8,128)(2,1)S(1)} %copy-done.8), custom_call_target="tpu_custom_call" | custom-call | tf_op jit(solution)/shard_map/combine/pallas_call | solution.py:145
  87.5 6.5 %all-to-all-start.2 = ((bf16[16,80,256]{2,1,0:T(8,128)(2,1)}), bf16[16,80,256]{2,1,0:T(8,128)(2,1)}, u32[]{:S(2)}, u32[]{:S(2)}) async-start(bf16[16,80,256]{2,1,0:T(8,128)(2,1)} %combine.1), calls=%async_computation.3 | async-start | bytes 1310720 | tf_op jit(solution)/shard_map/all_to_all | solution.py:273
  94.2 0.8 slice.52
  94.9 16.7 %all-to-all-done.2.stat_ref = bf16[16,80,256]{2,1,0:T(8,128)(2,1)} async-done(((bf16[16,80,256]{2,1,0:T(8,128)(2,1)}), bf16[16,80,256]{2,1,0:T(8,128)(2,1)}, u32[]{:S(2)}, u32[]{:S(2)}) %all-to-all-start.2) | async-done | bytes 655392 | tf_op jit(solution)/shard_map/all_to_all | solution.py:273
  111.6 13.6 %backward.1 = (bf16[1024,256]{1,0:T(8,128)(2,1)}, bf16[1024,256]{1,0:T(8,128)(2,1)S(1)}, bf16[1024,256]{1,0:T(8,128)(2,1)S(1)}, bf16[1024,256]{1,0:T(8,128)(2,1)S(1)}, bf16[1024,256]{1,0:T(8,128)(2,1)S(1)}) custom-call(s32[1]{0:T(128)} %bitcast.1.core_ref, bf16[1024,512]{1,0:T(8,128)(2,1)} %q_ref.3, bf16[16,176,256]{2,1,0:T(8,128)(2,1)} %copy-done, ...), custom_call_target="tpu_custom_call" | custom-call | tf_op jit(solution)/shard_map/backward/pallas_call | solution.py:219
  125.2 5.8 %all-to-all-start.3 = ((bf16[16,64,256]{2,1,0:T(8,128)(2,1)}), bf16[16,64,256]{2,1,0:T(8,128)(2,1)S(1)}, u32[]{:S(2)}, u32[]{:S(2)}) async-start(bf16[16,64,256]{2,1,0:T(8,128)(2,1)} %bitcast.12), calls=%async_computation.4 | async-start | bytes 1048576 | tf_op jit(solution)/shard_map/all_to_all | solution.py:288
  131.7 1.7 convolution_bitcast_fusion
  134.1 1.5 convolution_convert_fusion
  135.7 0.7 maximum_select_fusion.4
  136.4 2.4 %maximum_select_fusion = bf16[1024,512]{1,0:T(8,128)(2,1)} fusion(bf16[1024,256]{1,0:T(8,128)(2,1)} %collective-permute-done.5, bf16[1024,256]{1,0:T(8,128)(2,1)S(1)} %get-tuple-element.11, pred[]{:T(512)S(6)} %eq.2), kind=kLoop, calls=%fused_computation.3 | loop fusion | flops 4718592 | bytes 2097153 | tf_op jit(solution)/shard_map/jit(_where)/select_n | solution.py:238
  138.8 6.8 %all-to-all-done.3 = bf16[16,64,256]{2,1,0:T(8,128)(2,1)S(1)} async-done(((bf16[16,64,256]{2,1,0:T(8,128)(2,1)}), bf16[16,64,256]{2,1,0:T(8,128)(2,1)S(1)}, u32[]{:S(2)}, u32[]{:S(2)}) %all-to-all-start.3) | async-done | bytes 524320 | tf_op jit(solution)/shard_map/all_to_all | solution.py:288
  145.9 1.2 maximum_select_fusion.1
  147.7 28.3 %reduce-scatter.2.cloned.1.call-done = bf16[32,512]{1,0:T(8,128)(2,1)} async-done(((bf16[32,4096]{1,0:T(8,128)(2,1)}), bf16[32,512]{1,0:T(8,128)(2,1)}) %reduce-scatter.2.cloned.1.call-update) | async-done | bytes 32784 | tf_op jit(solution)/shard_map/reduce_scatter | solution.py:271
  (56 shorter events, 3.1 us)
Async XLA Ops:
  7.2 9.1 %copy-start.10 = (bf16[1024,512]{1,0:T(8,128)(2,1)S(1)}, bf16[1024,512]{1,0:T(8,128)(2,1)}, u32[]{:S(2)}) copy-start(bf16[1024,512]{1,0:T(8,128)(2,1)} %vo_ref.3) | copy-start | bytes 3145732
  8.7 12.9 %all-to-all-start = ((bf16[8,32,512]{2,1,0:T(8,128)(2,1)}), bf16[8,32,512]{2,1,0:T(8,128)(2,1)S(1)}, u32[]{:S(2)}, u32[]{:S(2)}) async-start(bf16[8,32,512]{2,1,0:T(8,128)(2,1)} %broadcast_in_dim.2), calls=%async_computation | async-start | bytes 524288 | tf_op jit(solution)/shard_map/all_to_all | solution.py:247
  16.3 10.5 %collective-permute-start = (bf16[1024,256]{1,0:T(8,128)(2,1)}, bf16[1024,256]{1,0:T(8,128)(2,1)S(1)}, u32[]{:S(2)}, u32[]{:S(2)}) collective-permute-start(bf16[1024,256]{1,0:T(8,128)(2,1)} %constant_dynamic-slice_fusion.7), channel_id=1, source_target_pairs={{0,8},{8,0},{1,9},{9,1},{2,10},{10,2},{3,11},{11,3},{4,12},{12,4},... | collective-permute-start | bytes 1572872 | tf_op jit(solution)/shard_map/ppermute | solution.py:229
  17.1 9.7 %collective-permute-start.1 = (bf16[1024,256]{1,0:T(8,128)(2,1)}, bf16[1024,256]{1,0:T(8,128)(2,1)S(1)}, u32[]{:S(2)}, u32[]{:S(2)}) collective-permute-start(bf16[1024,256]{1,0:T(8,128)(2,1)} %constant_dynamic-slice_fusion.6), channel_id=1, source_target_pairs={{0,8},{8,0},{1,9},{9,1},{2,10},{10,2},{3,11},{11,3},{4,12},{12,4},... | collective-permute-start | bytes 1572872 | tf_op jit(solution)/shard_map/ppermute | solution.py:229
  21.8 5.1 %copy-start.1 = (bf16[1024,512]{1,0:T(8,128)(2,1)S(1)}, bf16[1024,512]{1,0:T(8,128)(2,1)}, u32[]{:S(2)}) copy-start(bf16[1024,512]{1,0:T(8,128)(2,1)} %ko_ref.3) | copy-start | bytes 3145732
  21.8 5.1 %copy-start.2 = (bf16[1024,512]{1,0:T(8,128)(2,1)S(1)}, bf16[1024,512]{1,0:T(8,128)(2,1)}, u32[]{:S(2)}) copy-start(bf16[1024,512]{1,0:T(8,128)(2,1)} %q_ref.3) | copy-start | bytes 3145732
  25.5 1.3 collective-permute-start.2
  26.8 10.7 %copy-start.7 = (bf16[64,256]{1,0:T(8,128)(2,1)}, bf16[64,256]{1,0:T(8,128)(2,1)S(1)}, u32[]{:S(2)}) copy-start(bf16[64,256]{1,0:T(8,128)(2,1)S(1)} %maximum_select_fusion.5.dout_ref) | copy-start | bytes 98308
  26.8 10.6 %copy-start.3 = (bf16[1024,256]{1,0:T(8,128)(2,1)}, bf16[1024,256]{1,0:T(8,128)(2,1)S(1)}, u32[]{:S(2)}) copy-start(bf16[1024,256]{1,0:T(8,128)(2,1)S(1)} %collective-permute-done.kr_ref) | copy-start | bytes 1572868
  26.8 10.6 %copy-start.5 = (bf16[1024,256]{1,0:T(8,128)(2,1)}, bf16[1024,256]{1,0:T(8,128)(2,1)S(1)}, u32[]{:S(2)}) copy-start(bf16[1024,256]{1,0:T(8,128)(2,1)S(1)} %collective-permute-done.1.vr_ref) | copy-start | bytes 1572868
  37.4 47.3 %all-to-all-start.1 = ((bf16[16,176,256]{2,1,0:T(8,128)(2,1)}), bf16[16,176,256]{2,1,0:T(8,128)(2,1)S(1)}, u32[]{:S(2)}, u32[]{:S(2)}) async-start(bf16[16,176,256]{2,1,0:T(8,128)(2,1)} %forward.1), calls=%async_computation.1 | async-start | bytes 2883584 | tf_op jit(solution)/shard_map/all_to_all | solution.py:266
  84.7 9.3 %copy-start = (bf16[16,176,256]{2,1,0:T(8,128)(2,1)}, bf16[16,176,256]{2,1,0:T(8,128)(2,1)S(1)}, u32[]{:S(2)}) copy-start(bf16[16,176,256]{2,1,0:T(8,128)(2,1)S(1)} %all-to-all-done.1.num_ref.stat_ref.dout_ref) | copy-start | bytes 4325380
  85.5 26.1 %copy-start.4 = (bf16[1024,256]{1,0:T(8,128)(2,1)S(1)}, bf16[1024,256]{1,0:T(8,128)(2,1)}, u32[]{:S(2)}) copy-start(bf16[1024,256]{1,0:T(8,128)(2,1)} %copy-done.3) | copy-start | bytes 1572868
  85.5 26.1 %copy-start.6 = (bf16[1024,256]{1,0:T(8,128)(2,1)S(1)}, bf16[1024,256]{1,0:T(8,128)(2,1)}, u32[]{:S(2)}) copy-start(bf16[1024,256]{1,0:T(8,128)(2,1)} %copy-done.5) | copy-start | bytes 1572868
  87.5 24.1 %all-to-all-start.2 = ((bf16[16,80,256]{2,1,0:T(8,128)(2,1)}), bf16[16,80,256]{2,1,0:T(8,128)(2,1)}, u32[]{:S(2)}, u32[]{:S(2)}) async-start(bf16[16,80,256]{2,1,0:T(8,128)(2,1)} %combine.1), calls=%async_computation.3 | async-start | bytes 1310720 | tf_op jit(solution)/shard_map/all_to_all | solution.py:273
  94.1 37.6 %collective-permute-start.7 = (bf16[16,32,256]{2,1,0:T(8,128)(2,1)S(1)}, bf16[16,32,256]{2,1,0:T(8,128)(2,1)}, u32[]{:S(2)}, u32[]{:S(2)}) collective-permute-start(bf16[16,32,256]{2,1,0:T(8,128)(2,1)S(1)} %slice.54), channel_id=1, source_target_pairs={{0,8},{8,0},{1,9},{9,1},{2,10},{10,2},{3,11},{11,3},{4,12},{12,4},... | collective-permute-start | bytes 786440 | tf_op jit(solution)/shard_map/ppermute | solution.py:229
  125.2 20.5 %all-to-all-start.3 = ((bf16[16,64,256]{2,1,0:T(8,128)(2,1)}), bf16[16,64,256]{2,1,0:T(8,128)(2,1)S(1)}, u32[]{:S(2)}, u32[]{:S(2)}) async-start(bf16[16,64,256]{2,1,0:T(8,128)(2,1)} %bitcast.12), calls=%async_computation.4 | async-start | bytes 1048576 | tf_op jit(solution)/shard_map/all_to_all | solution.py:288
  130.9 45.0 %reduce-scatter.2.cloned.1.call-start = ((), (), s32[]{:S(2)}) async-start(), calls=%async_computation.5 | async-start | bytes 294912 | tf_op jit(solution)/shard_map/reduce_scatter | solution.py:271
  131.0 3.0 %collective-permute-start.3 = (bf16[32,256]{1,0:T(8,128)(2,1)S(1)}, bf16[32,256]{1,0:T(8,128)(2,1)S(1)}, u32[]{:S(2)}, u32[]{:S(2)}) collective-permute-start(bf16[32,256]{1,0:T(8,128)(2,1)S(1)} %get-tuple-element.20), channel_id=1, source_target_pairs={{0,8},{8,0},{1,9},{9,1},{2,10},{10,2},{3,11},{11,3},{4,12},{12,4},... | collective-permute-start | bytes 49160 | tf_op jit(solution)/shard_map/ppermute | solution.py:229
  131.1 5.3 %collective-permute-start.5 = (bf16[1024,256]{1,0:T(8,128)(2,1)S(1)}, bf16[1024,256]{1,0:T(8,128)(2,1)}, u32[]{:S(2)}, u32[]{:S(2)}) collective-permute-start(bf16[1024,256]{1,0:T(8,128)(2,1)S(1)} %get-tuple-element.12), channel_id=1, source_target_pairs={{0,8},{8,0},{1,9},{9,1},{2,10},{10,2},{3,11},{11,3},{4,12},{12,4},... | collective-permute-start | bytes 1572872 | tf_op jit(solution)/shard_map/ppermute | solution.py:229
  131.6 2.5 %copy-start.9 = (bf16[512,4096]{1,0:T(8,128)(2,1)S(1)}, bf16[512,4096]{1,0:T(8,128)(2,1)}, u32[]{:S(2)}) copy-start(bf16[512,4096]{1,0:T(8,128)(2,1)} %param.8) | copy-start | bytes 12582916
  131.6 14.3 %collective-permute-start.6 = (bf16[1024,256]{1,0:T(8,128)(2,1)S(1)}, bf16[1024,256]{1,0:T(8,128)(2,1)S(1)}, u32[]{:S(2)}, u32[]{:S(2)}) collective-permute-start(bf16[1024,256]{1,0:T(8,128)(2,1)S(1)} %get-tuple-element.14), channel_id=1, source_target_pairs={{0,8},{8,0},{1,9},{9,1},{2,10},{10,2},{3,11},{11,3},{4,12},{12,4},... | collective-permute-start | bytes 1572872 | tf_op jit(solution)/shard_map/ppermute | solution.py:229
  133.4 2.3 %collective-permute-start.8 = (f32[256,128]{1,0:T(8,128)S(1)}, f32[256,128]{1,0:T(8,128)S(1)}, u32[]{:S(2)}, u32[]{:S(2)}) collective-permute-start(f32[256,128]{1,0:T(8,128)S(1)} %get-tuple-element.16), channel_id=1, source_target_pairs={{0,8},{8,0},{1,9},{9,1},{2,10},{10,2},{3,11},{11,3},{4,12},{12,4},... | collective-permute-start | bytes 393224 | tf_op jit(solution)/shard_map/ppermute | solution.py:229
  145.8 1.3 collective-permute-start.4
  (1 other events, 0.8 us)
Sparse Core Ops, SparseCore 0:
  135.8 40.1 reduce-scatter.1

commit v2 on v0

v2 whole, which is shorter than its diff:
```python
import math

import jax
import jax.numpy as jnp
from jax import lax
from jax.experimental import pallas as pl
from jax.experimental.pallas import tpu as pltpu
from jax.sharding import Mesh
from jax.sharding import PartitionSpec as P

HDIM = 128
SCALE = HDIM ** (-0.5)
LOG2E = math.log2(math.e)
EXP2_SCALE = SCALE * LOG2E
CHIPS = ("y", "zh")
CTX = ("y", "zh", "core")
TP = ("x", "zl")
N_CHIPS = 16
HEADS_HERE = 2
WIDE = HEADS_HERE * HDIM
NUM, STAT, COT = 64, 48, 32
ROWS1 = NUM + STAT
ROWS2 = NUM + NUM + COT
LATENTS = N_CHIPS * NUM
F32 = jnp.float32
BF16 = jnp.bfloat16


def dot(a, b, ca, cb):
    return lax.dot_general(a, b, (((ca,), (cb,)), ((), ())), preferred_element_type=F32)


def in_three(x):
    high = x.astype(BF16)
    rest = x - high.astype(F32)
    middle = rest.astype(BF16)
    low = (rest - middle.astype(F32)).astype(BF16)
    return high, middle, low


def params(mib):
    return pltpu.CompilerParams(vmem_limit_bytes=mib * 1024 * 1024)


def whole(*shape):
    return pl.BlockSpec(shape, lambda *_: (0,) * len(shape))


def head_cols(h):
    return slice(h * HDIM, (h + 1) * HDIM)


def dout_kernel(place_ref, own_ref, other_ref, w_ref, out_ref, cot_ref):
    core = place_ref[0]
    for row, ref in ((core, own_ref), (1 - core, other_ref)):
        start = pl.multiple_of(row * COT, COT)
        for b in range(8):
            cot_ref[pl.ds(start, COT), b * 512 : (b + 1) * 512] = ref[b]
    dout = jnp.transpose(dot(w_ref[...], cot_ref[...], 1, 1)).astype(BF16)
    for c in range(N_CHIPS):
        out_ref[c] = dout


def dout_rows(place, cot, cot_in, out_weight):
    depth = out_weight.shape[1]
    grid_spec = pltpu.PrefetchScalarGridSpec(
        num_scalar_prefetch=1,
        grid=(1,),
        in_specs=[
            whole(8, COT, 512),
            whole(8, COT, 512),
            pl.BlockSpec((WIDE, depth), lambda i, c: (c[0], 0)),
        ],
        out_specs=whole(N_CHIPS, NUM, WIDE),
        scratch_shapes=[pltpu.VMEM((NUM, depth), BF16)],
    )
    return pl.pallas_call(
        dout_kernel,
        out_shape=jax.ShapeDtypeStruct((N_CHIPS, NUM, WIDE), BF16),
        grid_spec=grid_spec,
        compiler_params=params(60),
        name="dout",
    )(place, cot, cot_in, out_weight)


def forward_kernel(place_ref, q_ref, ko_ref, kr_ref, vo_ref, vr_ref, part_ref, lse_ref):
    heads = range(HEADS_HERE)
    scores = [
        [dot(k[:, head_cols(h)], q_ref[:, head_cols(h)], 1, 1) for k in (ko_ref, kr_ref)]
        for h in heads
    ]
    expos = []
    for h in heads:
        top = jnp.maximum(
            jnp.max(scores[h][0], axis=0, keepdims=True),
            jnp.max(scores[h][1], axis=0, keepdims=True),
        )
        shift = top * EXP2_SCALE
        expo = [jnp.exp2(s * EXP2_SCALE - shift) for s in scores[h]]
        den = jnp.sum(expo[0], axis=0, keepdims=True) + jnp.sum(expo[1], axis=0, keepdims=True)
        expos.append(([e.astype(BF16) for e in expo], den))
        lse_ref[h : h + 1, :] = top * SCALE + jnp.log(den)
    for h in heads:
        (own, other), den = expos[h]
        num = dot(vo_ref[:, head_cols(h)], own, 0, 0) + dot(vr_ref[:, head_cols(h)], other, 0, 0)
        part_ref[:, head_cols(h)] = jnp.transpose(num / den).astype(BF16)


def forward(place, queries, keys, keys_in, values, values_in):
    tokens = keys.shape[0]
    block = 512
    own = pl.BlockSpec((tokens, WIDE), lambda i, c: (0, c[0]))
    grid_spec = pltpu.PrefetchScalarGridSpec(
        num_scalar_prefetch=1,
        grid=(LATENTS // block,),
        in_specs=[
            pl.BlockSpec((block, WIDE), lambda i, c: (i, c[0])),
            own, own, own, own,
        ],
        out_specs=[
            pl.BlockSpec((block, WIDE), lambda i, c: (i, 0)),
            pl.BlockSpec((8, block), lambda i, c: (0, i)),
        ],
    )
    return pl.pallas_call(
        forward_kernel,
        out_shape=[
            jax.ShapeDtypeStruct((LATENTS, WIDE), BF16),
            jax.ShapeDtypeStruct((8, LATENTS), F32),
        ],
        grid_spec=grid_spec,
        compiler_params=params(60),
        cost_estimate=pl.CostEstimate(
            flops=9_000_000_000, bytes_accessed=4_000_000, transcendentals=4_194_304
        ),
        name="forward",
    )(place, queries, keys, keys_in, values, values_in)


def message_kernel(part_ref, lse_ref, dout_ref, msg_ref, stat_ref):
    rows = []
    deltas = []
    stat_ref[...] = jnp.zeros_like(stat_ref)
    for h in range(HEADS_HERE):
        cols = head_cols(h)
        dout = dout_ref[:, :, cols].reshape(LATENTS, HDIM).astype(F32)
        delta = jnp.sum(part_ref[:, cols].astype(F32) * dout, axis=1, keepdims=True)
        deltas.append(jnp.transpose(jnp.broadcast_to(delta, (LATENTS, HDIM)))[0:1, :])
        stat_ref[h : h + 1, :] = lse_ref[h : h + 1, :] * LOG2E
        stat_ref[2 + h : 3 + h, :] = deltas[h]
    for h in range(HEADS_HERE):
        rows.extend(in_three(lse_ref[h : h + 1, :]))
    for h in range(HEADS_HERE):
        rows.extend(in_three(deltas[h]))
    stats = jnp.concatenate(rows, axis=0)
    stats = jnp.concatenate([stats[:, i * WIDE : (i + 1) * WIDE] for i in range(4)], axis=0)
    for c in range(N_CHIPS):
        msg_ref[c, 0:NUM, :] = part_ref[c * NUM : (c + 1) * NUM, :]
        msg_ref[c, NUM:, :] = stats


def message(part, lse, dout):
    return pl.pallas_call(
        message_kernel,
        out_shape=[
            jax.ShapeDtypeStruct((N_CHIPS, ROWS1, WIDE), BF16),
            jax.ShapeDtypeStruct((8, LATENTS), F32),
        ],
        grid=(1,),
        in_specs=[whole(LATENTS, WIDE), whole(8, LATENTS), whole(N_CHIPS, NUM, WIDE)],
        out_specs=[whole(N_CHIPS, ROWS1, WIDE), whole(8, LATENTS)],
        compiler_params=params(60),
        name="message",
    )(part, lse, dout)


def combine_kernel(
    place_ref, msg_ref, cot_ref, own_ref, a_ref, b_ref, att_ref, stat_ref, out_ref
):
    y = place_ref[1]
    zh = place_ref[2]
    mine = [jnp.zeros((N_CHIPS, WIDE), F32) for _ in range(HEADS_HERE)]
    stat_ref[...] = jnp.zeros_like(stat_ref)
    for i in range(4):
        blocks = [msg_ref[c, NUM:, :].astype(F32) for c in range(N_CHIPS)]
        cols = slice(i * WIDE, (i + 1) * WIDE)

        def value(r):
            at = 12 * i + 3 * r
            return jnp.concatenate(
                [b[at : at + 1] + b[at + 1 : at + 2] + b[at + 2 : at + 3] for b in blocks], axis=0
            )

        for h in range(HEADS_HERE):
            lse = value(h)
            delta = value(2 + h)
            top = jnp.max(lse, axis=0, keepdims=True)
            total = top + jnp.log(jnp.sum(jnp.exp(lse - top), axis=0, keepdims=True))
            weight = jnp.exp(lse - total)
            stat_ref[h : h + 1, cols] = total * LOG2E
            stat_ref[2 + h : 3 + h, cols] = jnp.sum(weight * delta, axis=0, keepdims=True)
            mine[h] = jnp.where(y == i, weight, mine[h])
    att_all = []
    for h in range(HEADS_HERE):
        rows = jnp.zeros((N_CHIPS, NUM), F32)
        for z in range(4):
            rows = jnp.where(zh == z, mine[h][:, z * NUM : (z + 1) * NUM], rows)
        weight = jnp.transpose(rows)
        att = jnp.zeros((NUM, HDIM), F32)
        for c in range(N_CHIPS):
            att = att + msg_ref[c, 0:NUM, head_cols(h)].astype(F32) * weight[:, c : c + 1]
        att_all.append(att.astype(BF16))
    att = jnp.concatenate(att_all, axis=1)
    att_ref[...] = att
    for c in range(N_CHIPS):
        out_ref[c, NUM : 2 * NUM, :] = att
        out_ref[c, 2 * NUM :, :] = cot_ref[c // 2, :, c % 2 * WIDE : (c % 2 + 1) * WIDE]
    for h in range(HEADS_HERE):
        cols = head_cols(h)
        share = jnp.exp2(own_ref[h : h + 1, :] - stat_ref[h : h + 1, :]) * SCALE
        rest = stat_ref[2 + h : 3 + h, :] - own_ref[2 + h : 3 + h, :]
        dq = jnp.transpose(share * (a_ref[cols, :] - rest * b_ref[cols, :])).astype(BF16)
        out_ref[:, 0:NUM, cols] = dq.reshape(N_CHIPS, NUM, HDIM)


def combine(place, msg, cot, own_stats, a, b):
    grid_spec = pltpu.PrefetchScalarGridSpec(
        num_scalar_prefetch=1,
        grid=(1,),
        in_specs=[
            whole(N_CHIPS, ROWS1, WIDE), whole(8, COT, 512), whole(8, LATENTS),
            whole(WIDE, LATENTS), whole(WIDE, LATENTS),
        ],
        out_specs=[whole(NUM, WIDE), whole(8, LATENTS), whole(N_CHIPS, ROWS2, WIDE)],
    )
    return pl.pallas_call(
        combine_kernel,
        out_shape=[
            jax.ShapeDtypeStruct((NUM, WIDE), BF16),
            jax.ShapeDtypeStruct((8, LATENTS), F32),
            jax.ShapeDtypeStruct((N_CHIPS, ROWS2, WIDE), BF16),
        ],
        grid_spec=grid_spec,
        compiler_params=params(24),
        name="combine",
    )(place, msg, cot, own_stats, a, b)


def query_kernel(
    place_ref, q_ref, dout_ref, stat_ref, ko_ref, kr_ref, vo_ref, vr_ref,
    a_ref, b_ref, prob_ref, score_ref,
):
    h = pl.program_id(0)
    block = 256
    for src, (k_ref, v_ref) in enumerate(((ko_ref, vo_ref), (kr_ref, vr_ref))):
        k = k_ref[...]
        v = v_ref[...]
        for at in range(0, LATENTS, block):
            rows = slice(at, at + block)
            q = q_ref[rows, :]
            dout = dout_ref[at // NUM : (at + block) // NUM].reshape(block, HDIM)
            lse = stat_ref[pl.ds(h, 1), rows]
            delta = stat_ref[pl.ds(2 + h, 1), rows]
            probs = jnp.exp2(dot(k, q, 1, 1) * EXP2_SCALE - lse)
            dscore = (probs * (dot(v, dout, 1, 1) - delta)).astype(BF16)
            probs = probs.astype(BF16)
            prob_ref[0, src, :, rows] = probs
            score_ref[0, src, :, rows] = dscore
            a = dot(k, dscore, 0, 0)
            b = dot(k, probs, 0, 0)
            if src == 0:
                a_ref[:, rows] = a
                b_ref[:, rows] = b
            else:
                a_ref[:, rows] += a
                b_ref[:, rows] += b


def query_parts(place, queries, dout, stats, keys, keys_in, values, values_in):
    tokens = keys.shape[0]
    head = pl.BlockSpec((tokens, HDIM), lambda h, c: (0, c[0] * HEADS_HERE + h))
    sums = pl.BlockSpec((HDIM, LATENTS), lambda h, c: (h, 0))
    kept = pl.BlockSpec((1, 2, tokens, LATENTS), lambda h, c: (h, 0, 0, 0))
    grid_spec = pltpu.PrefetchScalarGridSpec(
        num_scalar_prefetch=1,
        grid=(HEADS_HERE,),
        in_specs=[
            pl.BlockSpec((LATENTS, HDIM), lambda h, c: (0, c[0] * HEADS_HERE + h)),
            pl.BlockSpec((N_CHIPS, NUM, HDIM), lambda h, c: (0, 0, h)),
            whole(8, LATENTS),
            head, head, head, head,
        ],
        out_specs=[sums, sums, kept, kept],
    )
    return pl.pallas_call(
        query_kernel,
        out_shape=[
            jax.ShapeDtypeStruct((WIDE, LATENTS), F32),
            jax.ShapeDtypeStruct((WIDE, LATENTS), F32),
            jax.ShapeDtypeStruct((HEADS_HERE, 2, tokens, LATENTS), BF16),
            jax.ShapeDtypeStruct((HEADS_HERE, 2, tokens, LATENTS), BF16),
        ],
        grid_spec=grid_spec,
        compiler_params=params(60),
        cost_estimate=pl.CostEstimate(
            flops=12_000_000_000, bytes_accessed=20_000_000, transcendentals=4_194_304
        ),
        name="query",
    )(place, queries, dout, stats, keys, keys_in, values, values_in)


def token_kernel(
    place_ref, q_ref, dout_ref, own_ref, stat_ref, prob_ref, score_ref,
    dko_ref, dkr_ref, dvo_ref, dvr_ref, both_ref, q_scaled_ref,
):
    h = pl.program_id(0)

    @pl.when(pl.program_id(1) == 0)
    def _():
        share = jnp.exp2(own_ref[pl.ds(h, 1), :] - stat_ref[pl.ds(h, 1), :])
        rest = share * (own_ref[pl.ds(2 + h, 1), :] - stat_ref[pl.ds(2 + h, 1), :])
        share = jnp.transpose(jnp.broadcast_to(share, (HDIM, LATENTS)))
        rest = jnp.transpose(jnp.broadcast_to(rest, (HDIM, LATENTS)))
        q = q_ref[...].astype(F32)
        dout = dout_ref[...].reshape(LATENTS, HDIM).astype(F32)
        both_ref[:, :HDIM] = (share * dout).astype(BF16)
        both_ref[:, HDIM:] = (rest * q).astype(BF16)
        q_scaled_ref[...] = (share * q).astype(BF16)

    block = dko_ref.shape[0]
    both = dot(prob_ref[0].reshape(2 * block, LATENTS), both_ref[...], 1, 0)
    dk = dot(score_ref[0].reshape(2 * block, LATENTS), q_scaled_ref[...], 1, 0)
    dk = ((dk + both[:, HDIM:]) * SCALE).astype(BF16)
    dv = both[:, :HDIM].astype(BF16)
    dko_ref[...] = dk[:block]
    dkr_ref[...] = dk[block:]
    dvo_ref[...] = dv[:block]
    dvr_ref[...] = dv[block:]


def token_grads(place, queries, dout, own_stats, stats, probs, dscores):
    tokens = probs.shape[2]
    block = 512
    own = pl.BlockSpec((block, HDIM), lambda h, i, c: (i, c[0] * HEADS_HERE + h))
    other = pl.BlockSpec((block, HDIM), lambda h, i, c: (i, h))
    kept = pl.BlockSpec((1, 2, block, LATENTS), lambda h, i, c: (h, 0, i, 0))
    grid_spec = pltpu.PrefetchScalarGridSpec(
        num_scalar_prefetch=1,
        grid=(HEADS_HERE, tokens // block),
        in_specs=[
            pl.BlockSpec((LATENTS, HDIM), lambda h, i, c: (0, c[0] * HEADS_HERE + h)),
            pl.BlockSpec((N_CHIPS, NUM, HDIM), lambda h, i, c: (0, 0, h)),
            whole(8, LATENTS),
            whole(8, LATENTS),
            kept, kept,
        ],
        out_specs=[own, other, own, other],
        scratch_shapes=[pltpu.VMEM((LATENTS, WIDE), BF16), pltpu.VMEM((LATENTS, HDIM), BF16)],
    )
    full = jax.ShapeDtypeStruct((tokens, 2 * WIDE), BF16)
    half_wide = jax.ShapeDtypeStruct((tokens, WIDE), BF16)
    return pl.pallas_call(
        token_kernel,
        out_shape=[full, half_wide, full, half_wide],
        grid_spec=grid_spec,
        compiler_params=params(60),
        cost_estimate=pl.CostEstimate(
            flops=6_000_000_000, bytes_accessed=22_000_000, transcendentals=0
        ),
        name="token",
    )(place, queries, dout, own_stats, stats, probs, dscores)


def weight_kernel(place_ref, att_ref, own_ref, other_ref, out_ref, cot_ref):
    core = place_ref[0]
    cot_ref[:, pl.ds(pl.multiple_of(core * COT, COT), COT), :] = own_ref[...]
    cot_ref[:, pl.ds(pl.multiple_of((1 - core) * COT, COT), COT), :] = other_ref[...]
    att = att_ref[...].reshape(LATENTS, WIDE)
    cot = cot_ref[...].reshape(LATENTS, WIDE)
    out_ref[...] = dot(att, cot, 0, 0)


def weight(place, msg, cot_in):
    grid_spec = pltpu.PrefetchScalarGridSpec(
        num_scalar_prefetch=1,
        grid=(1,),
        in_specs=[
            pl.BlockSpec((N_CHIPS, NUM, WIDE), lambda i, c: (0, 1, 0)),
            pl.BlockSpec((N_CHIPS, COT, WIDE), lambda i, c: (0, 2 * NUM // COT, 0)),
            whole(N_CHIPS, COT, WIDE),
        ],
        out_specs=whole(WIDE, WIDE),
        scratch_shapes=[pltpu.VMEM((N_CHIPS, NUM, WIDE), BF16)],
    )
    return pl.pallas_call(
        weight_kernel,
        out_shape=jax.ShapeDtypeStruct((WIDE, WIDE), F32),
        grid_spec=grid_spec,
        compiler_params=params(24),
        name="weight",
    )(place, msg, msg, cot_in)


def swap(x):
    return lax.ppermute(x, "core", [(0, 1), (1, 0)])


def half(x, index, axis):
    size = x.shape[axis] // 2
    return lax.dynamic_slice_in_dim(x, index * size, size, axis)


def in_order(core, mine, other, axis):
    return jnp.where(
        core == 0,
        jnp.concatenate([mine, other], axis),
        jnp.concatenate([other, mine], axis),
    )


def gather(x, axes, size):
    tiled = jnp.broadcast_to(x[None], (size,) + x.shape)
    return lax.all_to_all(tiled, axes, 0, 0, tiled=True)


def shift(x, axis, d):
    return lax.ppermute(x, axis, [(i, (i + d) % 4) for i in range(4)])


def after(x, *others):
    return lax.optimization_barrier((x,) + others)[0]


def body(queries, prefix_keys, prefix_values, out_weight, out_grad):
    core = lax.axis_index("core")
    at_x, at_zl = lax.axis_index("x"), lax.axis_index("zl")
    place = jnp.stack([core, lax.axis_index("y"), lax.axis_index("zh")]).astype(jnp.int32)
    cot = gather(out_grad, TP, 8)
    keys_in = swap(prefix_keys)
    values_in = swap(prefix_values)
    cot, keys_in, values_in = lax.optimization_barrier((cot, keys_in, values_in))
    tokens = (prefix_keys, keys_in, prefix_values, values_in)

    dout = dout_rows(place, cot, swap(cot), out_weight)
    dout = lax.all_to_all(dout, CHIPS, 0, 0, tiled=True)
    part, lse = forward(place, queries, *tokens)
    msg1, own_stats = message(part, lse, dout)
    msg1 = lax.all_to_all(msg1, CHIPS, 0, 0, tiled=True)
    a, b, probs, dscores = query_parts(place, queries, dout, own_stats, *tokens)

    att64, stats, msg2 = combine(place, msg1, cot, own_stats, a, b)
    msg2 = lax.all_to_all(msg2, CHIPS, 0, 0, tiled=True)

    att32 = in_order(core, half(att64, core, 0), swap(half(att64, 1 - core, 0)), 1)
    partial_out = dot(att32, out_weight, 1, 0).reshape(32, 4, 1024).transpose(1, 0, 2)
    by_x = [
        lax.dynamic_index_in_dim(partial_out, lax.rem(at_x + d, 4), 0, keepdims=False)
        for d in range(4)
    ]
    from_x = [shift(by_x[d].astype(BF16), "x", d) for d in (1, 2, 3)]
    dk, dk_out, dv, dv_out = token_grads(
        place, queries, dout, own_stats, after(stats, by_x[0]), probs, dscores
    )
    own_x, *from_x = lax.optimization_barrier((by_x[0], *from_x, dk))[:4]
    over_x = own_x + sum(x.astype(F32) for x in from_x)
    by_zl = over_x.reshape(32, 2, 512).transpose(1, 0, 2)
    from_zl = lax.ppermute(
        lax.dynamic_index_in_dim(by_zl, 1 - at_zl, 0, keepdims=False).astype(BF16),
        "zl",
        [(0, 1), (1, 0)],
    )
    own_zl = lax.dynamic_index_in_dim(by_zl, at_zl, 0, keepdims=False)
    other_cols = (jnp.int32(0), ((1 - core) * WIDE).astype(jnp.int32))
    key_grad = lax.dynamic_update_slice(dk, swap(dk_out), other_cols)
    value_grad = lax.dynamic_update_slice(dv, swap(dv_out), other_cols)
    from_zl = after(from_zl, key_grad, value_grad)
    latent_out = (own_zl + from_zl.astype(F32)).astype(BF16)

    msg2 = after(msg2, latent_out)
    cot_in = swap(msg2[:, 2 * NUM :])
    dq64 = jnp.sum(msg2[:, :NUM].astype(F32), axis=0).astype(BF16)
    dq_in = swap(half(dq64, 1 - core, 0))
    query_grad = in_order(core, half(dq64, core, 0), dq_in, 1)
    weight_part = weight(place, msg2, cot_in)
    weight_in = swap(half(weight_part, 1 - core, 1))
    weight_grad = in_order(core, half(weight_part, core, 1), weight_in, 0)
    return latent_out, query_grad, key_grad, value_grad, weight_grad


def solution(mesh):
    fine = Mesh(mesh.devices.reshape(4, 4, 2, 4, 2), ("y", "zh", "core", "x", "zl"))
    placed = (P(None, TP), P(CTX, TP), P(CTX, TP), P(TP, None), P(CTX, TP))
    return jax.shard_map(
        body,
        mesh=fine,
        in_specs=placed,
        out_specs=(P(CTX, TP), P(CTX, TP), P(CTX, TP), P(CTX, TP), P(TP, CTX)),
        check_vma=False,
    )
```

time: 746 us -> 135 us (0.18)
  waiting for transfers between devices: 328 us -> 31.6 us
  blocking collectives: 304 us -> 10.1 us
  matrix products: 58.6 us -> 3 us
  Pallas kernels: 0 us -> 44.2 us
  starting transfers between devices: 0.43 us -> 33.9 us
  local copies, waits for them, and re-layouts: 22.4 us -> 8.33 us
  between operations: 13.9 us -> 0.88 us
  other arithmetic: 14.2 us -> 2.69 us
    pmax x1 -> x0, blocking collectives: 141 us -> none  [body(): row_top = lax.pmax(jnp.max(scores, axis=2), 'ctx')]
    psum x1 -> x0, waiting for transfers between devices: 139 us -> none  [body(): numer, denom = lax.psum((partial_num, partial_den), 'ctx')]
    psum x1 -> x0, blocking collectives: 139 us -> none  [body(): numer, denom = lax.psum((partial_num, partial_den), 'ctx')]
    unnamed x6 -> x0, waiting for transfers between devices: 101 us -> none
    reduce_scatter x2 -> x0, waiting for transfers between devices: 87.9 us -> none  [the longest x1 52.9 us: body(): lax.psum_scatter(partial_query.reshape(latents, heads_here * HDIM), 'ctx'...]
    dot_general x9 -> x1, matrix products: 58.6 us -> 3 us  [dot(): lax.dot_general(a, b, (((ca,), (cb,)), ((), ())), preferred_element_type=...]
    pallas_call x0 -> x7, Pallas kernels: none -> 44.2 us  [the longest x1 13.4 us: query_parts(): pl.pallas_call(query_kernel, out_shape=[jax.ShapeDtypeStruct((WIDE, LATEN...]
    all_to_all x0 -> x3, waiting for transfers between devices: none -> 25.2 us  [the longest x1 10.8 us: body(): msg1 = lax.all_to_all(msg1, CHIPS, 0, 0, tiled=True)]
  transfers between devices with their start and end apart: 5 -> 16, of which waited for: 4 -> 9; matrix products, arithmetic and copies ran while one was open for 10% -> 6% of each run, Pallas kernels for 0% -> 25%
where the time goes in v2:
time: 135 us
  Pallas kernels  44.2 us (33%)
  starting transfers between devices  33.9 us (25%)
  waiting for transfers between devices  31.6 us (23%)
  blocking collectives  10.1 us (7%)
  local copies, waits for them, and re-layouts  8.33 us (6%)
  matrix products  3 us (2%)
  other arithmetic  2.69 us (2%)
    pallas_call x1, Pallas kernels, query_parts(): pl.pallas_call(query_kernel, out_shape=[jax.ShapeDtypeStruct((WIDE, LATEN...  13.4 us
    pallas_call x1, Pallas kernels, token_grads(): pl.pallas_call(token_kernel, out_shape=[full, half_wide, full, half_wide]...  11.1 us
    all_to_all x1, waiting for transfers between devices, body(): msg1 = lax.all_to_all(msg1, CHIPS, 0, 0, tiled=True)  10.8 us
    ppermute x9, starting transfers between devices, swap(): return lax.ppermute(x, 'core', [(0, 1), (1, 0)])  10.3 us
    all_to_all x1, blocking collectives, gather(): return lax.all_to_all(tiled, axes, 0, 0, tiled=True)  10.1 us
    all_to_all x1, starting transfers between devices, body(): dout = lax.all_to_all(dout, CHIPS, 0, 0, tiled=True)  10 us
    pallas_call x1, Pallas kernels, forward(): pl.pallas_call(forward_kernel, out_shape=[jax.ShapeDtypeStruct((LATENTS,...  9.08 us
    all_to_all x1, waiting for transfers between devices, body(): dout = lax.all_to_all(dout, CHIPS, 0, 0, tiled=True)  8.45 us
  transfers between devices with their start and end apart: 16, of which 9 were waited for; matrix products, arithmetic and copies ran while one was open for 6% of the time, Pallas kernels for 25%

profile of v2, /device:TPU:1, one launch (start us, length us, event | category | flops | bytes accessed | tf_op | source)
XLA Modules:
  0.0 134.6 jit_solution(15635254382674767019)
XLA Ops:
  0.6 3.3 %collective-permute-start = (bf16[1024,512]{1,0:T(8,128)(2,1)}, bf16[1024,512]{1,0:T(8,128)(2,1)S(1)}, u32[]{:S(2)}, u32[]{:S(2)}) collective-permute-start(bf16[1024,512]{1,0:T(8,128)(2,1)} %ko_ref.3), channel_id=1, source_target_pairs={{0,8},{8,0},{1,9},{9,1},{2,10},{10,2},{3,11},{11,3},{4,12},{12,4},... | collective-permute-start | bytes 3145736 | tf_op jit(solution)/shard_map/ppermute | solution.py:405
  4.8 10.1 %all_to_all.20.own_ref.cot_ref = bf16[8,32,512]{2,1,0:T(8,128)(2,1)S(1)} all-to-all(bf16[8,32,512]{2,1,0:T(8,128)(2,1)S(1)} %broadcast_in_dim.2), channel_id=1, replica_groups=mesh['y'=4,'zh'=4,'core'=2,'x'=4,'zl'=2] {'x','zl'}, dimensions={0} | all-to-all | bytes 524288 | tf_op jit(solution)/shard_map/all_to_all | solution.py:423
  15.0 1.6 %collective-permute-start.2 = (bf16[8,32,512]{2,1,0:T(8,128)(2,1)S(1)}, bf16[8,32,512]{2,1,0:T(8,128)(2,1)S(1)}, u32[]{:S(2)}, u32[]{:S(2)}) collective-permute-start(bf16[8,32,512]{2,1,0:T(8,128)(2,1)S(1)} %all_to_all.20.own_ref.cot_ref), channel_id=1, source_target_pairs={{0,8},{8,0},{1,9},{9,1},{2,10},{10,2},{3,11},{11,3},{4,12},{12,4},... | collective-permute-start | bytes 786440 | tf_op jit(solution)/shard_map/ppermute | solution.py:405
  18.5 4.1 %dout.1 = bf16[16,64,256]{2,1,0:T(8,128)(2,1)} custom-call(s32[3]{0:T(128)} %pad_add_fusion.place_ref, bf16[8,32,512]{2,1,0:T(8,128)(2,1)} %copy-done, bf16[8,32,512]{2,1,0:T(8,128)(2,1)} %copy-done.9, bf16[512,4096]{1,0:T(8,128)(2,1)} %w_ref.1), custom_call_target="tpu_custom_call" | custom-call | tf_op jit(solution)/shard_map/dout/pallas_call | solution.py:77
  22.5 10.0 %all-to-all-start.1 = ((bf16[16,64,256]{2,1,0:T(8,128)(2,1)}), bf16[16,64,256]{2,1,0:T(8,128)(2,1)S(1)}, u32[]{:S(2)}, u32[]{:S(2)}) async-start(bf16[16,64,256]{2,1,0:T(8,128)(2,1)} %dout.1), calls=%async_computation.1 | async-start | bytes 1048576 | tf_op jit(solution)/shard_map/all_to_all | solution.py:445
  32.6 9.1 %forward.1 = (bf16[1024,256]{1,0:T(8,128)(2,1)}, f32[8,1024]{1,0:T(8,128)}) custom-call(s32[3]{0:T(128)} %pad_add_fusion.place_ref, bf16[1024,512]{1,0:T(8,128)(2,1)} %q_ref.5, bf16[1024,512]{1,0:T(8,128)(2,1)} %ko_ref.3, bf16[1024,512]{1,0:T(8,128)(2,1)} %copy-done.10, bf16[1024,512]{1,0:T(8,128)(2,1)} %vo_ref.3, bf16[1024,512]{1,0:T(8,128)(2,1)} %copy-done.11), custom_call_target="tpu_custom_call" | custom-call | flops 8999999488 | bytes 4000000 | tf_op jit(solution)/shard_map/forward/pallas_call | solution.py:125
  41.7 8.4 %all-to-all-done.1.dout_ref = bf16[16,64,256]{2,1,0:T(8,128)(2,1)S(1)} async-done(((bf16[16,64,256]{2,1,0:T(8,128)(2,1)}), bf16[16,64,256]{2,1,0:T(8,128)(2,1)S(1)}, u32[]{:S(2)}, u32[]{:S(2)}) %all-to-all-start.1) | async-done | bytes 524320 | tf_op jit(solution)/shard_map/all_to_all | solution.py:445
  50.9 2.8 %message.1 = (bf16[16,112,256]{2,1,0:T(8,128)(2,1)}, f32[8,1024]{1,0:T(8,128)}) custom-call(bf16[1024,256]{1,0:T(8,128)(2,1)} %get-tuple-element.32.part_ref, f32[8,1024]{1,0:T(8,128)} %get-tuple-element.33.lse_ref, bf16[16,64,256]{2,1,0:T(8,128)(2,1)} %copy-done.8), custom_call_target="tpu_custom_call" | custom-call | tf_op jit(solution)/shard_map/message/pallas_call | solution.py:163
  53.7 3.9 %all-to-all-start.2 = ((bf16[16,112,256]{2,1,0:T(8,128)(2,1)}), bf16[16,112,256]{2,1,0:T(8,128)(2,1)S(1)}, u32[]{:S(2)}, u32[]{:S(2)}) async-start(bf16[16,112,256]{2,1,0:T(8,128)(2,1)} %get-tuple-element.35), calls=%async_computation.2 | async-start | bytes 1835008 | tf_op jit(solution)/shard_map/all_to_all | solution.py:448
  57.7 13.4 %query.1 = (f32[256,1024]{1,0:T(8,128)}, f32[256,1024]{1,0:T(8,128)}, bf16[2,2,1024,1024]{3,2,1,0:T(8,128)(2,1)}, bf16[2,2,1024,1024]{3,2,1,0:T(8,128)(2,1)}) custom-call(s32[3]{0:T(128)} %pad_add_fusion.place_ref, bf16[1024,512]{1,0:T(8,128)(2,1)} %q_ref.5, bf16[16,64,256]{2,1,0:T(8,128)(2,1)} %copy-done.8, f32[8,1024]{1,0:T(8,128)} %get-tuple-element.36.stat_ref.own_ref, ...), custom_call_target="tpu_custom_call" | custom-call | flops 12000000000 | bytes 20000000 | tf_op jit(solution)/shard_map/query/pallas_call | solution.py:295
  71.1 10.8 %all-to-all-done.2.msg_ref = bf16[16,112,256]{2,1,0:T(8,128)(2,1)S(1)} async-done(((bf16[16,112,256]{2,1,0:T(8,128)(2,1)}), bf16[16,112,256]{2,1,0:T(8,128)(2,1)S(1)}, u32[]{:S(2)}, u32[]{:S(2)}) %all-to-all-start.2) | async-done | bytes 917536 | tf_op jit(solution)/shard_map/all_to_all | solution.py:448
  81.9 1.2 copy-done.2
  83.1 1.2 copy-done.3
  84.3 2.9 %combine.1 = (bf16[64,256]{1,0:T(8,128)(2,1)S(1)}, f32[8,1024]{1,0:T(8,128)S(1)}, bf16[16,160,256]{2,1,0:T(8,128)(2,1)}) custom-call(s32[3]{0:T(128)S(1)} %copy-done.5, bf16[16,112,256]{2,1,0:T(8,128)(2,1)S(1)} %all-to-all-done.2.msg_ref, bf16[8,32,512]{2,1,0:T(8,128)(2,1)S(1)} %copy-done.1, f32[8,1024]{1,0:T(8,128)S(1)} %copy-done.4, ...), custom_call_target="tpu_custom_call" | custom-call | tf_op jit(solution)/shard_map/combine/pallas_call | solution.py:236
  87.8 6.2 %all-to-all-start.3 = ((bf16[16,160,256]{2,1,0:T(8,128)(2,1)}), bf16[16,160,256]{2,1,0:T(8,128)(2,1)S(1)}, u32[]{:S(2)}, u32[]{:S(2)}) async-start(bf16[16,160,256]{2,1,0:T(8,128)(2,1)} %get-tuple-element.53), calls=%async_computation.3 | async-start | bytes 2621440 | tf_op jit(solution)/shard_map/all_to_all | solution.py:452
  94.0 1.5 %collective-permute-start.3 = (bf16[32,256]{1,0:T(8,128)(2,1)S(1)}, bf16[32,256]{1,0:T(8,128)(2,1)S(1)}, u32[]{:S(2)}, u32[]{:S(2)}) collective-permute-start(bf16[32,256]{1,0:T(8,128)(2,1)S(1)} %get-tuple-element.63), channel_id=1, source_target_pairs={{0,8},{8,0},{1,9},{9,1},{2,10},{10,2},{3,11},{11,3},{4,12},{12,4},... | collective-permute-start | bytes 49160 | tf_op jit(solution)/shard_map/ppermute | solution.py:405
  96.3 3.0 %fusion.4 = f32[32,4096]{1,0:T(8,128)S(1)} fusion(bf16[512,4096]{1,0:T(8,128)(2,1)} %w_ref.1, bf16[32,256]{1,0:T(8,128)(2,1)S(1)} %collective-permute-done.3, bf16[32,256]{1,0:T(8,128)(2,1)S(1)} %get-tuple-element.62, pred[]{:T(512)S(6)} %eq.2), kind=kOutput, calls=%fused_computation.14 | convolution fusion | flops 134365184 | bytes 4751361 | tf_op jit(solution)/shard_map/dot_general | solution.py:30
  101.6 2.1 %collective-permute-start.6 = (bf16[32,1024]{1,0:T(8,128)(2,1)S(1)}, bf16[32,1024]{1,0:T(8,128)(2,1)S(1)}, u32[]{:S(2)}, u32[]{:S(2)}) collective-permute-start(bf16[32,1024]{1,0:T(8,128)(2,1)S(1)} %bitcast.26), channel_id=1, source_target_pairs={{0,6},{2,0},{4,2},{6,4},{1,7},{3,1},{5,3},{7,5},{8,14},{10,8},{12,... | collective-permute-start | bytes 196616 | tf_op jit(solution)/shard_map/ppermute | solution.py:427
  103.7 11.1 %token_.1 = (bf16[1024,512]{1,0:T(8,128)(2,1)}, bf16[1024,256]{1,0:T(8,128)(2,1)}, bf16[1024,512]{1,0:T(8,128)(2,1)}, bf16[1024,256]{1,0:T(8,128)(2,1)}) custom-call(s32[3]{0:T(128)} %pad_add_fusion.place_ref, bf16[1024,512]{1,0:T(8,128)(2,1)} %q_ref.5, bf16[16,64,256]{2,1,0:T(8,128)(2,1)} %copy-done.8, f32[8,1024]{1,0:T(8,128)} %get-tuple-element.36.stat_ref.own_ref, ...), custom_call_target="tpu_custom_call" | custom-call | flops 6000000000 | bytes 22000000 | tf_op jit(solution)/shard_map/token/pallas_call | solution.py:362
  116.5 1.2 collective-permute-done.8
  119.3 1.6 %collective-permute-done.7 = bf16[32,512]{1,0:T(8,128)(2,1)S(1)} collective-permute-done((bf16[32,512]{1,0:T(8,128)(2,1)S(1)}, bf16[32,512]{1,0:T(8,128)(2,1)S(1)}, u32[]{:S(2)}, u32[]{:S(2)}) %collective-permute-start.7) | collective-permute-done | bytes 32800 | tf_op jit(solution)/shard_map/ppermute | solution.py:467
  121.6 6.0 %all-to-all-done.3.att_ref.own_ref = bf16[16,160,256]{2,1,0:T(8,128)(2,1)S(1)} async-done(((bf16[16,160,256]{2,1,0:T(8,128)(2,1)}), bf16[16,160,256]{2,1,0:T(8,128)(2,1)S(1)}, u32[]{:S(2)}, u32[]{:S(2)}) %all-to-all-start.3) | async-done | bytes 1310752 | tf_op jit(solution)/shard_map/all_to_all | solution.py:452
  127.5 2.0 %collective-permute-start.11 = (bf16[16,32,256]{2,1,0:T(8,128)(2,1)S(1)}, bf16[16,32,256]{2,1,0:T(8,128)(2,1)S(1)}, u32[]{:S(2)}, u32[]{:S(2)}) collective-permute-start(bf16[16,32,256]{2,1,0:T(8,128)(2,1)S(1)} %slice.7), channel_id=1, source_target_pairs={{0,8},{8,0},{1,9},{9,1},{2,10},{10,2},{3,11},{11,3},{4,12},{12,4},... | collective-permute-start | bytes 786440 | tf_op jit(solution)/shard_map/ppermute | solution.py:405
  129.6 1.1 collective-permute-done.11.other_ref
  (65 shorter events, 15.0 us)
Async XLA Ops:
  0.6 14.3 %collective-permute-start = (bf16[1024,512]{1,0:T(8,128)(2,1)}, bf16[1024,512]{1,0:T(8,128)(2,1)S(1)}, u32[]{:S(2)}, u32[]{:S(2)}) collective-permute-start(bf16[1024,512]{1,0:T(8,128)(2,1)} %ko_ref.3), channel_id=1, source_target_pairs={{0,8},{8,0},{1,9},{9,1},{2,10},{10,2},{3,11},{11,3},{4,12},{12,4},... | collective-permute-start | bytes 3145736 | tf_op jit(solution)/shard_map/ppermute | solution.py:405
  4.0 11.0 %collective-permute-start.1 = (bf16[1024,512]{1,0:T(8,128)(2,1)}, bf16[1024,512]{1,0:T(8,128)(2,1)S(1)}, u32[]{:S(2)}, u32[]{:S(2)}) collective-permute-start(bf16[1024,512]{1,0:T(8,128)(2,1)} %vo_ref.3), channel_id=1, source_target_pairs={{0,8},{8,0},{1,9},{9,1},{2,10},{10,2},{3,11},{11,3},{4,12},{12,4},... | collective-permute-start | bytes 3145736 | tf_op jit(solution)/shard_map/ppermute | solution.py:405
  14.9 2.8 %copy-start = (bf16[8,32,512]{2,1,0:T(8,128)(2,1)}, bf16[8,32,512]{2,1,0:T(8,128)(2,1)S(1)}, u32[]{:S(2)}) copy-start(bf16[8,32,512]{2,1,0:T(8,128)(2,1)S(1)} %all_to_all.20.own_ref.cot_ref) | copy-start | bytes 786436
  14.9 17.6 %copy-start.10 = (bf16[1024,512]{1,0:T(8,128)(2,1)}, bf16[1024,512]{1,0:T(8,128)(2,1)S(1)}, u32[]{:S(2)}) copy-start(bf16[1024,512]{1,0:T(8,128)(2,1)S(1)} %collective-permute-done.kr_ref) | copy-start | bytes 3145732
  15.0 17.6 %copy-start.11 = (bf16[1024,512]{1,0:T(8,128)(2,1)}, bf16[1024,512]{1,0:T(8,128)(2,1)S(1)}, u32[]{:S(2)}) copy-start(bf16[1024,512]{1,0:T(8,128)(2,1)S(1)} %collective-permute-done.1.vr_ref) | copy-start | bytes 3145732
  15.0 2.8 %collective-permute-start.2 = (bf16[8,32,512]{2,1,0:T(8,128)(2,1)S(1)}, bf16[8,32,512]{2,1,0:T(8,128)(2,1)S(1)}, u32[]{:S(2)}, u32[]{:S(2)}) collective-permute-start(bf16[8,32,512]{2,1,0:T(8,128)(2,1)S(1)} %all_to_all.20.own_ref.cot_ref), channel_id=1, source_target_pairs={{0,8},{8,0},{1,9},{9,1},{2,10},{10,2},{3,11},{11,3},{4,12},{12,4},... | collective-permute-start | bytes 786440 | tf_op jit(solution)/shard_map/ppermute | solution.py:405
  22.5 27.6 %all-to-all-start.1 = ((bf16[16,64,256]{2,1,0:T(8,128)(2,1)}), bf16[16,64,256]{2,1,0:T(8,128)(2,1)S(1)}, u32[]{:S(2)}, u32[]{:S(2)}) async-start(bf16[16,64,256]{2,1,0:T(8,128)(2,1)} %dout.1), calls=%async_computation.1 | async-start | bytes 1048576 | tf_op jit(solution)/shard_map/all_to_all | solution.py:445
  53.7 28.1 %all-to-all-start.2 = ((bf16[16,112,256]{2,1,0:T(8,128)(2,1)}), bf16[16,112,256]{2,1,0:T(8,128)(2,1)S(1)}, u32[]{:S(2)}, u32[]{:S(2)}) async-start(bf16[16,112,256]{2,1,0:T(8,128)(2,1)} %get-tuple-element.35), calls=%async_computation.2 | async-start | bytes 1835008 | tf_op jit(solution)/shard_map/all_to_all | solution.py:448
  57.7 24.2 %copy-start.1 = (bf16[8,32,512]{2,1,0:T(8,128)(2,1)S(1)}, bf16[8,32,512]{2,1,0:T(8,128)(2,1)}, u32[]{:S(2)}) copy-start(bf16[8,32,512]{2,1,0:T(8,128)(2,1)} %copy-done) | copy-start | bytes 786436
  57.7 24.2 %copy-start.4 = (f32[8,1024]{1,0:T(8,128)S(1)}, f32[8,1024]{1,0:T(8,128)}, u32[]{:S(2)}) copy-start(f32[8,1024]{1,0:T(8,128)} %get-tuple-element.36.stat_ref.own_ref) | copy-start | bytes 98308
  57.7 24.2 %copy-start.5 = (s32[3]{0:T(128)S(1)}, s32[3]{0:T(128)}, u32[]{:S(2)}) copy-start(s32[3]{0:T(128)} %pad_add_fusion.place_ref) | copy-start | bytes 40
  81.9 1.2 copy-start.2
  87.8 39.7 %all-to-all-start.3 = ((bf16[16,160,256]{2,1,0:T(8,128)(2,1)}), bf16[16,160,256]{2,1,0:T(8,128)(2,1)S(1)}, u32[]{:S(2)}, u32[]{:S(2)}) async-start(bf16[16,160,256]{2,1,0:T(8,128)(2,1)} %get-tuple-element.53), calls=%async_computation.3 | async-start | bytes 2621440 | tf_op jit(solution)/shard_map/all_to_all | solution.py:452
  94.0 2.3 %collective-permute-start.3 = (bf16[32,256]{1,0:T(8,128)(2,1)S(1)}, bf16[32,256]{1,0:T(8,128)(2,1)S(1)}, u32[]{:S(2)}, u32[]{:S(2)}) collective-permute-start(bf16[32,256]{1,0:T(8,128)(2,1)S(1)} %get-tuple-element.63), channel_id=1, source_target_pairs={{0,8},{8,0},{1,9},{9,1},{2,10},{10,2},{3,11},{11,3},{4,12},{12,4},... | collective-permute-start | bytes 49160 | tf_op jit(solution)/shard_map/ppermute | solution.py:405
  100.3 15.7 %collective-permute-start.4 = (bf16[32,1024]{1,0:T(8,128)(2,1)S(1)}, bf16[32,1024]{1,0:T(8,128)(2,1)S(1)}, u32[]{:S(2)}, u32[]{:S(2)}) collective-permute-start(bf16[32,1024]{1,0:T(8,128)(2,1)S(1)} %bitcast.24), channel_id=1, source_target_pairs={{0,2},{2,4},{4,6},{6,0},{1,3},{3,5},{5,7},{7,1},{8,10},{10,12},{12... | collective-permute-start | bytes 196616 | tf_op jit(solution)/shard_map/ppermute | solution.py:427
  101.1 14.9 %collective-permute-start.5 = (bf16[32,1024]{1,0:T(8,128)(2,1)S(1)}, bf16[32,1024]{1,0:T(8,128)(2,1)S(1)}, u32[]{:S(2)}, u32[]{:S(2)}) collective-permute-start(bf16[32,1024]{1,0:T(8,128)(2,1)S(1)} %bitcast.25), channel_id=1, source_target_pairs={{0,4},{2,6},{4,0},{6,2},{1,5},{3,7},{5,1},{7,3},{8,12},{10,14},{12... | collective-permute-start | bytes 196616 | tf_op jit(solution)/shard_map/ppermute | solution.py:427
  101.6 14.4 %collective-permute-start.6 = (bf16[32,1024]{1,0:T(8,128)(2,1)S(1)}, bf16[32,1024]{1,0:T(8,128)(2,1)S(1)}, u32[]{:S(2)}, u32[]{:S(2)}) collective-permute-start(bf16[32,1024]{1,0:T(8,128)(2,1)S(1)} %bitcast.26), channel_id=1, source_target_pairs={{0,6},{2,0},{4,2},{6,4},{1,7},{3,1},{5,3},{7,5},{8,14},{10,8},{12,... | collective-permute-start | bytes 196616 | tf_op jit(solution)/shard_map/ppermute | solution.py:427
  114.9 15.8 %copy-start.6 = (s32[3]{0:T(128)S(1)}, s32[3]{0:T(128)}, u32[]{:S(2)}) copy-start(s32[3]{0:T(128)} %pad_add_fusion.place_ref) | copy-start | bytes 40
  114.9 2.8 %collective-permute-start.8 = (bf16[1024,256]{1,0:T(8,128)(2,1)}, bf16[1024,256]{1,0:T(8,128)(2,1)S(1)}, u32[]{:S(2)}, u32[]{:S(2)}) collective-permute-start(bf16[1024,256]{1,0:T(8,128)(2,1)} %get-tuple-element.49), channel_id=1, source_target_pairs={{0,8},{8,0},{1,9},{9,1},{2,10},{10,2},{3,11},{11,3},{4,12},{12,4},... | collective-permute-start | bytes 1572872 | tf_op jit(solution)/shard_map/ppermute | solution.py:405
  115.9 2.6 %collective-permute-start.9 = (bf16[1024,256]{1,0:T(8,128)(2,1)}, bf16[1024,256]{1,0:T(8,128)(2,1)S(1)}, u32[]{:S(2)}, u32[]{:S(2)}) collective-permute-start(bf16[1024,256]{1,0:T(8,128)(2,1)} %get-tuple-element.51), channel_id=1, source_target_pairs={{0,8},{8,0},{1,9},{9,1},{2,10},{10,2},{3,11},{11,3},{4,12},{12,4},... | collective-permute-start | bytes 1572872 | tf_op jit(solution)/shard_map/ppermute | solution.py:405
  116.3 4.7 %collective-permute-start.7 = (bf16[32,512]{1,0:T(8,128)(2,1)S(1)}, bf16[32,512]{1,0:T(8,128)(2,1)S(1)}, u32[]{:S(2)}, u32[]{:S(2)}) collective-permute-start(bf16[32,512]{1,0:T(8,128)(2,1)S(1)} %bitcast.27), channel_id=1, source_target_pairs={{0,1},{1,0},{2,3},{3,2},{4,5},{5,4},{6,7},{7,6},{8,9},{9,8},{10,11... | collective-permute-start | bytes 98312 | tf_op jit(solution)/shard_map/ppermute | solution.py:467
  127.5 3.1 %collective-permute-start.11 = (bf16[16,32,256]{2,1,0:T(8,128)(2,1)S(1)}, bf16[16,32,256]{2,1,0:T(8,128)(2,1)S(1)}, u32[]{:S(2)}, u32[]{:S(2)}) collective-permute-start(bf16[16,32,256]{2,1,0:T(8,128)(2,1)S(1)} %slice.7), channel_id=1, source_target_pairs={{0,8},{8,0},{1,9},{9,1},{2,10},{10,2},{3,11},{11,3},{4,12},{12,4},... | collective-permute-start | bytes 786440 | tf_op jit(solution)/shard_map/ppermute | solution.py:405
  131.6 2.3 %collective-permute-start.12 = (f32[256,128]{1,0:T(8,128)S(1)}, f32[256,128]{1,0:T(8,128)S(1)}, u32[]{:S(2)}, u32[]{:S(2)}) collective-permute-start(f32[256,128]{1,0:T(8,128)S(1)} %get-tuple-element.59), channel_id=1, source_target_pairs={{0,8},{8,0},{1,9},{9,1},{2,10},{10,2},{3,11},{11,3},{4,12},{12,4},... | collective-permute-start | bytes 393224 | tf_op jit(solution)/shard_map/ppermute | solution.py:405
  132.1 1.2 collective-permute-start.10
  (4 other events, 3.3 us)

commit v3 on v2

--- a/solution.py
+++ b/solution.py
@@ -18,9 +18,10 @@
 N_CHIPS = 16
 HEADS_HERE = 2
 WIDE = HEADS_HERE * HDIM
-NUM, STAT, COT = 64, 48, 32
+NUM, STAT, COT, PART = 64, 48, 32, 16
 ROWS1 = NUM + STAT
-ROWS2 = NUM + NUM + COT
+ROWS2 = NUM + NUM
+ROWS0 = NUM + PART
 LATENTS = N_CHIPS * NUM
 F32 = jnp.float32
 BF16 = jnp.bfloat16
@@ -57,8 +58,10 @@
         for b in range(8):
             cot_ref[pl.ds(start, COT), b * 512 : (b + 1) * 512] = ref[b]
     dout = jnp.transpose(dot(w_ref[...], cot_ref[...], 1, 1)).astype(BF16)
+    start = pl.multiple_of(core * COT + place_ref[3] * PART, PART)
     for c in range(N_CHIPS):
-        out_ref[c] = dout
+        out_ref[c, 0:NUM, :] = dout
+        out_ref[c, NUM:, :] = cot_ref[pl.ds(start, PART), c * WIDE : (c + 1) * WIDE]
 
 
 def dout_rows(place, cot, cot_in, out_weight):
@@ -71,12 +74,12 @@
             whole(8, COT, 512),
             pl.BlockSpec((WIDE, depth), lambda i, c: (c[0], 0)),
         ],
-        out_specs=whole(N_CHIPS, NUM, WIDE),
+        out_specs=whole(N_CHIPS, ROWS0, WIDE),
         scratch_shapes=[pltpu.VMEM((NUM, depth), BF16)],
     )
     return pl.pallas_call(
         dout_kernel,
-        out_shape=jax.ShapeDtypeStruct((N_CHIPS, NUM, WIDE), BF16),
+        out_shape=jax.ShapeDtypeStruct((N_CHIPS, ROWS0, WIDE), BF16),
         grid_spec=grid_spec,
         compiler_params=params(60),
         name="dout",
@@ -175,7 +178,7 @@
 
 
 def combine_kernel(
-    place_ref, msg_ref, cot_ref, own_ref, a_ref, b_ref, att_ref, stat_ref, out_ref
+    place_ref, msg_ref, own_ref, a_ref, b_ref, att_ref, stat_ref, out_ref
 ):
     y = place_ref[1]
     zh = place_ref[2]
@@ -213,22 +216,21 @@
     att = jnp.concatenate(att_all, axis=1)
     att_ref[...] = att
     for c in range(N_CHIPS):
-        out_ref[c, NUM : 2 * NUM, :] = att
-        out_ref[c, 2 * NUM :, :] = cot_ref[c // 2, :, c % 2 * WIDE : (c % 2 + 1) * WIDE]
+        out_ref[c, NUM:, :] = att
     for h in range(HEADS_HERE):
         cols = head_cols(h)
         share = jnp.exp2(own_ref[h : h + 1, :] - stat_ref[h : h + 1, :]) * SCALE
         rest = stat_ref[2 + h : 3 + h, :] - own_ref[2 + h : 3 + h, :]
-        dq = jnp.transpose(share * (a_ref[cols, :] - rest * b_ref[cols, :])).astype(BF16)
+        dq = jnp.transpose(share * (a_ref[cols, :].astype(F32) - rest * b_ref[cols, :].astype(F32))).astype(BF16)
         out_ref[:, 0:NUM, cols] = dq.reshape(N_CHIPS, NUM, HDIM)
 
 
-def combine(place, msg, cot, own_stats, a, b):
+def combine(place, msg, own_stats, a, b):
     grid_spec = pltpu.PrefetchScalarGridSpec(
         num_scalar_prefetch=1,
         grid=(1,),
         in_specs=[
-            whole(N_CHIPS, ROWS1, WIDE), whole(8, COT, 512), whole(8, LATENTS),
+            whole(N_CHIPS, ROWS1, WIDE), whole(8, LATENTS),
             whole(WIDE, LATENTS), whole(WIDE, LATENTS),
         ],
         out_specs=[whole(NUM, WIDE), whole(8, LATENTS), whole(N_CHIPS, ROWS2, WIDE)],
@@ -243,37 +245,33 @@
         grid_spec=grid_spec,
         compiler_params=params(24),
         name="combine",
-    )(place, msg, cot, own_stats, a, b)
+    )(place, msg, own_stats, a, b)
 
 
 def query_kernel(
     place_ref, q_ref, dout_ref, stat_ref, ko_ref, kr_ref, vo_ref, vr_ref,
-    a_ref, b_ref, prob_ref, score_ref,
+    a_ref, b_ref, prob_ref,
 ):
     h = pl.program_id(0)
     block = 256
-    for src, (k_ref, v_ref) in enumerate(((ko_ref, vo_ref), (kr_ref, vr_ref))):
-        k = k_ref[...]
-        v = v_ref[...]
-        for at in range(0, LATENTS, block):
-            rows = slice(at, at + block)
-            q = q_ref[rows, :]
-            dout = dout_ref[at // NUM : (at + block) // NUM].reshape(block, HDIM)
-            lse = stat_ref[pl.ds(h, 1), rows]
-            delta = stat_ref[pl.ds(2 + h, 1), rows]
+    for at in range(0, LATENTS, block):
+        rows = slice(at, at + block)
+        q = q_ref[rows, :]
+        dout = dout_ref[at // NUM : (at + block) // NUM].reshape(block, HDIM)
+        lse = stat_ref[pl.ds(h, 1), rows]
+        delta = stat_ref[pl.ds(2 + h, 1), rows]
+        a = 0
+        b = 0
+        for src, (k_ref, v_ref) in enumerate(((ko_ref, vo_ref), (kr_ref, vr_ref))):
+            k = k_ref[...]
             probs = jnp.exp2(dot(k, q, 1, 1) * EXP2_SCALE - lse)
-            dscore = (probs * (dot(v, dout, 1, 1) - delta)).astype(BF16)
+            dscore = (probs * (dot(v_ref[...], dout, 1, 1) - delta)).astype(BF16)
             probs = probs.astype(BF16)
             prob_ref[0, src, :, rows] = probs
-            score_ref[0, src, :, rows] = dscore
-            a = dot(k, dscore, 0, 0)
-            b = dot(k, probs, 0, 0)
-            if src == 0:
-                a_ref[:, rows] = a
-                b_ref[:, rows] = b
-            else:
-                a_ref[:, rows] += a
-                b_ref[:, rows] += b
+            a = a + dot(k, dscore, 0, 0)
+            b = b + dot(k, probs, 0, 0)
+        a_ref[:, rows] = a.astype(BF16)
+        b_ref[:, rows] = b.astype(BF16)
 
 
 def query_parts(place, queries, dout, stats, keys, keys_in, values, values_in):
@@ -290,14 +288,13 @@
             whole(8, LATENTS),
             head, head, head, head,
         ],
-        out_specs=[sums, sums, kept, kept],
+        out_specs=[sums, sums, kept],
     )
     return pl.pallas_call(
         query_kernel,
         out_shape=[
-            jax.ShapeDtypeStruct((WIDE, LATENTS), F32),
-            jax.ShapeDtypeStruct((WIDE, LATENTS), F32),
-            jax.ShapeDtypeStruct((HEADS_HERE, 2, tokens, LATENTS), BF16),
+            jax.ShapeDtypeStruct((WIDE, LATENTS), BF16),
+            jax.ShapeDtypeStruct((WIDE, LATENTS), BF16),
             jax.ShapeDtypeStruct((HEADS_HERE, 2, tokens, LATENTS), BF16),
         ],
         grid_spec=grid_spec,
@@ -310,35 +307,33 @@
 
 
 def token_kernel(
-    place_ref, q_ref, dout_ref, own_ref, stat_ref, prob_ref, score_ref,
-    dko_ref, dkr_ref, dvo_ref, dvr_ref, both_ref, q_scaled_ref,
+    place_ref, q_ref, dout_ref, own_ref, stat_ref, prob_ref, vo_ref, vr_ref,
+    dko_ref, dkr_ref, dvo_ref, dvr_ref, dout_scaled_ref, q_scaled_ref,
 ):
     h = pl.program_id(0)
 
     @pl.when(pl.program_id(1) == 0)
     def _():
         share = jnp.exp2(own_ref[pl.ds(h, 1), :] - stat_ref[pl.ds(h, 1), :])
-        rest = share * (own_ref[pl.ds(2 + h, 1), :] - stat_ref[pl.ds(2 + h, 1), :])
         share = jnp.transpose(jnp.broadcast_to(share, (HDIM, LATENTS)))
-        rest = jnp.transpose(jnp.broadcast_to(rest, (HDIM, LATENTS)))
-        q = q_ref[...].astype(F32)
         dout = dout_ref[...].reshape(LATENTS, HDIM).astype(F32)
-        both_ref[:, :HDIM] = (share * dout).astype(BF16)
-        both_ref[:, HDIM:] = (rest * q).astype(BF16)
-        q_scaled_ref[...] = (share * q).astype(BF16)
-
-    block = dko_ref.shape[0]
-    both = dot(prob_ref[0].reshape(2 * block, LATENTS), both_ref[...], 1, 0)
-    dk = dot(score_ref[0].reshape(2 * block, LATENTS), q_scaled_ref[...], 1, 0)
-    dk = ((dk + both[:, HDIM:]) * SCALE).astype(BF16)
-    dv = both[:, :HDIM].astype(BF16)
-    dko_ref[...] = dk[:block]
-    dkr_ref[...] = dk[block:]
-    dvo_ref[...] = dv[:block]
-    dvr_ref[...] = dv[block:]
-
-
-def token_grads(place, queries, dout, own_stats, stats, probs, dscores):
+        dout_scaled_ref[...] = (share * dout).astype(BF16)
+        q_scaled_ref[...] = (share * q_ref[...].astype(F32)).astype(BF16)
+
+    delta = stat_ref[pl.ds(2 + h, 1), :]
+    dout = dout_ref[...].reshape(LATENTS, HDIM)
+    dprobs = [dot(v_ref[...], dout, 1, 1) for v_ref in (vo_ref, vr_ref)]
+    dv = [dot(prob_ref[0, src], dout_scaled_ref[...], 1, 0) for src in (0, 1)]
+    dscores = [
+        (prob_ref[0, src].astype(F32) * (dprobs[src] - delta)).astype(BF16) for src in (0, 1)
+    ]
+    dk = [dot(dscores[src], q_scaled_ref[...], 1, 0) for src in (0, 1)]
+    for src, (dk_ref, dv_ref) in enumerate(((dko_ref, dvo_ref), (dkr_ref, dvr_ref))):
+        dv_ref[...] = dv[src].astype(BF16)
+        dk_ref[...] = (dk[src] * SCALE).astype(BF16)
+
+
+def token_grads(place, queries, dout, own_stats, stats, probs, values, values_in):
     tokens = probs.shape[2]
     block = 512
     own = pl.BlockSpec((block, HDIM), lambda h, i, c: (i, c[0] * HEADS_HERE + h))
@@ -352,10 +347,10 @@
             pl.BlockSpec((N_CHIPS, NUM, HDIM), lambda h, i, c: (0, 0, h)),
             whole(8, LATENTS),
             whole(8, LATENTS),
-            kept, kept,
+            kept, own, own,
         ],
         out_specs=[own, other, own, other],
-        scratch_shapes=[pltpu.VMEM((LATENTS, WIDE), BF16), pltpu.VMEM((LATENTS, HDIM), BF16)],
+        scratch_shapes=[pltpu.VMEM((LATENTS, HDIM), BF16), pltpu.VMEM((LATENTS, HDIM), BF16)],
     )
     full = jax.ShapeDtypeStruct((tokens, 2 * WIDE), BF16)
     half_wide = jax.ShapeDtypeStruct((tokens, WIDE), BF16)
@@ -365,10 +360,10 @@
         grid_spec=grid_spec,
         compiler_params=params(60),
         cost_estimate=pl.CostEstimate(
-            flops=6_000_000_000, bytes_accessed=22_000_000, transcendentals=0
+            flops=8_000_000_000, bytes_accessed=14_000_000, transcendentals=0
         ),
         name="token",
-    )(place, queries, dout, own_stats, stats, probs, dscores)
+    )(place, queries, dout, own_stats, stats, probs, values, values_in)
 
 
 def weight_kernel(place_ref, att_ref, own_ref, other_ref, out_ref, cot_ref):
@@ -380,13 +375,13 @@
     out_ref[...] = dot(att, cot, 0, 0)
 
 
-def weight(place, msg, cot_in):
+def weight(place, msg, cot, cot_in):
     grid_spec = pltpu.PrefetchScalarGridSpec(
         num_scalar_prefetch=1,
         grid=(1,),
         in_specs=[
             pl.BlockSpec((N_CHIPS, NUM, WIDE), lambda i, c: (0, 1, 0)),
-            pl.BlockSpec((N_CHIPS, COT, WIDE), lambda i, c: (0, 2 * NUM // COT, 0)),
+            whole(N_CHIPS, COT, WIDE),
             whole(N_CHIPS, COT, WIDE),
         ],
         out_specs=whole(WIDE, WIDE),
@@ -398,7 +393,7 @@
         grid_spec=grid_spec,
         compiler_params=params(24),
         name="weight",
-    )(place, msg, msg, cot_in)
+    )(place, msg, cot, cot_in)
 
 
 def swap(x):
@@ -434,7 +429,8 @@
 def body(queries, prefix_keys, prefix_values, out_weight, out_grad):
     core = lax.axis_index("core")
     at_x, at_zl = lax.axis_index("x"), lax.axis_index("zl")
-    place = jnp.stack([core, lax.axis_index("y"), lax.axis_index("zh")]).astype(jnp.int32)
+    odd_x = lax.rem(at_x, 2)
+    place = jnp.stack([core, lax.axis_index("y"), lax.axis_index("zh"), odd_x]).astype(jnp.int32)
     cot = gather(out_grad, TP, 8)
     keys_in = swap(prefix_keys)
     values_in = swap(prefix_values)
@@ -446,9 +442,14 @@
     part, lse = forward(place, queries, *tokens)
     msg1, own_stats = message(part, lse, dout)
     msg1 = lax.all_to_all(msg1, CHIPS, 0, 0, tiled=True)
-    a, b, probs, dscores = query_parts(place, queries, dout, own_stats, *tokens)
-
-    att64, stats, msg2 = combine(place, msg1, cot, own_stats, a, b)
+    cot_part = dout[:, NUM:]
+    cot_other = lax.ppermute(cot_part, "x", [(0, 1), (1, 0), (2, 3), (3, 2)])
+    cot_mine = in_order(odd_x, cot_part, cot_other, 1)
+    cot_in = swap(cot_mine)
+    a, b, probs = query_parts(place, queries, dout, own_stats, *tokens)
+
+    msg1, cot_mine, cot_in = lax.optimization_barrier((msg1, cot_mine, cot_in))
+    att64, stats, msg2 = combine(place, msg1, own_stats, a, b)
     msg2 = lax.all_to_all(msg2, CHIPS, 0, 0, tiled=True)
 
     att32 = in_order(core, half(att64, core, 0), swap(half(att64, 1 - core, 0)), 1)
@@ -459,7 +460,7 @@
     ]
     from_x = [shift(by_x[d].astype(BF16), "x", d) for d in (1, 2, 3)]
     dk, dk_out, dv, dv_out = token_grads(
-        place, queries, dout, own_stats, after(stats, by_x[0]), probs, dscores
+        place, queries, dout, own_stats, after(stats, by_x[0]), probs, prefix_values, values_in
     )
     own_x, *from_x = lax.optimization_barrier((by_x[0], *from_x, dk))[:4]
     over_x = own_x + sum(x.astype(F32) for x in from_x)
@@ -473,15 +474,13 @@
     other_cols = (jnp.int32(0), ((1 - core) * WIDE).astype(jnp.int32))
     key_grad = lax.dynamic_update_slice(dk, swap(dk_out), other_cols)
     value_grad = lax.dynamic_update_slice(dv, swap(dv_out), other_cols)
-    from_zl = after(from_zl, key_grad, value_grad)
+
+    msg2, from_zl = lax.optimization_barrier((msg2, from_zl, key_grad, value_grad))[:2]
     latent_out = (own_zl + from_zl.astype(F32)).astype(BF16)
-
-    msg2 = after(msg2, latent_out)
-    cot_in = swap(msg2[:, 2 * NUM :])
     dq64 = jnp.sum(msg2[:, :NUM].astype(F32), axis=0).astype(BF16)
     dq_in = swap(half(dq64, 1 - core, 0))
     query_grad = in_order(core, half(dq64, core, 0), dq_in, 1)
-    weight_part = weight(place, msg2, cot_in)
+    weight_part = weight(place, msg2, cot_mine, cot_in)
     weight_in = swap(half(weight_part, 1 - core, 1))
     weight_grad = in_order(core, half(weight_part, core, 1), weight_in, 0)
     return latent_out, query_grad, key_grad, value_grad, weight_grad

time: 135 us -> 132 us (0.978)
  waiting for transfers between devices: 31.6 us -> 24.7 us
  starting transfers between devices: 33.9 us -> 38 us
  Pallas kernels: 44.2 us -> 42.7 us
    all_to_all x1, waiting for transfers between devices: 10.8 us -> 3.78 us  [body(): msg1 = lax.all_to_all(msg1, CHIPS, 0, 0, tiled=True)]
    ppermute x9, starting transfers between devices: 10.3 us -> 16.1 us  [swap(): return lax.ppermute(x, 'core', [(0, 1), (1, 0)])]
    ppermute x0 -> x1, waiting for transfers between devices: none -> 3.8 us  [body(): cot_other = lax.ppermute(cot_part, 'x', [(0, 1), (1, 0), (2, 3), (3, 2)])]
    ppermute x9, waiting for transfers between devices: 4.75 us -> 1.65 us  [swap(): return lax.ppermute(x, 'core', [(0, 1), (1, 0)])]
    all_to_all x1, waiting for transfers between devices: 8.45 us -> 11.1 us  [body(): dout = lax.all_to_all(dout, CHIPS, 0, 0, tiled=True)]
    all_to_all x1, starting transfers between devices: 6.18 us -> 3.65 us  [body(): msg2 = lax.all_to_all(msg2, CHIPS, 0, 0, tiled=True)]
    all_to_all x1, waiting for transfers between devices: 5.96 us -> 3.85 us  [body(): msg2 = lax.all_to_all(msg2, CHIPS, 0, 0, tiled=True)]
    pallas_call x1, Pallas kernels: 13.4 us -> 11.7 us  [query_parts(): pl.pallas_call(query_kernel, out_shape=[jax.ShapeDtypeStruct((WIDE, LATEN...]
  transfers between devices with their start and end apart: 16 -> 17, of which waited for: 9 -> 8; matrix products, arithmetic and copies ran while one was open for 6% -> 7% of each run, Pallas kernels for 25% -> 25%
where the time goes in v3:
time: 132 us; the launch traced here: 131 us
  Pallas kernels  42.7 us (32%)
  starting transfers between devices  38 us (29%)
  waiting for transfers between devices  24.7 us (19%)
  blocking collectives  10.1 us (8%)
  local copies, waits for them, and re-layouts  9.28 us (7%)
  matrix products  3.01 us (2%)
  other arithmetic  2.77 us (2%)
    ppermute x9, starting transfers between devices, swap(): return lax.ppermute(x, 'core', [(0, 1), (1, 0)])  16.1 us
    pallas_call x1, Pallas kernels, query_parts(): pl.pallas_call(query_kernel, out_shape=[jax.ShapeDtypeStruct((WIDE, LATEN...  11.7 us
    pallas_call x1, Pallas kernels, token_grads(): pl.pallas_call(token_kernel, out_shape=[full, half_wide, full, half_wide]...  11.4 us
    all_to_all x1, waiting for transfers between devices, body(): dout = lax.all_to_all(dout, CHIPS, 0, 0, tiled=True)  11.1 us
    all_to_all x1, blocking collectives, gather(): return lax.all_to_all(tiled, axes, 0, 0, tiled=True)  10.1 us
    all_to_all x1, starting transfers between devices, body(): dout = lax.all_to_all(dout, CHIPS, 0, 0, tiled=True)  10 us
    pallas_call x1, Pallas kernels, forward(): pl.pallas_call(forward_kernel, out_shape=[jax.ShapeDtypeStruct((LATENTS,...  9.07 us
    unnamed x27, local copies, waits for them, and re-layouts  4.74 us
  transfers between devices with their start and end apart: 17, of which 8 were waited for; matrix products, arithmetic and copies ran while one was open for 7% of the time, Pallas kernels for 25%

profile of v3, /device:TPU:1, one launch (start us, length us, event | category | flops | bytes accessed | tf_op | source)
XLA Modules:
  0.0 131.5 jit_solution(11641405460186915687)
XLA Ops:
  0.6 3.3 %collective-permute-start = (bf16[1024,512]{1,0:T(8,128)(2,1)}, bf16[1024,512]{1,0:T(8,128)(2,1)S(1)}, u32[]{:S(2)}, u32[]{:S(2)}) collective-permute-start(bf16[1024,512]{1,0:T(8,128)(2,1)} %ko_ref.3), channel_id=1, source_target_pairs={{0,8},{8,0},{1,9},{9,1},{2,10},{10,2},{3,11},{11,3},{4,12},{12,4},... | collective-permute-start | bytes 3145736 | tf_op jit(solution)/shard_map/ppermute | solution.py:400
  4.8 10.1 %all_to_all.20.own_ref = bf16[8,32,512]{2,1,0:T(8,128)(2,1)S(1)} all-to-all(bf16[8,32,512]{2,1,0:T(8,128)(2,1)S(1)} %broadcast_in_dim.2), channel_id=1, replica_groups=mesh['y'=4,'zh'=4,'core'=2,'x'=4,'zl'=2] {'x','zl'}, dimensions={0} | all-to-all | bytes 524288 | tf_op jit(solution)/shard_map/all_to_all | solution.py:418
  15.9 1.6 %collective-permute-start.2 = (bf16[8,32,512]{2,1,0:T(8,128)(2,1)S(1)}, bf16[8,32,512]{2,1,0:T(8,128)(2,1)S(1)}, u32[]{:S(2)}, u32[]{:S(2)}) collective-permute-start(bf16[8,32,512]{2,1,0:T(8,128)(2,1)S(1)} %all_to_all.20.own_ref), channel_id=1, source_target_pairs={{0,8},{8,0},{1,9},{9,1},{2,10},{10,2},{3,11},{11,3},{4,12},{12,4},... | collective-permute-start | bytes 786440 | tf_op jit(solution)/shard_map/ppermute | solution.py:400
  19.4 4.1 %dout.1 = bf16[16,80,256]{2,1,0:T(8,128)(2,1)} custom-call(s32[4]{0:T(128)} %pad_add_fusion.place_ref, bf16[8,32,512]{2,1,0:T(8,128)(2,1)} %copy-done.7, bf16[8,32,512]{2,1,0:T(8,128)(2,1)} %copy-done.8, bf16[512,4096]{1,0:T(8,128)(2,1)} %w_ref.1), custom_call_target="tpu_custom_call" | custom-call | tf_op jit(solution)/shard_map/dout/pallas_call | solution.py:80
  23.4 10.0 %all-to-all-start.1 = ((bf16[16,80,256]{2,1,0:T(8,128)(2,1)}), bf16[16,80,256]{2,1,0:T(8,128)(2,1)S(1)}, u32[]{:S(2)}, u32[]{:S(2)}) async-start(bf16[16,80,256]{2,1,0:T(8,128)(2,1)} %dout.1), calls=%async_computation.1 | async-start | bytes 1310720 | tf_op jit(solution)/shard_map/all_to_all | solution.py:441
  33.5 9.1 %forward.1 = (bf16[1024,256]{1,0:T(8,128)(2,1)}, f32[8,1024]{1,0:T(8,128)}) custom-call(s32[4]{0:T(128)} %pad_add_fusion.place_ref, bf16[1024,512]{1,0:T(8,128)(2,1)} %q_ref.5, bf16[1024,512]{1,0:T(8,128)(2,1)} %ko_ref.3, bf16[1024,512]{1,0:T(8,128)(2,1)} %copy-done.10, bf16[1024,512]{1,0:T(8,128)(2,1)} %vo_ref.5, bf16[1024,512]{1,0:T(8,128)(2,1)} %copy-done.9), custom_call_target="tpu_custom_call" | custom-call | flops 8999999488 | bytes 4000000 | tf_op jit(solution)/shard_map/forward/pallas_call | solution.py:128
  42.5 11.1 %all-to-all-done.1.dout_ref = bf16[16,80,256]{2,1,0:T(8,128)(2,1)S(1)} async-done(((bf16[16,80,256]{2,1,0:T(8,128)(2,1)}), bf16[16,80,256]{2,1,0:T(8,128)(2,1)S(1)}, u32[]{:S(2)}, u32[]{:S(2)}) %all-to-all-start.1) | async-done | bytes 655392 | tf_op jit(solution)/shard_map/all_to_all | solution.py:441
  54.5 2.8 %message.1 = (bf16[16,112,256]{2,1,0:T(8,128)(2,1)}, f32[8,1024]{1,0:T(8,128)}) custom-call(bf16[1024,256]{1,0:T(8,128)(2,1)} %get-tuple-element.34.part_ref, f32[8,1024]{1,0:T(8,128)} %get-tuple-element.35.lse_ref, bf16[16,80,256]{2,1,0:T(8,128)(2,1)} %copy-done.6), custom_call_target="tpu_custom_call" | custom-call | tf_op jit(solution)/shard_map/message/pallas_call | solution.py:166
  57.2 4.3 %all-to-all-start.2 = ((bf16[16,112,256]{2,1,0:T(8,128)(2,1)}), bf16[16,112,256]{2,1,0:T(8,128)(2,1)S(1)}, u32[]{:S(2)}, u32[]{:S(2)}) async-start(bf16[16,112,256]{2,1,0:T(8,128)(2,1)} %get-tuple-element.37), calls=%async_computation.2 | async-start | bytes 1835008 | tf_op jit(solution)/shard_map/all_to_all | solution.py:444
  62.6 3.8 %collective-permute-done.3 = bf16[16,16,256]{2,1,0:T(8,128)(2,1)S(1)} collective-permute-done((bf16[16,16,256]{2,1,0:T(8,128)(2,1)S(1)}, bf16[16,16,256]{2,1,0:T(8,128)(2,1)S(1)}, u32[]{:S(2)}, u32[]{:S(2)}) %collective-permute-start.3) | collective-permute-done | bytes 131104 | tf_op jit(solution)/shard_map/ppermute | solution.py:446
  66.5 3.3 %collective-permute-start.4 = (bf16[16,32,256]{2,1,0:T(8,128)(2,1)S(1)}, bf16[16,32,256]{2,1,0:T(8,128)(2,1)S(1)}, u32[]{:S(2)}, u32[]{:S(2)}) collective-permute-start(bf16[16,32,256]{2,1,0:T(8,128)(2,1)S(1)} %maximum_select_fusion.own_ref), channel_id=1, source_target_pairs={{0,8},{8,0},{1,9},{9,1},{2,10},{10,2},{3,11},{11,3},{4,12},{12,4},... | collective-permute-start | bytes 786440 | tf_op jit(solution)/shard_map/ppermute | solution.py:400
  69.8 11.7 %query.1 = (bf16[256,1024]{1,0:T(8,128)(2,1)}, bf16[256,1024]{1,0:T(8,128)(2,1)}, bf16[2,2,1024,1024]{3,2,1,0:T(8,128)(2,1)}) custom-call(s32[4]{0:T(128)} %pad_add_fusion.place_ref, bf16[1024,512]{1,0:T(8,128)(2,1)} %q_ref.5, bf16[16,80,256]{2,1,0:T(8,128)(2,1)} %copy-done.6, f32[8,1024]{1,0:T(8,128)} %get-tuple-element.39.stat_ref.own_ref, ...), custom_call_target="tpu_custom_call" | custom-call | flops 12000000000 | bytes 20000000 | tf_op jit(solution)/shard_map/query/pallas_call | solution.py:293
  81.5 3.8 %all-to-all-done.2.msg_ref = bf16[16,112,256]{2,1,0:T(8,128)(2,1)S(1)} async-done(((bf16[16,112,256]{2,1,0:T(8,128)(2,1)}), bf16[16,112,256]{2,1,0:T(8,128)(2,1)S(1)}, u32[]{:S(2)}, u32[]{:S(2)}) %all-to-all-start.2) | async-done | bytes 917536 | tf_op jit(solution)/shard_map/all_to_all | solution.py:444
  85.3 1.0 copy-done
  87.4 2.8 %combine.1 = (bf16[64,256]{1,0:T(8,128)(2,1)S(1)}, f32[8,1024]{1,0:T(8,128)S(1)}, bf16[16,128,256]{2,1,0:T(8,128)(2,1)}) custom-call(s32[4]{0:T(128)S(1)} %copy-done.3, bf16[16,112,256]{2,1,0:T(8,128)(2,1)S(1)} %all-to-all-done.2.msg_ref, f32[8,1024]{1,0:T(8,128)S(1)} %copy-done.2, bf16[256,1024]{1,0:T(8,128)(2,1)S(1)} %copy-done, ...), custom_call_target="tpu_custom_call" | custom-call | tf_op jit(solution)/shard_map/combine/pallas_call | solution.py:238
  90.2 3.7 %collective-permute-start.5 = (bf16[32,256]{1,0:T(8,128)(2,1)S(1)}, bf16[32,256]{1,0:T(8,128)(2,1)S(1)}, u32[]{:S(2)}, u32[]{:S(2)}) collective-permute-start(bf16[32,256]{1,0:T(8,128)(2,1)S(1)} %get-tuple-element.67), channel_id=1, source_target_pairs={{0,8},{8,0},{1,9},{9,1},{2,10},{10,2},{3,11},{11,3},{4,12},{12,4},... | collective-permute-start | bytes 49160 | tf_op jit(solution)/shard_map/ppermute | solution.py:400
  93.9 3.7 %all-to-all-start.3 = ((bf16[16,128,256]{2,1,0:T(8,128)(2,1)}), bf16[16,128,256]{2,1,0:T(8,128)(2,1)S(1)}, u32[]{:S(2)}, u32[]{:S(2)}) async-start(bf16[16,128,256]{2,1,0:T(8,128)(2,1)} %get-tuple-element.51), calls=%async_computation.3 | async-start | bytes 2097152 | tf_op jit(solution)/shard_map/all_to_all | solution.py:453
  97.6 3.0 %fusion.4 = f32[32,4096]{1,0:T(8,128)S(1)} fusion(bf16[512,4096]{1,0:T(8,128)(2,1)} %w_ref.1, bf16[32,256]{1,0:T(8,128)(2,1)S(1)} %collective-permute-done.5, bf16[32,256]{1,0:T(8,128)(2,1)S(1)} %get-tuple-element.66, pred[]{:T(512)S(6)} %eq.8), kind=kOutput, calls=%fused_computation.15 | convolution fusion | flops 134365184 | bytes 4751361 | tf_op jit(solution)/shard_map/dot_general | solution.py:31
  101.7 1.6 %collective-permute-start.7 = (bf16[32,1024]{1,0:T(8,128)(2,1)S(1)}, bf16[32,1024]{1,0:T(8,128)(2,1)S(1)}, u32[]{:S(2)}, u32[]{:S(2)}) collective-permute-start(bf16[32,1024]{1,0:T(8,128)(2,1)S(1)} %bitcast.26), channel_id=1, source_target_pairs={{0,4},{2,6},{4,0},{6,2},{1,5},{3,7},{5,1},{7,3},{8,12},{10,14},{12... | collective-permute-start | bytes 196616 | tf_op jit(solution)/shard_map/ppermute | solution.py:422
  103.3 2.1 %collective-permute-start.8 = (bf16[32,1024]{1,0:T(8,128)(2,1)S(1)}, bf16[32,1024]{1,0:T(8,128)(2,1)S(1)}, u32[]{:S(2)}, u32[]{:S(2)}) collective-permute-start(bf16[32,1024]{1,0:T(8,128)(2,1)S(1)} %bitcast.27), channel_id=1, source_target_pairs={{0,6},{2,0},{4,2},{6,4},{1,7},{3,1},{5,3},{7,5},{8,14},{10,8},{12,... | collective-permute-start | bytes 196616 | tf_op jit(solution)/shard_map/ppermute | solution.py:422
  105.4 11.4 %token_.1 = (bf16[1024,512]{1,0:T(8,128)(2,1)}, bf16[1024,256]{1,0:T(8,128)(2,1)}, bf16[1024,512]{1,0:T(8,128)(2,1)}, bf16[1024,256]{1,0:T(8,128)(2,1)}) custom-call(s32[4]{0:T(128)} %pad_add_fusion.place_ref, bf16[1024,512]{1,0:T(8,128)(2,1)} %q_ref.5, bf16[16,80,256]{2,1,0:T(8,128)(2,1)} %copy-done.6, f32[8,1024]{1,0:T(8,128)} %get-tuple-element.39.stat_ref.own_ref, ...), custom_call_target="tpu_custom_call" | custom-call | flops 8000000000 | bytes 14000000 | tf_op jit(solution)/shard_map/token/pallas_call | solution.py:357
  116.8 1.5 %collective-permute-start.10 = (bf16[1024,256]{1,0:T(8,128)(2,1)}, bf16[1024,256]{1,0:T(8,128)(2,1)S(1)}, u32[]{:S(2)}, u32[]{:S(2)}) collective-permute-start(bf16[1024,256]{1,0:T(8,128)(2,1)} %get-tuple-element.52), channel_id=1, source_target_pairs={{0,8},{8,0},{1,9},{9,1},{2,10},{10,2},{3,11},{11,3},{4,12},{12,4},... | collective-permute-start | bytes 1572872 | tf_op jit(solution)/shard_map/ppermute | solution.py:400
  122.2 3.8 %all-to-all-done.3.att_ref = bf16[16,128,256]{2,1,0:T(8,128)(2,1)S(1)} async-done(((bf16[16,128,256]{2,1,0:T(8,128)(2,1)}), bf16[16,128,256]{2,1,0:T(8,128)(2,1)S(1)}, u32[]{:S(2)}, u32[]{:S(2)}) %all-to-all-start.3) | async-done | bytes 1048608 | tf_op jit(solution)/shard_map/all_to_all | solution.py:453
  126.2 2.2 %collective-permute-start.12 = (bf16[32,256]{1,0:T(8,128)(2,1)S(1)}, bf16[32,256]{1,0:T(8,128)(2,1)S(1)}, u32[]{:S(2)}, u32[]{:S(2)}) collective-permute-start(bf16[32,256]{1,0:T(8,128)(2,1)S(1)} %get-tuple-element.65), channel_id=1, source_target_pairs={{0,8},{8,0},{1,9},{9,1},{2,10},{10,2},{3,11},{11,3},{4,12},{12,4},... | collective-permute-start | bytes 49160 | tf_op jit(solution)/shard_map/ppermute | solution.py:400
  (66 shorter events, 14.9 us)
Async XLA Ops:
  0.6 14.3 %collective-permute-start = (bf16[1024,512]{1,0:T(8,128)(2,1)}, bf16[1024,512]{1,0:T(8,128)(2,1)S(1)}, u32[]{:S(2)}, u32[]{:S(2)}) collective-permute-start(bf16[1024,512]{1,0:T(8,128)(2,1)} %ko_ref.3), channel_id=1, source_target_pairs={{0,8},{8,0},{1,9},{9,1},{2,10},{10,2},{3,11},{11,3},{4,12},{12,4},... | collective-permute-start | bytes 3145736 | tf_op jit(solution)/shard_map/ppermute | solution.py:400
  4.0 11.0 %collective-permute-start.1 = (bf16[1024,512]{1,0:T(8,128)(2,1)}, bf16[1024,512]{1,0:T(8,128)(2,1)S(1)}, u32[]{:S(2)}, u32[]{:S(2)}) collective-permute-start(bf16[1024,512]{1,0:T(8,128)(2,1)} %vo_ref.5), channel_id=1, source_target_pairs={{0,8},{8,0},{1,9},{9,1},{2,10},{10,2},{3,11},{11,3},{4,12},{12,4},... | collective-permute-start | bytes 3145736 | tf_op jit(solution)/shard_map/ppermute | solution.py:400
  14.9 3.7 %copy-start.7 = (bf16[8,32,512]{2,1,0:T(8,128)(2,1)}, bf16[8,32,512]{2,1,0:T(8,128)(2,1)S(1)}, u32[]{:S(2)}) copy-start(bf16[8,32,512]{2,1,0:T(8,128)(2,1)S(1)} %all_to_all.20.own_ref) | copy-start | bytes 786436
  15.9 17.5 %copy-start.9 = (bf16[1024,512]{1,0:T(8,128)(2,1)}, bf16[1024,512]{1,0:T(8,128)(2,1)S(1)}, u32[]{:S(2)}) copy-start(bf16[1024,512]{1,0:T(8,128)(2,1)S(1)} %collective-permute-done.1.vr_ref) | copy-start | bytes 3145732
  15.9 2.7 %collective-permute-start.2 = (bf16[8,32,512]{2,1,0:T(8,128)(2,1)S(1)}, bf16[8,32,512]{2,1,0:T(8,128)(2,1)S(1)}, u32[]{:S(2)}, u32[]{:S(2)}) collective-permute-start(bf16[8,32,512]{2,1,0:T(8,128)(2,1)S(1)} %all_to_all.20.own_ref), channel_id=1, source_target_pairs={{0,8},{8,0},{1,9},{9,1},{2,10},{10,2},{3,11},{11,3},{4,12},{12,4},... | collective-permute-start | bytes 786440 | tf_op jit(solution)/shard_map/ppermute | solution.py:400
  23.4 30.2 %all-to-all-start.1 = ((bf16[16,80,256]{2,1,0:T(8,128)(2,1)}), bf16[16,80,256]{2,1,0:T(8,128)(2,1)S(1)}, u32[]{:S(2)}, u32[]{:S(2)}) async-start(bf16[16,80,256]{2,1,0:T(8,128)(2,1)} %dout.1), calls=%async_computation.1 | async-start | bytes 1310720 | tf_op jit(solution)/shard_map/all_to_all | solution.py:441
  57.2 28.1 %all-to-all-start.2 = ((bf16[16,112,256]{2,1,0:T(8,128)(2,1)}), bf16[16,112,256]{2,1,0:T(8,128)(2,1)S(1)}, u32[]{:S(2)}, u32[]{:S(2)}) async-start(bf16[16,112,256]{2,1,0:T(8,128)(2,1)} %get-tuple-element.37), calls=%async_computation.2 | async-start | bytes 1835008 | tf_op jit(solution)/shard_map/all_to_all | solution.py:444
  62.5 3.9 %collective-permute-start.3 = (bf16[16,16,256]{2,1,0:T(8,128)(2,1)S(1)}, bf16[16,16,256]{2,1,0:T(8,128)(2,1)S(1)}, u32[]{:S(2)}, u32[]{:S(2)}) collective-permute-start(bf16[16,16,256]{2,1,0:T(8,128)(2,1)S(1)} %slice.8), channel_id=1, source_target_pairs={{0,2},{2,0},{4,6},{6,4},{1,3},{3,1},{5,7},{7,5},{8,10},{10,8},{12,... | collective-permute-start | bytes 393224 | tf_op jit(solution)/shard_map/ppermute | solution.py:446
  66.5 15.0 %collective-permute-start.4 = (bf16[16,32,256]{2,1,0:T(8,128)(2,1)S(1)}, bf16[16,32,256]{2,1,0:T(8,128)(2,1)S(1)}, u32[]{:S(2)}, u32[]{:S(2)}) collective-permute-start(bf16[16,32,256]{2,1,0:T(8,128)(2,1)S(1)} %maximum_select_fusion.own_ref), channel_id=1, source_target_pairs={{0,8},{8,0},{1,9},{9,1},{2,10},{10,2},{3,11},{11,3},{4,12},{12,4},... | collective-permute-start | bytes 786440 | tf_op jit(solution)/shard_map/ppermute | solution.py:400
  69.8 15.5 %copy-start.2 = (f32[8,1024]{1,0:T(8,128)S(1)}, f32[8,1024]{1,0:T(8,128)}, u32[]{:S(2)}) copy-start(f32[8,1024]{1,0:T(8,128)} %get-tuple-element.39.stat_ref.own_ref) | copy-start | bytes 98308
  69.8 15.5 %copy-start.3 = (s32[4]{0:T(128)S(1)}, s32[4]{0:T(128)}, u32[]{:S(2)}) copy-start(s32[4]{0:T(128)} %pad_add_fusion.place_ref) | copy-start | bytes 52
  85.3 1.0 copy-start
  90.2 3.7 %copy-start.5 = (f32[8,1024]{1,0:T(8,128)}, f32[8,1024]{1,0:T(8,128)S(1)}, u32[]{:S(2)}) copy-start(f32[8,1024]{1,0:T(8,128)S(1)} %get-tuple-element.44.stat_ref) | copy-start | bytes 98308
  90.2 7.3 %collective-permute-start.5 = (bf16[32,256]{1,0:T(8,128)(2,1)S(1)}, bf16[32,256]{1,0:T(8,128)(2,1)S(1)}, u32[]{:S(2)}, u32[]{:S(2)}) collective-permute-start(bf16[32,256]{1,0:T(8,128)(2,1)S(1)} %get-tuple-element.67), channel_id=1, source_target_pairs={{0,8},{8,0},{1,9},{9,1},{2,10},{10,2},{3,11},{11,3},{4,12},{12,4},... | collective-permute-start | bytes 49160 | tf_op jit(solution)/shard_map/ppermute | solution.py:400
  93.9 32.2 %all-to-all-start.3 = ((bf16[16,128,256]{2,1,0:T(8,128)(2,1)}), bf16[16,128,256]{2,1,0:T(8,128)(2,1)S(1)}, u32[]{:S(2)}, u32[]{:S(2)}) async-start(bf16[16,128,256]{2,1,0:T(8,128)(2,1)} %get-tuple-element.51), calls=%async_computation.3 | async-start | bytes 2097152 | tf_op jit(solution)/shard_map/all_to_all | solution.py:453
  101.6 17.1 %collective-permute-start.6 = (bf16[32,1024]{1,0:T(8,128)(2,1)S(1)}, bf16[32,1024]{1,0:T(8,128)(2,1)S(1)}, u32[]{:S(2)}, u32[]{:S(2)}) collective-permute-start(bf16[32,1024]{1,0:T(8,128)(2,1)S(1)} %bitcast.25), channel_id=1, source_target_pairs={{0,2},{2,4},{4,6},{6,0},{1,3},{3,5},{5,7},{7,1},{8,10},{10,12},{12... | collective-permute-start | bytes 196616 | tf_op jit(solution)/shard_map/ppermute | solution.py:422
  101.7 16.9 %collective-permute-start.7 = (bf16[32,1024]{1,0:T(8,128)(2,1)S(1)}, bf16[32,1024]{1,0:T(8,128)(2,1)S(1)}, u32[]{:S(2)}, u32[]{:S(2)}) collective-permute-start(bf16[32,1024]{1,0:T(8,128)(2,1)S(1)} %bitcast.26), channel_id=1, source_target_pairs={{0,4},{2,6},{4,0},{6,2},{1,5},{3,7},{5,1},{7,3},{8,12},{10,14},{12... | collective-permute-start | bytes 196616 | tf_op jit(solution)/shard_map/ppermute | solution.py:422
  103.3 15.4 %collective-permute-start.8 = (bf16[32,1024]{1,0:T(8,128)(2,1)S(1)}, bf16[32,1024]{1,0:T(8,128)(2,1)S(1)}, u32[]{:S(2)}, u32[]{:S(2)}) collective-permute-start(bf16[32,1024]{1,0:T(8,128)(2,1)S(1)} %bitcast.27), channel_id=1, source_target_pairs={{0,6},{2,0},{4,2},{6,4},{1,7},{3,1},{5,3},{7,5},{8,14},{10,8},{12,... | collective-permute-start | bytes 196616 | tf_op jit(solution)/shard_map/ppermute | solution.py:422
  105.4 22.9 %copy-start.4 = (s32[4]{0:T(128)S(1)}, s32[4]{0:T(128)}, u32[]{:S(2)}) copy-start(s32[4]{0:T(128)} %pad_add_fusion.place_ref) | copy-start | bytes 52
  116.8 3.3 %collective-permute-start.10 = (bf16[1024,256]{1,0:T(8,128)(2,1)}, bf16[1024,256]{1,0:T(8,128)(2,1)S(1)}, u32[]{:S(2)}, u32[]{:S(2)}) collective-permute-start(bf16[1024,256]{1,0:T(8,128)(2,1)} %get-tuple-element.52), channel_id=1, source_target_pairs={{0,8},{8,0},{1,9},{9,1},{2,10},{10,2},{3,11},{11,3},{4,12},{12,4},... | collective-permute-start | bytes 1572872 | tf_op jit(solution)/shard_map/ppermute | solution.py:400
  118.3 2.6 %collective-permute-start.11 = (bf16[1024,256]{1,0:T(8,128)(2,1)}, bf16[1024,256]{1,0:T(8,128)(2,1)S(1)}, u32[]{:S(2)}, u32[]{:S(2)}) collective-permute-start(bf16[1024,256]{1,0:T(8,128)(2,1)} %get-tuple-element.54), channel_id=1, source_target_pairs={{0,8},{8,0},{1,9},{9,1},{2,10},{10,2},{3,11},{11,3},{4,12},{12,4},... | collective-permute-start | bytes 1572872 | tf_op jit(solution)/shard_map/ppermute | solution.py:400
  118.9 3.3 %collective-permute-start.9 = (bf16[32,512]{1,0:T(8,128)(2,1)S(1)}, bf16[32,512]{1,0:T(8,128)(2,1)S(1)}, u32[]{:S(2)}, u32[]{:S(2)}) collective-permute-start(bf16[32,512]{1,0:T(8,128)(2,1)S(1)} %bitcast.28), channel_id=1, source_target_pairs={{0,1},{1,0},{2,3},{3,2},{4,5},{5,4},{6,7},{7,6},{8,9},{9,8},{10,11... | collective-permute-start | bytes 98312 | tf_op jit(solution)/shard_map/ppermute | solution.py:468
  126.2 3.9 %collective-permute-start.12 = (bf16[32,256]{1,0:T(8,128)(2,1)S(1)}, bf16[32,256]{1,0:T(8,128)(2,1)S(1)}, u32[]{:S(2)}, u32[]{:S(2)}) collective-permute-start(bf16[32,256]{1,0:T(8,128)(2,1)S(1)} %get-tuple-element.65), channel_id=1, source_target_pairs={{0,8},{8,0},{1,9},{9,1},{2,10},{10,2},{3,11},{11,3},{4,12},{12,4},... | collective-permute-start | bytes 49160 | tf_op jit(solution)/shard_map/ppermute | solution.py:400
  129.3 1.4 %collective-permute-start.13 = (f32[256,128]{1,0:T(8,128)S(1)}, f32[256,128]{1,0:T(8,128)S(1)}, u32[]{:S(2)}, u32[]{:S(2)}) collective-permute-start(f32[256,128]{1,0:T(8,128)S(1)} %get-tuple-element.63), channel_id=1, source_target_pairs={{0,8},{8,0},{1,9},{9,1},{2,10},{10,2},{3,11},{11,3},{4,12},{12,4},... | collective-permute-start | bytes 393224 | tf_op jit(solution)/shard_map/ppermute | solution.py:400
  (4 other events, 3.6 us)

commit v4 on v3

--- a/solution.py
+++ b/solution.py
@@ -178,7 +178,7 @@
 
 
 def combine_kernel(
-    place_ref, msg_ref, own_ref, a_ref, b_ref, att_ref, stat_ref, out_ref
+    place_ref, msg_ref, own_ref, sums_ref, att_ref, stat_ref, out_ref
 ):
     y = place_ref[1]
     zh = place_ref[2]
@@ -221,17 +221,19 @@
         cols = head_cols(h)
         share = jnp.exp2(own_ref[h : h + 1, :] - stat_ref[h : h + 1, :]) * SCALE
         rest = stat_ref[2 + h : 3 + h, :] - own_ref[2 + h : 3 + h, :]
-        dq = jnp.transpose(share * (a_ref[cols, :].astype(F32) - rest * b_ref[cols, :].astype(F32))).astype(BF16)
+        at_scores = sums_ref[0, cols, :].astype(F32)
+        at_probs = sums_ref[1, cols, :].astype(F32)
+        dq = jnp.transpose(share * (at_scores - rest * at_probs)).astype(BF16)
         out_ref[:, 0:NUM, cols] = dq.reshape(N_CHIPS, NUM, HDIM)
 
 
-def combine(place, msg, own_stats, a, b):
+def combine(place, msg, own_stats, sums):
     grid_spec = pltpu.PrefetchScalarGridSpec(
         num_scalar_prefetch=1,
         grid=(1,),
         in_specs=[
             whole(N_CHIPS, ROWS1, WIDE), whole(8, LATENTS),
-            whole(WIDE, LATENTS), whole(WIDE, LATENTS),
+            whole(2, WIDE, LATENTS),
         ],
         out_specs=[whole(NUM, WIDE), whole(8, LATENTS), whole(N_CHIPS, ROWS2, WIDE)],
     )
@@ -245,12 +247,12 @@
         grid_spec=grid_spec,
         compiler_params=params(24),
         name="combine",
-    )(place, msg, own_stats, a, b)
+    )(place, msg, own_stats, sums)
 
 
 def query_kernel(
     place_ref, q_ref, dout_ref, stat_ref, ko_ref, kr_ref, vo_ref, vr_ref,
-    a_ref, b_ref, prob_ref,
+    sums_ref, prob_ref,
 ):
     h = pl.program_id(0)
     block = 256
@@ -270,14 +272,14 @@
             prob_ref[0, src, :, rows] = probs
             a = a + dot(k, dscore, 0, 0)
             b = b + dot(k, probs, 0, 0)
-        a_ref[:, rows] = a.astype(BF16)
-        b_ref[:, rows] = b.astype(BF16)
+        sums_ref[0, :, rows] = a.astype(BF16)
+        sums_ref[1, :, rows] = b.astype(BF16)
 
 
 def query_parts(place, queries, dout, stats, keys, keys_in, values, values_in):
     tokens = keys.shape[0]
     head = pl.BlockSpec((tokens, HDIM), lambda h, c: (0, c[0] * HEADS_HERE + h))
-    sums = pl.BlockSpec((HDIM, LATENTS), lambda h, c: (h, 0))
+    sums = pl.BlockSpec((2, HDIM, LATENTS), lambda h, c: (0, h, 0))
     kept = pl.BlockSpec((1, 2, tokens, LATENTS), lambda h, c: (h, 0, 0, 0))
     grid_spec = pltpu.PrefetchScalarGridSpec(
         num_scalar_prefetch=1,
@@ -288,13 +290,12 @@
             whole(8, LATENTS),
             head, head, head, head,
         ],
-        out_specs=[sums, sums, kept],
+        out_specs=[sums, kept],
     )
     return pl.pallas_call(
         query_kernel,
         out_shape=[
-            jax.ShapeDtypeStruct((WIDE, LATENTS), BF16),
-            jax.ShapeDtypeStruct((WIDE, LATENTS), BF16),
+            jax.ShapeDtypeStruct((2, WIDE, LATENTS), BF16),
             jax.ShapeDtypeStruct((HEADS_HERE, 2, tokens, LATENTS), BF16),
         ],
         grid_spec=grid_spec,
@@ -444,12 +445,12 @@
     msg1 = lax.all_to_all(msg1, CHIPS, 0, 0, tiled=True)
     cot_part = dout[:, NUM:]
     cot_other = lax.ppermute(cot_part, "x", [(0, 1), (1, 0), (2, 3), (3, 2)])
-    cot_mine = in_order(odd_x, cot_part, cot_other, 1)
+    sums, probs = query_parts(place, queries, dout, own_stats, *tokens)
+    cot_mine = in_order(odd_x, cot_part, after(cot_other, sums), 1)
     cot_in = swap(cot_mine)
-    a, b, probs = query_parts(place, queries, dout, own_stats, *tokens)
 
     msg1, cot_mine, cot_in = lax.optimization_barrier((msg1, cot_mine, cot_in))
-    att64, stats, msg2 = combine(place, msg1, own_stats, a, b)
+    att64, stats, msg2 = combine(place, msg1, own_stats, sums)
     msg2 = lax.all_to_all(msg2, CHIPS, 0, 0, tiled=True)
 
     att32 = in_order(core, half(att64, core, 0), swap(half(att64, 1 - core, 0)), 1)

time: 132 us -> 131 us (level)
  local copies, waits for them, and re-layouts: 9.28 us -> 7.44 us
    ppermute x1, waiting for transfers between devices: 3.8 us -> 0.01 us  [body(): cot_other = lax.ppermute(cot_part, 'x', [(0, 1), (1, 0), (2, 3), (3, 2)])]
    all_to_all x1, waiting for transfers between devices: 3.78 us -> 6.97 us  [body(): msg1 = lax.all_to_all(msg1, CHIPS, 0, 0, tiled=True)]
    unnamed x27 -> x25, local copies, waits for them, and re-layouts: 4.74 us -> 2.9 us
    ppermute x9, waiting for transfers between devices: 1.65 us -> 3.01 us  [swap(): return lax.ppermute(x, 'core', [(0, 1), (1, 0)])]
where the time goes in v4:
time: 131 us; the launch traced here: 130 us
  Pallas kernels  42.7 us (33%)
  starting transfers between devices  37.5 us (29%)
  waiting for transfers between devices  25.4 us (19%)
  blocking collectives  10.1 us (8%)
  local copies, waits for them, and re-layouts  7.44 us (6%)
  matrix products  3.01 us (2%)
  other arithmetic  2.8 us (2%)
    ppermute x9, starting transfers between devices, swap(): return lax.ppermute(x, 'core', [(0, 1), (1, 0)])  15.6 us
    pallas_call x1, Pallas kernels, query_parts(): pl.pallas_call(query_kernel, out_shape=[jax.ShapeDtypeStruct((2, WIDE, LA...  11.7 us
    pallas_call x1, Pallas kernels, token_grads(): pl.pallas_call(token_kernel, out_shape=[full, half_wide, full, half_wide]...  11.4 us
    all_to_all x1, waiting for transfers between devices, body(): dout = lax.all_to_all(dout, CHIPS, 0, 0, tiled=True)  11.1 us
    all_to_all x1, blocking collectives, gather(): return lax.all_to_all(tiled, axes, 0, 0, tiled=True)  10.1 us
    all_to_all x1, starting transfers between devices, body(): dout = lax.all_to_all(dout, CHIPS, 0, 0, tiled=True)  10 us
    pallas_call x1, Pallas kernels, forward(): pl.pallas_call(forward_kernel, out_shape=[jax.ShapeDtypeStruct((LATENTS,...  9.08 us
    all_to_all x1, waiting for transfers between devices, body(): msg1 = lax.all_to_all(msg1, CHIPS, 0, 0, tiled=True)  6.97 us
  transfers between devices with their start and end apart: 17, of which 8 were waited for; matrix products, arithmetic and copies ran while one was open for 7% of the time, Pallas kernels for 25%

profile of v4, /device:TPU:1, one launch (start us, length us, event | category | flops | bytes accessed | tf_op | source)
XLA Modules:
  0.0 129.9 jit_solution(2435853777916563147)
XLA Ops:
  0.6 3.3 %collective-permute-start = (bf16[1024,512]{1,0:T(8,128)(2,1)}, bf16[1024,512]{1,0:T(8,128)(2,1)S(1)}, u32[]{:S(2)}, u32[]{:S(2)}) collective-permute-start(bf16[1024,512]{1,0:T(8,128)(2,1)} %ko_ref.3), channel_id=1, source_target_pairs={{0,8},{8,0},{1,9},{9,1},{2,10},{10,2},{3,11},{11,3},{4,12},{12,4},... | collective-permute-start | bytes 3145736 | tf_op jit(solution)/shard_map/ppermute | solution.py:401
  4.8 10.1 %all_to_all.20.own_ref = bf16[8,32,512]{2,1,0:T(8,128)(2,1)S(1)} all-to-all(bf16[8,32,512]{2,1,0:T(8,128)(2,1)S(1)} %broadcast_in_dim.2), channel_id=1, replica_groups=mesh['y'=4,'zh'=4,'core'=2,'x'=4,'zl'=2] {'x','zl'}, dimensions={0} | all-to-all | bytes 524288 | tf_op jit(solution)/shard_map/all_to_all | solution.py:419
  15.0 1.6 %collective-permute-start.2 = (bf16[8,32,512]{2,1,0:T(8,128)(2,1)S(1)}, bf16[8,32,512]{2,1,0:T(8,128)(2,1)S(1)}, u32[]{:S(2)}, u32[]{:S(2)}) collective-permute-start(bf16[8,32,512]{2,1,0:T(8,128)(2,1)S(1)} %all_to_all.20.own_ref), channel_id=1, source_target_pairs={{0,8},{8,0},{1,9},{9,1},{2,10},{10,2},{3,11},{11,3},{4,12},{12,4},... | collective-permute-start | bytes 786440 | tf_op jit(solution)/shard_map/ppermute | solution.py:401
  18.5 4.1 %dout.1 = bf16[16,80,256]{2,1,0:T(8,128)(2,1)} custom-call(s32[4]{0:T(128)} %pad_add_fusion.place_ref, bf16[8,32,512]{2,1,0:T(8,128)(2,1)} %copy-done.6, bf16[8,32,512]{2,1,0:T(8,128)(2,1)} %copy-done.7, bf16[512,4096]{1,0:T(8,128)(2,1)} %w_ref.1), custom_call_target="tpu_custom_call" | custom-call | tf_op jit(solution)/shard_map/dout/pallas_call | solution.py:80
  22.5 10.0 %all-to-all-start.1 = ((bf16[16,80,256]{2,1,0:T(8,128)(2,1)}), bf16[16,80,256]{2,1,0:T(8,128)(2,1)S(1)}, u32[]{:S(2)}, u32[]{:S(2)}) async-start(bf16[16,80,256]{2,1,0:T(8,128)(2,1)} %dout.1), calls=%async_computation.1 | async-start | bytes 1310720 | tf_op jit(solution)/shard_map/all_to_all | solution.py:442
  32.6 9.1 %forward.1 = (bf16[1024,256]{1,0:T(8,128)(2,1)}, f32[8,1024]{1,0:T(8,128)}) custom-call(s32[4]{0:T(128)} %pad_add_fusion.place_ref, bf16[1024,512]{1,0:T(8,128)(2,1)} %q_ref.5, bf16[1024,512]{1,0:T(8,128)(2,1)} %ko_ref.3, bf16[1024,512]{1,0:T(8,128)(2,1)} %copy-done.9, bf16[1024,512]{1,0:T(8,128)(2,1)} %vo_ref.5, bf16[1024,512]{1,0:T(8,128)(2,1)} %copy-done.8), custom_call_target="tpu_custom_call" | custom-call | flops 8999999488 | bytes 4000000 | tf_op jit(solution)/shard_map/forward/pallas_call | solution.py:128
  41.7 11.1 %all-to-all-done.1.dout_ref = bf16[16,80,256]{2,1,0:T(8,128)(2,1)S(1)} async-done(((bf16[16,80,256]{2,1,0:T(8,128)(2,1)}), bf16[16,80,256]{2,1,0:T(8,128)(2,1)S(1)}, u32[]{:S(2)}, u32[]{:S(2)}) %all-to-all-start.1) | async-done | bytes 655392 | tf_op jit(solution)/shard_map/all_to_all | solution.py:442
  53.6 2.8 %message.1 = (bf16[16,112,256]{2,1,0:T(8,128)(2,1)}, f32[8,1024]{1,0:T(8,128)}) custom-call(bf16[1024,256]{1,0:T(8,128)(2,1)} %get-tuple-element.34.part_ref, f32[8,1024]{1,0:T(8,128)} %get-tuple-element.35.lse_ref, bf16[16,80,256]{2,1,0:T(8,128)(2,1)} %copy-done.5), custom_call_target="tpu_custom_call" | custom-call | tf_op jit(solution)/shard_map/message/pallas_call | solution.py:166
  56.4 4.3 %all-to-all-start.2 = ((bf16[16,112,256]{2,1,0:T(8,128)(2,1)}), bf16[16,112,256]{2,1,0:T(8,128)(2,1)S(1)}, u32[]{:S(2)}, u32[]{:S(2)}) async-start(bf16[16,112,256]{2,1,0:T(8,128)(2,1)} %get-tuple-element.37), calls=%async_computation.2 | async-start | bytes 1835008 | tf_op jit(solution)/shard_map/all_to_all | solution.py:445
  61.8 11.7 %query.1 = (bf16[2,256,1024]{2,1,0:T(8,128)(2,1)}, bf16[2,2,1024,1024]{3,2,1,0:T(8,128)(2,1)}) custom-call(s32[4]{0:T(128)} %pad_add_fusion.place_ref, bf16[1024,512]{1,0:T(8,128)(2,1)} %q_ref.5, bf16[16,80,256]{2,1,0:T(8,128)(2,1)} %copy-done.5, f32[8,1024]{1,0:T(8,128)} %get-tuple-element.38.stat_ref.own_ref, bf16[1024,512]{1,0:T(8,128)(2,1)} %ko_ref.3, ...), custom_call_target="tpu_custom_call" | custom-call | flops 12000000000 | bytes 20000000 | tf_op jit(solution)/shard_map/query/pallas_call | solution.py:295
  73.6 2.8 %collective-permute-start.4 = (bf16[16,32,256]{2,1,0:T(8,128)(2,1)S(1)}, bf16[16,32,256]{2,1,0:T(8,128)(2,1)S(1)}, u32[]{:S(2)}, u32[]{:S(2)}) collective-permute-start(bf16[16,32,256]{2,1,0:T(8,128)(2,1)S(1)} %maximum_select_fusion.own_ref), channel_id=1, source_target_pairs={{0,8},{8,0},{1,9},{9,1},{2,10},{10,2},{3,11},{11,3},{4,12},{12,4},... | collective-permute-start | bytes 786440 | tf_op jit(solution)/shard_map/ppermute | solution.py:401
  77.5 7.0 %all-to-all-done.2.msg_ref = bf16[16,112,256]{2,1,0:T(8,128)(2,1)S(1)} async-done(((bf16[16,112,256]{2,1,0:T(8,128)(2,1)}), bf16[16,112,256]{2,1,0:T(8,128)(2,1)S(1)}, u32[]{:S(2)}, u32[]{:S(2)}) %all-to-all-start.2) | async-done | bytes 917536 | tf_op jit(solution)/shard_map/all_to_all | solution.py:445
  84.5 1.2 copy-done
  85.7 2.8 %combine.1 = (bf16[64,256]{1,0:T(8,128)(2,1)S(1)}, f32[8,1024]{1,0:T(8,128)S(1)}, bf16[16,128,256]{2,1,0:T(8,128)(2,1)}) custom-call(s32[4]{0:T(128)S(1)} %copy-done.2, bf16[16,112,256]{2,1,0:T(8,128)(2,1)S(1)} %all-to-all-done.2.msg_ref, f32[8,1024]{1,0:T(8,128)S(1)} %copy-done.1, bf16[2,256,1024]{2,1,0:T(8,128)(2,1)S(1)} %copy-done), custom_call_target="tpu_custom_call" | custom-call | tf_op jit(solution)/shard_map/combine/pallas_call | solution.py:240
  88.5 3.7 %collective-permute-start.5 = (bf16[32,256]{1,0:T(8,128)(2,1)S(1)}, bf16[32,256]{1,0:T(8,128)(2,1)S(1)}, u32[]{:S(2)}, u32[]{:S(2)}) collective-permute-start(bf16[32,256]{1,0:T(8,128)(2,1)S(1)} %get-tuple-element.67), channel_id=1, source_target_pairs={{0,8},{8,0},{1,9},{9,1},{2,10},{10,2},{3,11},{11,3},{4,12},{12,4},... | collective-permute-start | bytes 49160 | tf_op jit(solution)/shard_map/ppermute | solution.py:401
  92.2 3.7 %all-to-all-start.3 = ((bf16[16,128,256]{2,1,0:T(8,128)(2,1)}), bf16[16,128,256]{2,1,0:T(8,128)(2,1)S(1)}, u32[]{:S(2)}, u32[]{:S(2)}) async-start(bf16[16,128,256]{2,1,0:T(8,128)(2,1)} %get-tuple-element.51), calls=%async_computation.3 | async-start | bytes 2097152 | tf_op jit(solution)/shard_map/all_to_all | solution.py:454
  95.9 3.0 %fusion.4 = f32[32,4096]{1,0:T(8,128)S(1)} fusion(bf16[512,4096]{1,0:T(8,128)(2,1)} %w_ref.1, bf16[32,256]{1,0:T(8,128)(2,1)S(1)} %collective-permute-done.5, bf16[32,256]{1,0:T(8,128)(2,1)S(1)} %get-tuple-element.66, pred[]{:T(512)S(6)} %eq.8), kind=kOutput, calls=%fused_computation.15 | convolution fusion | flops 134365184 | bytes 4751361 | tf_op jit(solution)/shard_map/dot_general | solution.py:31
  100.0 1.6 %collective-permute-start.7 = (bf16[32,1024]{1,0:T(8,128)(2,1)S(1)}, bf16[32,1024]{1,0:T(8,128)(2,1)S(1)}, u32[]{:S(2)}, u32[]{:S(2)}) collective-permute-start(bf16[32,1024]{1,0:T(8,128)(2,1)S(1)} %bitcast.26), channel_id=1, source_target_pairs={{0,4},{2,6},{4,0},{6,2},{1,5},{3,7},{5,1},{7,3},{8,12},{10,14},{12... | collective-permute-start | bytes 196616 | tf_op jit(solution)/shard_map/ppermute | solution.py:423
  101.6 2.1 %collective-permute-start.8 = (bf16[32,1024]{1,0:T(8,128)(2,1)S(1)}, bf16[32,1024]{1,0:T(8,128)(2,1)S(1)}, u32[]{:S(2)}, u32[]{:S(2)}) collective-permute-start(bf16[32,1024]{1,0:T(8,128)(2,1)S(1)} %bitcast.27), channel_id=1, source_target_pairs={{0,6},{2,0},{4,2},{6,4},{1,7},{3,1},{5,3},{7,5},{8,14},{10,8},{12,... | collective-permute-start | bytes 196616 | tf_op jit(solution)/shard_map/ppermute | solution.py:423
  103.7 11.4 %token_.1 = (bf16[1024,512]{1,0:T(8,128)(2,1)}, bf16[1024,256]{1,0:T(8,128)(2,1)}, bf16[1024,512]{1,0:T(8,128)(2,1)}, bf16[1024,256]{1,0:T(8,128)(2,1)}) custom-call(s32[4]{0:T(128)} %pad_add_fusion.place_ref, bf16[1024,512]{1,0:T(8,128)(2,1)} %q_ref.5, bf16[16,80,256]{2,1,0:T(8,128)(2,1)} %copy-done.5, f32[8,1024]{1,0:T(8,128)} %get-tuple-element.38.stat_ref.own_ref, ...), custom_call_target="tpu_custom_call" | custom-call | flops 8000000000 | bytes 14000000 | tf_op jit(solution)/shard_map/token/pallas_call | solution.py:358
  115.1 1.5 %collective-permute-start.10 = (bf16[1024,256]{1,0:T(8,128)(2,1)}, bf16[1024,256]{1,0:T(8,128)(2,1)S(1)}, u32[]{:S(2)}, u32[]{:S(2)}) collective-permute-start(bf16[1024,256]{1,0:T(8,128)(2,1)} %get-tuple-element.52), channel_id=1, source_target_pairs={{0,8},{8,0},{1,9},{9,1},{2,10},{10,2},{3,11},{11,3},{4,12},{12,4},... | collective-permute-start | bytes 1572872 | tf_op jit(solution)/shard_map/ppermute | solution.py:401
  117.1 1.2 collective-permute-done.10
  120.5 3.8 %all-to-all-done.3.att_ref = bf16[16,128,256]{2,1,0:T(8,128)(2,1)S(1)} async-done(((bf16[16,128,256]{2,1,0:T(8,128)(2,1)}), bf16[16,128,256]{2,1,0:T(8,128)(2,1)S(1)}, u32[]{:S(2)}, u32[]{:S(2)}) %all-to-all-start.3) | async-done | bytes 1048608 | tf_op jit(solution)/shard_map/all_to_all | solution.py:454
  124.5 2.3 %collective-permute-start.12 = (bf16[32,256]{1,0:T(8,128)(2,1)S(1)}, bf16[32,256]{1,0:T(8,128)(2,1)S(1)}, u32[]{:S(2)}, u32[]{:S(2)}) collective-permute-start(bf16[32,256]{1,0:T(8,128)(2,1)S(1)} %get-tuple-element.65), channel_id=1, source_target_pairs={{0,8},{8,0},{1,9},{9,1},{2,10},{10,2},{3,11},{11,3},{4,12},{12,4},... | collective-permute-start | bytes 49160 | tf_op jit(solution)/shard_map/ppermute | solution.py:401
  (64 shorter events, 12.8 us)
Async XLA Ops:
  0.6 14.3 %collective-permute-start = (bf16[1024,512]{1,0:T(8,128)(2,1)}, bf16[1024,512]{1,0:T(8,128)(2,1)S(1)}, u32[]{:S(2)}, u32[]{:S(2)}) collective-permute-start(bf16[1024,512]{1,0:T(8,128)(2,1)} %ko_ref.3), channel_id=1, source_target_pairs={{0,8},{8,0},{1,9},{9,1},{2,10},{10,2},{3,11},{11,3},{4,12},{12,4},... | collective-permute-start | bytes 3145736 | tf_op jit(solution)/shard_map/ppermute | solution.py:401
  4.0 11.0 %collective-permute-start.1 = (bf16[1024,512]{1,0:T(8,128)(2,1)}, bf16[1024,512]{1,0:T(8,128)(2,1)S(1)}, u32[]{:S(2)}, u32[]{:S(2)}) collective-permute-start(bf16[1024,512]{1,0:T(8,128)(2,1)} %vo_ref.5), channel_id=1, source_target_pairs={{0,8},{8,0},{1,9},{9,1},{2,10},{10,2},{3,11},{11,3},{4,12},{12,4},... | collective-permute-start | bytes 3145736 | tf_op jit(solution)/shard_map/ppermute | solution.py:401
  14.9 2.8 %copy-start.6 = (bf16[8,32,512]{2,1,0:T(8,128)(2,1)}, bf16[8,32,512]{2,1,0:T(8,128)(2,1)S(1)}, u32[]{:S(2)}) copy-start(bf16[8,32,512]{2,1,0:T(8,128)(2,1)S(1)} %all_to_all.20.own_ref) | copy-start | bytes 786436
  14.9 17.6 %copy-start.9 = (bf16[1024,512]{1,0:T(8,128)(2,1)}, bf16[1024,512]{1,0:T(8,128)(2,1)S(1)}, u32[]{:S(2)}) copy-start(bf16[1024,512]{1,0:T(8,128)(2,1)S(1)} %collective-permute-done.kr_ref) | copy-start | bytes 3145732
  15.0 17.6 %copy-start.8 = (bf16[1024,512]{1,0:T(8,128)(2,1)}, bf16[1024,512]{1,0:T(8,128)(2,1)S(1)}, u32[]{:S(2)}) copy-start(bf16[1024,512]{1,0:T(8,128)(2,1)S(1)} %collective-permute-done.1.vr_ref) | copy-start | bytes 3145732
  15.0 2.8 %collective-permute-start.2 = (bf16[8,32,512]{2,1,0:T(8,128)(2,1)S(1)}, bf16[8,32,512]{2,1,0:T(8,128)(2,1)S(1)}, u32[]{:S(2)}, u32[]{:S(2)}) collective-permute-start(bf16[8,32,512]{2,1,0:T(8,128)(2,1)S(1)} %all_to_all.20.own_ref), channel_id=1, source_target_pairs={{0,8},{8,0},{1,9},{9,1},{2,10},{10,2},{3,11},{11,3},{4,12},{12,4},... | collective-permute-start | bytes 786440 | tf_op jit(solution)/shard_map/ppermute | solution.py:401
  22.5 30.2 %all-to-all-start.1 = ((bf16[16,80,256]{2,1,0:T(8,128)(2,1)}), bf16[16,80,256]{2,1,0:T(8,128)(2,1)S(1)}, u32[]{:S(2)}, u32[]{:S(2)}) async-start(bf16[16,80,256]{2,1,0:T(8,128)(2,1)} %dout.1), calls=%async_computation.1 | async-start | bytes 1310720 | tf_op jit(solution)/shard_map/all_to_all | solution.py:442
  56.4 28.1 %all-to-all-start.2 = ((bf16[16,112,256]{2,1,0:T(8,128)(2,1)}), bf16[16,112,256]{2,1,0:T(8,128)(2,1)S(1)}, u32[]{:S(2)}, u32[]{:S(2)}) async-start(bf16[16,112,256]{2,1,0:T(8,128)(2,1)} %get-tuple-element.37), calls=%async_computation.2 | async-start | bytes 1835008 | tf_op jit(solution)/shard_map/all_to_all | solution.py:445
  61.6 11.8 %collective-permute-start.3 = (bf16[16,16,256]{2,1,0:T(8,128)(2,1)S(1)}, bf16[16,16,256]{2,1,0:T(8,128)(2,1)S(1)}, u32[]{:S(2)}, u32[]{:S(2)}) collective-permute-start(bf16[16,16,256]{2,1,0:T(8,128)(2,1)S(1)} %slice.8), channel_id=1, source_target_pairs={{0,2},{2,0},{4,6},{6,4},{1,3},{3,1},{5,7},{7,5},{8,10},{10,8},{12,... | collective-permute-start | bytes 393224 | tf_op jit(solution)/shard_map/ppermute | solution.py:447
  61.7 22.7 %copy-start.1 = (f32[8,1024]{1,0:T(8,128)S(1)}, f32[8,1024]{1,0:T(8,128)}, u32[]{:S(2)}) copy-start(f32[8,1024]{1,0:T(8,128)} %get-tuple-element.38.stat_ref.own_ref) | copy-start | bytes 98308
  61.8 22.7 %copy-start.2 = (s32[4]{0:T(128)S(1)}, s32[4]{0:T(128)}, u32[]{:S(2)}) copy-start(s32[4]{0:T(128)} %pad_add_fusion.place_ref) | copy-start | bytes 52
  73.6 3.9 %collective-permute-start.4 = (bf16[16,32,256]{2,1,0:T(8,128)(2,1)S(1)}, bf16[16,32,256]{2,1,0:T(8,128)(2,1)S(1)}, u32[]{:S(2)}, u32[]{:S(2)}) collective-permute-start(bf16[16,32,256]{2,1,0:T(8,128)(2,1)S(1)} %maximum_select_fusion.own_ref), channel_id=1, source_target_pairs={{0,8},{8,0},{1,9},{9,1},{2,10},{10,2},{3,11},{11,3},{4,12},{12,4},... | collective-permute-start | bytes 786440 | tf_op jit(solution)/shard_map/ppermute | solution.py:401
  88.5 3.7 %copy-start.4 = (f32[8,1024]{1,0:T(8,128)}, f32[8,1024]{1,0:T(8,128)S(1)}, u32[]{:S(2)}) copy-start(f32[8,1024]{1,0:T(8,128)S(1)} %get-tuple-element.44.stat_ref) | copy-start | bytes 98308
  88.5 7.3 %collective-permute-start.5 = (bf16[32,256]{1,0:T(8,128)(2,1)S(1)}, bf16[32,256]{1,0:T(8,128)(2,1)S(1)}, u32[]{:S(2)}, u32[]{:S(2)}) collective-permute-start(bf16[32,256]{1,0:T(8,128)(2,1)S(1)} %get-tuple-element.67), channel_id=1, source_target_pairs={{0,8},{8,0},{1,9},{9,1},{2,10},{10,2},{3,11},{11,3},{4,12},{12,4},... | collective-permute-start | bytes 49160 | tf_op jit(solution)/shard_map/ppermute | solution.py:401
  92.2 32.2 %all-to-all-start.3 = ((bf16[16,128,256]{2,1,0:T(8,128)(2,1)}), bf16[16,128,256]{2,1,0:T(8,128)(2,1)S(1)}, u32[]{:S(2)}, u32[]{:S(2)}) async-start(bf16[16,128,256]{2,1,0:T(8,128)(2,1)} %get-tuple-element.51), calls=%async_computation.3 | async-start | bytes 2097152 | tf_op jit(solution)/shard_map/all_to_all | solution.py:454
  99.9 16.8 %collective-permute-start.6 = (bf16[32,1024]{1,0:T(8,128)(2,1)S(1)}, bf16[32,1024]{1,0:T(8,128)(2,1)S(1)}, u32[]{:S(2)}, u32[]{:S(2)}) collective-permute-start(bf16[32,1024]{1,0:T(8,128)(2,1)S(1)} %bitcast.25), channel_id=1, source_target_pairs={{0,2},{2,4},{4,6},{6,0},{1,3},{3,5},{5,7},{7,1},{8,10},{10,12},{12... | collective-permute-start | bytes 196616 | tf_op jit(solution)/shard_map/ppermute | solution.py:423
  100.0 16.7 %collective-permute-start.7 = (bf16[32,1024]{1,0:T(8,128)(2,1)S(1)}, bf16[32,1024]{1,0:T(8,128)(2,1)S(1)}, u32[]{:S(2)}, u32[]{:S(2)}) collective-permute-start(bf16[32,1024]{1,0:T(8,128)(2,1)S(1)} %bitcast.26), channel_id=1, source_target_pairs={{0,4},{2,6},{4,0},{6,2},{1,5},{3,7},{5,1},{7,3},{8,12},{10,14},{12... | collective-permute-start | bytes 196616 | tf_op jit(solution)/shard_map/ppermute | solution.py:423
  101.6 15.1 %collective-permute-start.8 = (bf16[32,1024]{1,0:T(8,128)(2,1)S(1)}, bf16[32,1024]{1,0:T(8,128)(2,1)S(1)}, u32[]{:S(2)}, u32[]{:S(2)}) collective-permute-start(bf16[32,1024]{1,0:T(8,128)(2,1)S(1)} %bitcast.27), channel_id=1, source_target_pairs={{0,6},{2,0},{4,2},{6,4},{1,7},{3,1},{5,3},{7,5},{8,14},{10,8},{12,... | collective-permute-start | bytes 196616 | tf_op jit(solution)/shard_map/ppermute | solution.py:423
  103.7 23.1 %copy-start.3 = (s32[4]{0:T(128)S(1)}, s32[4]{0:T(128)}, u32[]{:S(2)}) copy-start(s32[4]{0:T(128)} %pad_add_fusion.place_ref) | copy-start | bytes 52
  115.1 3.3 %collective-permute-start.10 = (bf16[1024,256]{1,0:T(8,128)(2,1)}, bf16[1024,256]{1,0:T(8,128)(2,1)S(1)}, u32[]{:S(2)}, u32[]{:S(2)}) collective-permute-start(bf16[1024,256]{1,0:T(8,128)(2,1)} %get-tuple-element.52), channel_id=1, source_target_pairs={{0,8},{8,0},{1,9},{9,1},{2,10},{10,2},{3,11},{11,3},{4,12},{12,4},... | collective-permute-start | bytes 1572872 | tf_op jit(solution)/shard_map/ppermute | solution.py:401
  116.6 2.6 %collective-permute-start.11 = (bf16[1024,256]{1,0:T(8,128)(2,1)}, bf16[1024,256]{1,0:T(8,128)(2,1)S(1)}, u32[]{:S(2)}, u32[]{:S(2)}) collective-permute-start(bf16[1024,256]{1,0:T(8,128)(2,1)} %get-tuple-element.54), channel_id=1, source_target_pairs={{0,8},{8,0},{1,9},{9,1},{2,10},{10,2},{3,11},{11,3},{4,12},{12,4},... | collective-permute-start | bytes 1572872 | tf_op jit(solution)/shard_map/ppermute | solution.py:401
  117.0 3.6 %collective-permute-start.9 = (bf16[32,512]{1,0:T(8,128)(2,1)S(1)}, bf16[32,512]{1,0:T(8,128)(2,1)S(1)}, u32[]{:S(2)}, u32[]{:S(2)}) collective-permute-start(bf16[32,512]{1,0:T(8,128)(2,1)S(1)} %bitcast.28), channel_id=1, source_target_pairs={{0,1},{1,0},{2,3},{3,2},{4,5},{5,4},{6,7},{7,6},{8,9},{9,8},{10,11... | collective-permute-start | bytes 98312 | tf_op jit(solution)/shard_map/ppermute | solution.py:469
  124.5 4.0 %collective-permute-start.12 = (bf16[32,256]{1,0:T(8,128)(2,1)S(1)}, bf16[32,256]{1,0:T(8,128)(2,1)S(1)}, u32[]{:S(2)}, u32[]{:S(2)}) collective-permute-start(bf16[32,256]{1,0:T(8,128)(2,1)S(1)} %get-tuple-element.65), channel_id=1, source_target_pairs={{0,8},{8,0},{1,9},{9,1},{2,10},{10,2},{3,11},{11,3},{4,12},{12,4},... | collective-permute-start | bytes 49160 | tf_op jit(solution)/shard_map/ppermute | solution.py:401
  127.8 1.4 %collective-permute-start.13 = (f32[256,128]{1,0:T(8,128)S(1)}, f32[256,128]{1,0:T(8,128)S(1)}, u32[]{:S(2)}, u32[]{:S(2)}) collective-permute-start(f32[256,128]{1,0:T(8,128)S(1)} %get-tuple-element.63), channel_id=1, source_target_pairs={{0,8},{8,0},{1,9},{9,1},{2,10},{10,2},{3,11},{11,3},{4,12},{12,4},... | collective-permute-start | bytes 393224 | tf_op jit(solution)/shard_map/ppermute | solution.py:401
  (3 other events, 2.8 us)

commit v5 on v4

--- a/solution.py
+++ b/solution.py
@@ -476,8 +476,9 @@
     key_grad = lax.dynamic_update_slice(dk, swap(dk_out), other_cols)
     value_grad = lax.dynamic_update_slice(dv, swap(dv_out), other_cols)
 
-    msg2, from_zl = lax.optimization_barrier((msg2, from_zl, key_grad, value_grad))[:2]
+    from_zl = after(from_zl, key_grad, value_grad)
     latent_out = (own_zl + from_zl.astype(F32)).astype(BF16)
+    msg2 = after(msg2, latent_out)
     dq64 = jnp.sum(msg2[:, :NUM].astype(F32), axis=0).astype(BF16)
     dq_in = swap(half(dq64, 1 - core, 0))
     query_grad = in_order(core, half(dq64, core, 0), dq_in, 1)

time: 131 us -> 131 us (level)
  no operation moved by 1% of the time
where the time goes in v5:
time: 131 us; the launch traced here: 130 us
  Pallas kernels  42.7 us (33%)
  starting transfers between devices  37.5 us (29%)
  waiting for transfers between devices  25.8 us (20%)
  blocking collectives  10.1 us (8%)
  local copies, waits for them, and re-layouts  7.43 us (6%)
  matrix products  3.01 us (2%)
  other arithmetic  2.8 us (2%)
    ppermute x9, starting transfers between devices, swap(): return lax.ppermute(x, 'core', [(0, 1), (1, 0)])  15.6 us
    pallas_call x1, Pallas kernels, query_parts(): pl.pallas_call(query_kernel, out_shape=[jax.ShapeDtypeStruct((2, WIDE, LA...  11.7 us
    pallas_call x1, Pallas kernels, token_grads(): pl.pallas_call(token_kernel, out_shape=[full, half_wide, full, half_wide]...  11.4 us
    all_to_all x1, waiting for transfers between devices, body(): dout = lax.all_to_all(dout, CHIPS, 0, 0, tiled=True)  11.1 us
    all_to_all x1, blocking collectives, gather(): return lax.all_to_all(tiled, axes, 0, 0, tiled=True)  10.1 us
    all_to_all x1, starting transfers between devices, body(): dout = lax.all_to_all(dout, CHIPS, 0, 0, tiled=True)  10 us
    pallas_call x1, Pallas kernels, forward(): pl.pallas_call(forward_kernel, out_shape=[jax.ShapeDtypeStruct((LATENTS,...  9.08 us
    all_to_all x1, waiting for transfers between devices, body(): msg1 = lax.all_to_all(msg1, CHIPS, 0, 0, tiled=True)  6.97 us
  transfers between devices with their start and end apart: 17, of which 8 were waited for; matrix products, arithmetic and copies ran while one was open for 7% of the time, Pallas kernels for 25%

profile of v5, /device:TPU:1, one launch (start us, length us, event | category | flops | bytes accessed | tf_op | source)
XLA Modules:
  0.0 130.3 jit_solution(9439078537693873348)
XLA Ops:
  0.6 3.3 %collective-permute-start = (bf16[1024,512]{1,0:T(8,128)(2,1)}, bf16[1024,512]{1,0:T(8,128)(2,1)S(1)}, u32[]{:S(2)}, u32[]{:S(2)}) collective-permute-start(bf16[1024,512]{1,0:T(8,128)(2,1)} %ko_ref.3), channel_id=1, source_target_pairs={{0,8},{8,0},{1,9},{9,1},{2,10},{10,2},{3,11},{11,3},{4,12},{12,4},... | collective-permute-start | bytes 3145736 | tf_op jit(solution)/shard_map/ppermute | solution.py:401
  4.8 10.1 %all_to_all.20.own_ref = bf16[8,32,512]{2,1,0:T(8,128)(2,1)S(1)} all-to-all(bf16[8,32,512]{2,1,0:T(8,128)(2,1)S(1)} %broadcast_in_dim.2), channel_id=1, replica_groups=mesh['y'=4,'zh'=4,'core'=2,'x'=4,'zl'=2] {'x','zl'}, dimensions={0} | all-to-all | bytes 524288 | tf_op jit(solution)/shard_map/all_to_all | solution.py:419
  15.0 1.6 %collective-permute-start.2 = (bf16[8,32,512]{2,1,0:T(8,128)(2,1)S(1)}, bf16[8,32,512]{2,1,0:T(8,128)(2,1)S(1)}, u32[]{:S(2)}, u32[]{:S(2)}) collective-permute-start(bf16[8,32,512]{2,1,0:T(8,128)(2,1)S(1)} %all_to_all.20.own_ref), channel_id=1, source_target_pairs={{0,8},{8,0},{1,9},{9,1},{2,10},{10,2},{3,11},{11,3},{4,12},{12,4},... | collective-permute-start | bytes 786440 | tf_op jit(solution)/shard_map/ppermute | solution.py:401
  18.5 4.1 %dout.1 = bf16[16,80,256]{2,1,0:T(8,128)(2,1)} custom-call(s32[4]{0:T(128)} %pad_add_fusion.place_ref, bf16[8,32,512]{2,1,0:T(8,128)(2,1)} %copy-done.6, bf16[8,32,512]{2,1,0:T(8,128)(2,1)} %copy-done.7, bf16[512,4096]{1,0:T(8,128)(2,1)} %w_ref.1), custom_call_target="tpu_custom_call" | custom-call | tf_op jit(solution)/shard_map/dout/pallas_call | solution.py:80
  22.5 10.0 %all-to-all-start.1 = ((bf16[16,80,256]{2,1,0:T(8,128)(2,1)}), bf16[16,80,256]{2,1,0:T(8,128)(2,1)S(1)}, u32[]{:S(2)}, u32[]{:S(2)}) async-start(bf16[16,80,256]{2,1,0:T(8,128)(2,1)} %dout.1), calls=%async_computation.1 | async-start | bytes 1310720 | tf_op jit(solution)/shard_map/all_to_all | solution.py:442
  32.6 9.1 %forward.1 = (bf16[1024,256]{1,0:T(8,128)(2,1)}, f32[8,1024]{1,0:T(8,128)}) custom-call(s32[4]{0:T(128)} %pad_add_fusion.place_ref, bf16[1024,512]{1,0:T(8,128)(2,1)} %q_ref.5, bf16[1024,512]{1,0:T(8,128)(2,1)} %ko_ref.3, bf16[1024,512]{1,0:T(8,128)(2,1)} %copy-done.9, bf16[1024,512]{1,0:T(8,128)(2,1)} %vo_ref.5, bf16[1024,512]{1,0:T(8,128)(2,1)} %copy-done.8), custom_call_target="tpu_custom_call" | custom-call | flops 8999999488 | bytes 4000000 | tf_op jit(solution)/shard_map/forward/pallas_call | solution.py:128
  41.7 11.1 %all-to-all-done.1.dout_ref = bf16[16,80,256]{2,1,0:T(8,128)(2,1)S(1)} async-done(((bf16[16,80,256]{2,1,0:T(8,128)(2,1)}), bf16[16,80,256]{2,1,0:T(8,128)(2,1)S(1)}, u32[]{:S(2)}, u32[]{:S(2)}) %all-to-all-start.1) | async-done | bytes 655392 | tf_op jit(solution)/shard_map/all_to_all | solution.py:442
  53.6 2.8 %message.1 = (bf16[16,112,256]{2,1,0:T(8,128)(2,1)}, f32[8,1024]{1,0:T(8,128)}) custom-call(bf16[1024,256]{1,0:T(8,128)(2,1)} %get-tuple-element.34.part_ref, f32[8,1024]{1,0:T(8,128)} %get-tuple-element.35.lse_ref, bf16[16,80,256]{2,1,0:T(8,128)(2,1)} %copy-done.5), custom_call_target="tpu_custom_call" | custom-call | tf_op jit(solution)/shard_map/message/pallas_call | solution.py:166
  56.4 4.3 %all-to-all-start.2 = ((bf16[16,112,256]{2,1,0:T(8,128)(2,1)}), bf16[16,112,256]{2,1,0:T(8,128)(2,1)S(1)}, u32[]{:S(2)}, u32[]{:S(2)}) async-start(bf16[16,112,256]{2,1,0:T(8,128)(2,1)} %get-tuple-element.37), calls=%async_computation.2 | async-start | bytes 1835008 | tf_op jit(solution)/shard_map/all_to_all | solution.py:445
  61.8 11.7 %query.1 = (bf16[2,256,1024]{2,1,0:T(8,128)(2,1)}, bf16[2,2,1024,1024]{3,2,1,0:T(8,128)(2,1)}) custom-call(s32[4]{0:T(128)} %pad_add_fusion.place_ref, bf16[1024,512]{1,0:T(8,128)(2,1)} %q_ref.5, bf16[16,80,256]{2,1,0:T(8,128)(2,1)} %copy-done.5, f32[8,1024]{1,0:T(8,128)} %get-tuple-element.38.stat_ref.own_ref, bf16[1024,512]{1,0:T(8,128)(2,1)} %ko_ref.3, ...), custom_call_target="tpu_custom_call" | custom-call | flops 12000000000 | bytes 20000000 | tf_op jit(solution)/shard_map/query/pallas_call | solution.py:295
  73.6 2.8 %collective-permute-start.4 = (bf16[16,32,256]{2,1,0:T(8,128)(2,1)S(1)}, bf16[16,32,256]{2,1,0:T(8,128)(2,1)S(1)}, u32[]{:S(2)}, u32[]{:S(2)}) collective-permute-start(bf16[16,32,256]{2,1,0:T(8,128)(2,1)S(1)} %maximum_select_fusion.own_ref), channel_id=1, source_target_pairs={{0,8},{8,0},{1,9},{9,1},{2,10},{10,2},{3,11},{11,3},{4,12},{12,4},... | collective-permute-start | bytes 786440 | tf_op jit(solution)/shard_map/ppermute | solution.py:401
  77.5 7.0 %all-to-all-done.2.msg_ref = bf16[16,112,256]{2,1,0:T(8,128)(2,1)S(1)} async-done(((bf16[16,112,256]{2,1,0:T(8,128)(2,1)}), bf16[16,112,256]{2,1,0:T(8,128)(2,1)S(1)}, u32[]{:S(2)}, u32[]{:S(2)}) %all-to-all-start.2) | async-done | bytes 917536 | tf_op jit(solution)/shard_map/all_to_all | solution.py:445
  84.5 1.2 copy-done
  85.7 2.8 %combine.1 = (bf16[64,256]{1,0:T(8,128)(2,1)S(1)}, f32[8,1024]{1,0:T(8,128)S(1)}, bf16[16,128,256]{2,1,0:T(8,128)(2,1)}) custom-call(s32[4]{0:T(128)S(1)} %copy-done.2, bf16[16,112,256]{2,1,0:T(8,128)(2,1)S(1)} %all-to-all-done.2.msg_ref, f32[8,1024]{1,0:T(8,128)S(1)} %copy-done.1, bf16[2,256,1024]{2,1,0:T(8,128)(2,1)S(1)} %copy-done), custom_call_target="tpu_custom_call" | custom-call | tf_op jit(solution)/shard_map/combine/pallas_call | solution.py:240
  88.5 3.7 %collective-permute-start.5 = (bf16[32,256]{1,0:T(8,128)(2,1)S(1)}, bf16[32,256]{1,0:T(8,128)(2,1)S(1)}, u32[]{:S(2)}, u32[]{:S(2)}) collective-permute-start(bf16[32,256]{1,0:T(8,128)(2,1)S(1)} %get-tuple-element.67), channel_id=1, source_target_pairs={{0,8},{8,0},{1,9},{9,1},{2,10},{10,2},{3,11},{11,3},{4,12},{12,4},... | collective-permute-start | bytes 49160 | tf_op jit(solution)/shard_map/ppermute | solution.py:401
  92.2 3.7 %all-to-all-start.3 = ((bf16[16,128,256]{2,1,0:T(8,128)(2,1)}), bf16[16,128,256]{2,1,0:T(8,128)(2,1)S(1)}, u32[]{:S(2)}, u32[]{:S(2)}) async-start(bf16[16,128,256]{2,1,0:T(8,128)(2,1)} %get-tuple-element.55), calls=%async_computation.3 | async-start | bytes 2097152 | tf_op jit(solution)/shard_map/all_to_all | solution.py:454
  95.9 3.0 %fusion.4 = f32[32,4096]{1,0:T(8,128)S(1)} fusion(bf16[512,4096]{1,0:T(8,128)(2,1)} %w_ref.1, bf16[32,256]{1,0:T(8,128)(2,1)S(1)} %collective-permute-done.5, bf16[32,256]{1,0:T(8,128)(2,1)S(1)} %get-tuple-element.66, pred[]{:T(512)S(6)} %eq.8), kind=kOutput, calls=%fused_computation.15 | convolution fusion | flops 134365184 | bytes 4751361 | tf_op jit(solution)/shard_map/dot_general | solution.py:31
  100.0 1.6 %collective-permute-start.7 = (bf16[32,1024]{1,0:T(8,128)(2,1)S(1)}, bf16[32,1024]{1,0:T(8,128)(2,1)S(1)}, u32[]{:S(2)}, u32[]{:S(2)}) collective-permute-start(bf16[32,1024]{1,0:T(8,128)(2,1)S(1)} %bitcast.26), channel_id=1, source_target_pairs={{0,4},{2,6},{4,0},{6,2},{1,5},{3,7},{5,1},{7,3},{8,12},{10,14},{12... | collective-permute-start | bytes 196616 | tf_op jit(solution)/shard_map/ppermute | solution.py:423
  101.6 2.1 %collective-permute-start.8 = (bf16[32,1024]{1,0:T(8,128)(2,1)S(1)}, bf16[32,1024]{1,0:T(8,128)(2,1)S(1)}, u32[]{:S(2)}, u32[]{:S(2)}) collective-permute-start(bf16[32,1024]{1,0:T(8,128)(2,1)S(1)} %bitcast.27), channel_id=1, source_target_pairs={{0,6},{2,0},{4,2},{6,4},{1,7},{3,1},{5,3},{7,5},{8,14},{10,8},{12,... | collective-permute-start | bytes 196616 | tf_op jit(solution)/shard_map/ppermute | solution.py:423
  103.7 11.4 %token_.1 = (bf16[1024,512]{1,0:T(8,128)(2,1)}, bf16[1024,256]{1,0:T(8,128)(2,1)}, bf16[1024,512]{1,0:T(8,128)(2,1)}, bf16[1024,256]{1,0:T(8,128)(2,1)}) custom-call(s32[4]{0:T(128)} %pad_add_fusion.place_ref, bf16[1024,512]{1,0:T(8,128)(2,1)} %q_ref.5, bf16[16,80,256]{2,1,0:T(8,128)(2,1)} %copy-done.5, f32[8,1024]{1,0:T(8,128)} %get-tuple-element.38.stat_ref.own_ref, ...), custom_call_target="tpu_custom_call" | custom-call | flops 8000000000 | bytes 14000000 | tf_op jit(solution)/shard_map/token/pallas_call | solution.py:358
  115.1 1.5 %collective-permute-start.10 = (bf16[1024,256]{1,0:T(8,128)(2,1)}, bf16[1024,256]{1,0:T(8,128)(2,1)S(1)}, u32[]{:S(2)}, u32[]{:S(2)}) collective-permute-start(bf16[1024,256]{1,0:T(8,128)(2,1)} %get-tuple-element.51), channel_id=1, source_target_pairs={{0,8},{8,0},{1,9},{9,1},{2,10},{10,2},{3,11},{11,3},{4,12},{12,4},... | collective-permute-start | bytes 1572872 | tf_op jit(solution)/shard_map/ppermute | solution.py:401
  117.1 1.2 collective-permute-done.10
  121.2 3.2 %all-to-all-done.3.att_ref = bf16[16,128,256]{2,1,0:T(8,128)(2,1)S(1)} async-done(((bf16[16,128,256]{2,1,0:T(8,128)(2,1)}), bf16[16,128,256]{2,1,0:T(8,128)(2,1)S(1)}, u32[]{:S(2)}, u32[]{:S(2)}) %all-to-all-start.3) | async-done | bytes 1048608 | tf_op jit(solution)/shard_map/all_to_all | solution.py:454
  125.4 2.3 %collective-permute-start.13 = (f32[256,128]{1,0:T(8,128)S(1)}, f32[256,128]{1,0:T(8,128)S(1)}, u32[]{:S(2)}, u32[]{:S(2)}) collective-permute-start(f32[256,128]{1,0:T(8,128)S(1)} %get-tuple-element.63), channel_id=1, source_target_pairs={{0,8},{8,0},{1,9},{9,1},{2,10},{10,2},{3,11},{11,3},{4,12},{12,4},... | collective-permute-start | bytes 393224 | tf_op jit(solution)/shard_map/ppermute | solution.py:401
  (64 shorter events, 13.8 us)
Async XLA Ops:
  0.6 14.3 %collective-permute-start = (bf16[1024,512]{1,0:T(8,128)(2,1)}, bf16[1024,512]{1,0:T(8,128)(2,1)S(1)}, u32[]{:S(2)}, u32[]{:S(2)}) collective-permute-start(bf16[1024,512]{1,0:T(8,128)(2,1)} %ko_ref.3), channel_id=1, source_target_pairs={{0,8},{8,0},{1,9},{9,1},{2,10},{10,2},{3,11},{11,3},{4,12},{12,4},... | collective-permute-start | bytes 3145736 | tf_op jit(solution)/shard_map/ppermute | solution.py:401
  4.0 11.0 %collective-permute-start.1 = (bf16[1024,512]{1,0:T(8,128)(2,1)}, bf16[1024,512]{1,0:T(8,128)(2,1)S(1)}, u32[]{:S(2)}, u32[]{:S(2)}) collective-permute-start(bf16[1024,512]{1,0:T(8,128)(2,1)} %vo_ref.5), channel_id=1, source_target_pairs={{0,8},{8,0},{1,9},{9,1},{2,10},{10,2},{3,11},{11,3},{4,12},{12,4},... | collective-permute-start | bytes 3145736 | tf_op jit(solution)/shard_map/ppermute | solution.py:401
  14.9 2.8 %copy-start.6 = (bf16[8,32,512]{2,1,0:T(8,128)(2,1)}, bf16[8,32,512]{2,1,0:T(8,128)(2,1)S(1)}, u32[]{:S(2)}) copy-start(bf16[8,32,512]{2,1,0:T(8,128)(2,1)S(1)} %all_to_all.20.own_ref) | copy-start | bytes 786436
  14.9 17.6 %copy-start.9 = (bf16[1024,512]{1,0:T(8,128)(2,1)}, bf16[1024,512]{1,0:T(8,128)(2,1)S(1)}, u32[]{:S(2)}) copy-start(bf16[1024,512]{1,0:T(8,128)(2,1)S(1)} %collective-permute-done.kr_ref) | copy-start | bytes 3145732
  15.0 17.6 %copy-start.8 = (bf16[1024,512]{1,0:T(8,128)(2,1)}, bf16[1024,512]{1,0:T(8,128)(2,1)S(1)}, u32[]{:S(2)}) copy-start(bf16[1024,512]{1,0:T(8,128)(2,1)S(1)} %collective-permute-done.1.vr_ref) | copy-start | bytes 3145732
  15.0 2.8 %collective-permute-start.2 = (bf16[8,32,512]{2,1,0:T(8,128)(2,1)S(1)}, bf16[8,32,512]{2,1,0:T(8,128)(2,1)S(1)}, u32[]{:S(2)}, u32[]{:S(2)}) collective-permute-start(bf16[8,32,512]{2,1,0:T(8,128)(2,1)S(1)} %all_to_all.20.own_ref), channel_id=1, source_target_pairs={{0,8},{8,0},{1,9},{9,1},{2,10},{10,2},{3,11},{11,3},{4,12},{12,4},... | collective-permute-start | bytes 786440 | tf_op jit(solution)/shard_map/ppermute | solution.py:401
  22.5 30.2 %all-to-all-start.1 = ((bf16[16,80,256]{2,1,0:T(8,128)(2,1)}), bf16[16,80,256]{2,1,0:T(8,128)(2,1)S(1)}, u32[]{:S(2)}, u32[]{:S(2)}) async-start(bf16[16,80,256]{2,1,0:T(8,128)(2,1)} %dout.1), calls=%async_computation.1 | async-start | bytes 1310720 | tf_op jit(solution)/shard_map/all_to_all | solution.py:442
  56.4 28.1 %all-to-all-start.2 = ((bf16[16,112,256]{2,1,0:T(8,128)(2,1)}), bf16[16,112,256]{2,1,0:T(8,128)(2,1)S(1)}, u32[]{:S(2)}, u32[]{:S(2)}) async-start(bf16[16,112,256]{2,1,0:T(8,128)(2,1)} %get-tuple-element.37), calls=%async_computation.2 | async-start | bytes 1835008 | tf_op jit(solution)/shard_map/all_to_all | solution.py:445
  61.6 11.8 %collective-permute-start.3 = (bf16[16,16,256]{2,1,0:T(8,128)(2,1)S(1)}, bf16[16,16,256]{2,1,0:T(8,128)(2,1)S(1)}, u32[]{:S(2)}, u32[]{:S(2)}) collective-permute-start(bf16[16,16,256]{2,1,0:T(8,128)(2,1)S(1)} %slice.8), channel_id=1, source_target_pairs={{0,2},{2,0},{4,6},{6,4},{1,3},{3,1},{5,7},{7,5},{8,10},{10,8},{12,... | collective-permute-start | bytes 393224 | tf_op jit(solution)/shard_map/ppermute | solution.py:447
  61.7 22.7 %copy-start.1 = (f32[8,1024]{1,0:T(8,128)S(1)}, f32[8,1024]{1,0:T(8,128)}, u32[]{:S(2)}) copy-start(f32[8,1024]{1,0:T(8,128)} %get-tuple-element.38.stat_ref.own_ref) | copy-start | bytes 98308
  61.8 22.7 %copy-start.2 = (s32[4]{0:T(128)S(1)}, s32[4]{0:T(128)}, u32[]{:S(2)}) copy-start(s32[4]{0:T(128)} %pad_add_fusion.place_ref) | copy-start | bytes 52
  73.6 3.9 %collective-permute-start.4 = (bf16[16,32,256]{2,1,0:T(8,128)(2,1)S(1)}, bf16[16,32,256]{2,1,0:T(8,128)(2,1)S(1)}, u32[]{:S(2)}, u32[]{:S(2)}) collective-permute-start(bf16[16,32,256]{2,1,0:T(8,128)(2,1)S(1)} %maximum_select_fusion.own_ref), channel_id=1, source_target_pairs={{0,8},{8,0},{1,9},{9,1},{2,10},{10,2},{3,11},{11,3},{4,12},{12,4},... | collective-permute-start | bytes 786440 | tf_op jit(solution)/shard_map/ppermute | solution.py:401
  88.5 3.7 %copy-start.4 = (f32[8,1024]{1,0:T(8,128)}, f32[8,1024]{1,0:T(8,128)S(1)}, u32[]{:S(2)}) copy-start(f32[8,1024]{1,0:T(8,128)S(1)} %get-tuple-element.44.stat_ref) | copy-start | bytes 98308
  88.5 7.3 %collective-permute-start.5 = (bf16[32,256]{1,0:T(8,128)(2,1)S(1)}, bf16[32,256]{1,0:T(8,128)(2,1)S(1)}, u32[]{:S(2)}, u32[]{:S(2)}) collective-permute-start(bf16[32,256]{1,0:T(8,128)(2,1)S(1)} %get-tuple-element.67), channel_id=1, source_target_pairs={{0,8},{8,0},{1,9},{9,1},{2,10},{10,2},{3,11},{11,3},{4,12},{12,4},... | collective-permute-start | bytes 49160 | tf_op jit(solution)/shard_map/ppermute | solution.py:401
  92.2 32.2 %all-to-all-start.3 = ((bf16[16,128,256]{2,1,0:T(8,128)(2,1)}), bf16[16,128,256]{2,1,0:T(8,128)(2,1)S(1)}, u32[]{:S(2)}, u32[]{:S(2)}) async-start(bf16[16,128,256]{2,1,0:T(8,128)(2,1)} %get-tuple-element.55), calls=%async_computation.3 | async-start | bytes 2097152 | tf_op jit(solution)/shard_map/all_to_all | solution.py:454
  99.9 16.8 %collective-permute-start.6 = (bf16[32,1024]{1,0:T(8,128)(2,1)S(1)}, bf16[32,1024]{1,0:T(8,128)(2,1)S(1)}, u32[]{:S(2)}, u32[]{:S(2)}) collective-permute-start(bf16[32,1024]{1,0:T(8,128)(2,1)S(1)} %bitcast.25), channel_id=1, source_target_pairs={{0,2},{2,4},{4,6},{6,0},{1,3},{3,5},{5,7},{7,1},{8,10},{10,12},{12... | collective-permute-start | bytes 196616 | tf_op jit(solution)/shard_map/ppermute | solution.py:423
  100.0 16.7 %collective-permute-start.7 = (bf16[32,1024]{1,0:T(8,128)(2,1)S(1)}, bf16[32,1024]{1,0:T(8,128)(2,1)S(1)}, u32[]{:S(2)}, u32[]{:S(2)}) collective-permute-start(bf16[32,1024]{1,0:T(8,128)(2,1)S(1)} %bitcast.26), channel_id=1, source_target_pairs={{0,4},{2,6},{4,0},{6,2},{1,5},{3,7},{5,1},{7,3},{8,12},{10,14},{12... | collective-permute-start | bytes 196616 | tf_op jit(solution)/shard_map/ppermute | solution.py:423
  101.6 15.1 %collective-permute-start.8 = (bf16[32,1024]{1,0:T(8,128)(2,1)S(1)}, bf16[32,1024]{1,0:T(8,128)(2,1)S(1)}, u32[]{:S(2)}, u32[]{:S(2)}) collective-permute-start(bf16[32,1024]{1,0:T(8,128)(2,1)S(1)} %bitcast.27), channel_id=1, source_target_pairs={{0,6},{2,0},{4,2},{6,4},{1,7},{3,1},{5,3},{7,5},{8,14},{10,8},{12,... | collective-permute-start | bytes 196616 | tf_op jit(solution)/shard_map/ppermute | solution.py:423
  103.7 20.8 %copy-start.3 = (s32[4]{0:T(128)S(1)}, s32[4]{0:T(128)}, u32[]{:S(2)}) copy-start(s32[4]{0:T(128)} %pad_add_fusion.place_ref) | copy-start | bytes 52
  115.1 3.3 %collective-permute-start.10 = (bf16[1024,256]{1,0:T(8,128)(2,1)}, bf16[1024,256]{1,0:T(8,128)(2,1)S(1)}, u32[]{:S(2)}, u32[]{:S(2)}) collective-permute-start(bf16[1024,256]{1,0:T(8,128)(2,1)} %get-tuple-element.51), channel_id=1, source_target_pairs={{0,8},{8,0},{1,9},{9,1},{2,10},{10,2},{3,11},{11,3},{4,12},{12,4},... | collective-permute-start | bytes 1572872 | tf_op jit(solution)/shard_map/ppermute | solution.py:401
  116.6 2.6 %collective-permute-start.11 = (bf16[1024,256]{1,0:T(8,128)(2,1)}, bf16[1024,256]{1,0:T(8,128)(2,1)S(1)}, u32[]{:S(2)}, u32[]{:S(2)}) collective-permute-start(bf16[1024,256]{1,0:T(8,128)(2,1)} %get-tuple-element.53), channel_id=1, source_target_pairs={{0,8},{8,0},{1,9},{9,1},{2,10},{10,2},{3,11},{11,3},{4,12},{12,4},... | collective-permute-start | bytes 1572872 | tf_op jit(solution)/shard_map/ppermute | solution.py:401
  117.0 3.6 %collective-permute-start.9 = (bf16[32,512]{1,0:T(8,128)(2,1)S(1)}, bf16[32,512]{1,0:T(8,128)(2,1)S(1)}, u32[]{:S(2)}, u32[]{:S(2)}) collective-permute-start(bf16[32,512]{1,0:T(8,128)(2,1)S(1)} %bitcast.28), channel_id=1, source_target_pairs={{0,1},{1,0},{2,3},{3,2},{4,5},{5,4},{6,7},{7,6},{8,9},{9,8},{10,11... | collective-permute-start | bytes 98312 | tf_op jit(solution)/shard_map/ppermute | solution.py:469
  125.4 4.2 %collective-permute-start.13 = (f32[256,128]{1,0:T(8,128)S(1)}, f32[256,128]{1,0:T(8,128)S(1)}, u32[]{:S(2)}, u32[]{:S(2)}) collective-permute-start(f32[256,128]{1,0:T(8,128)S(1)} %get-tuple-element.63), channel_id=1, source_target_pairs={{0,8},{8,0},{1,9},{9,1},{2,10},{10,2},{3,11},{11,3},{4,12},{12,4},... | collective-permute-start | bytes 393224 | tf_op jit(solution)/shard_map/ppermute | solution.py:401
  127.7 1.2 collective-permute-start.12
  (3 other events, 2.8 us)
